TPU v7x, 32 devices: a whole 2x2x4 slice. The times are simulated.
32 devices in a mesh: dp: 8 (over z, x), seq: 4 (over y, core).
Axes of the slice: x: 2, y: 2, z: 4, core: 2. Of those that a mesh axis runs over, the one named last changes fastest.
Arguments:
- inputs: bfloat16 [16, 1024, 768], P('dp', 'seq'), may hold values from -6 to 6
- cotangent: bfloat16 [16, 1024, 768], P('dp', 'seq'), may hold values from -6 to 6
- task_table: int32 [16], P('dp'), may hold values from 0 to 3, as said below
- type_counts: int32 [16, 3], P('dp'), may hold values from 1 to 512, 1024 in all within a row
- gain_one: float32 [2, 768], replicated, may hold values from 0.5 to 1.5
- bias_one: float32 [2, 768], replicated, may hold values from -2 to 2
- proj_qkv: bfloat16 [2, 768, 2304], replicated, may hold values from -0.21875 to 0.21875
- proj_out: bfloat16 [2, 768, 768], replicated, may hold values from -0.875 to 0.875
- gain_two: float32 [2, 768], replicated, may hold values from 0.5 to 1.5
- bias_two: float32 [2, 768], replicated, may hold values from -2 to 2
- proj_up: bfloat16 [2, 768, 3072], replicated, may hold values from -0.21875 to 0.21875
- proj_down: bfloat16 [2, 3072, 768], replicated, may hold values from -0.109375 to 0.109375
Outputs:
- outputs: bfloat16 [16, 1024, 768], P('dp', 'seq')
- back_inputs: float32 [16, 1024, 768], P('dp', 'seq')
- grad_gain_one: float32 [2, 768], P(None, ('dp', 'seq'))
- grad_bias_one: float32 [2, 768], P(None, ('dp', 'seq'))
- grad_qkv: float32 [2, 768, 2304], P(None, ('dp', 'seq'))
- grad_out: float32 [2, 768, 768], P(None, ('dp', 'seq'))
- grad_gain_two: float32 [2, 768], P(None, ('dp', 'seq'))
- grad_bias_two: float32 [2, 768], P(None, ('dp', 'seq'))
- grad_up: float32 [2, 768, 3072], P(None, ('dp', 'seq'))
- grad_down: float32 [2, 3072, 768], P(None, ('dp', 'seq'))
Inputs may be any that keep to these rules, and one draw needn't show every extreme that they name: `task_table`: the first slot of each index of dp holds a task below 3; every task holds at least one sequence; 3 marks an empty slot. `type_counts`: Image, action and text tokens follow one another in that order and fill the sequence.
All inputs are finite; a program needn't handle non-finite values.
Results may differ from a plain program's by a relative error of at most 0.013.
Values may be sent and summed in bfloat16 or wider, within the bound.
A program may use at most 320 MiB of HBM per device.

v0:
```python
import functools
import math

import jax
import jax.numpy as jnp
import numpy as np
from jax import lax
from jax.experimental import pallas as pl
from jax.experimental.pallas import tpu as pltpu
from jax.sharding import PartitionSpec as P

HEADS = 12
HEAD_DIM = 64
LAYERS = 2
TASKS = 3
AXES = ("dp", "seq")
F32 = jnp.float32
BF16 = jnp.bfloat16
epsilon = 1e-05
PAIRS = 2
VMEM_BYTES = 32 * 1024 * 1024
SMALL_COST = pl.CostEstimate(flops=1000, bytes_accessed=1000, transcendentals=0)


def in_hbm(*values):
    return tuple(pltpu.with_memory_space_constraint(v, pltpu.HBM) for v in values)


def dot_nn(a, b):
    return lax.dot_general(a, b, (((1,), (0,)), ((), ())), preferred_element_type=F32)


def dot_nt(a, b):
    return lax.dot_general(a, b, (((1,), (1,)), ((), ())), preferred_element_type=F32)


def dot_tn(a, b):
    return lax.dot_general(a, b, (((0,), (0,)), ((), ())), preferred_element_type=F32)


def gelu_and_slope(x):
    z = jnp.abs(x) * 0.7071067811865476
    d = 1.0 + 0.3275911 * z
    t = pl.reciprocal(d, approx=True)
    t = t * (2.0 - d * t)
    poly = t * (
        0.254829592
        + t * (-0.284496736 + t * (1.421413741 + t * (-1.453152027 + t * 1.061405429)))
    )
    bell = jnp.exp(-0.5 * x * x)
    tail = 0.5 * poly * bell
    below = jnp.where(x >= 0.0, 1.0 - tail, tail)
    return x * below, below + x * bell * 0.3989422804014327


def head_masks(scale):
    lane = lax.broadcasted_iota(jnp.int32, (1, 2 * HEAD_DIM), 1)
    first = jnp.where(lane < HEAD_DIM, scale, 0.0)
    return first.astype(BF16), (scale - first).astype(BF16)


def stacked(value, masks):
    return jnp.concatenate([value * masks[0], value * masks[1]], 0)


def merged(value):
    rows = value.shape[0] // 2
    lane = lax.broadcasted_iota(jnp.int32, (rows, 2 * HEAD_DIM), 1)
    return jnp.where(lane < HEAD_DIM, value[:rows], value[rows:])


def by_variant(meta, run):
    @pl.when(meta[0] == 0)
    def _():
        run(0)

    @pl.when(meta[0] == 1)
    def _():
        run(1)


def attention_forward_kernel(meta, q_ref, ko_ref, vo_ref, kx_ref, vx_ref, out_ref, lse_ref):
    def run_all(variant):
        for pair in range(PAIRS):
            lanes = (slice(None), slice(pair * 2 * HEAD_DIM, (pair + 1) * 2 * HEAD_DIM))
            refs = [ref.at[lanes] for ref in (q_ref, ko_ref, vo_ref, kx_ref, vx_ref, out_ref)]
            attention_forward_pair(variant, *refs, lse_ref.at[pair])

    by_variant(meta, run_all)


def attention_forward_pair(variant, q_ref, ko_ref, vo_ref, kx_ref, vx_ref, out_ref, lse_ref):
    rows = q_ref.shape[0] // 2
    masks = head_masks(1.0 / math.sqrt(HEAD_DIM))

    def run(variant):
        position = lax.broadcasted_iota(jnp.int32, (2 * rows, rows), 0) % rows
        below = lax.broadcasted_iota(jnp.int32, (2 * rows, rows), 1) <= position
        low, high = slice(0, rows), slice(rows, 2 * rows)
        if variant == 0:
            plan = [
                (low, [(ko_ref, vo_ref, low)]),
                (high, [(ko_ref, vo_ref, low), (kx_ref, vx_ref, low), (kx_ref, vx_ref, high), (ko_ref, vo_ref, high)]),
            ]
        else:
            plan = [
                (low, [(kx_ref, vx_ref, low), (ko_ref, vo_ref, low)]),
                (high, [(ko_ref, vo_ref, low), (kx_ref, vx_ref, low), (ko_ref, vo_ref, high)]),
            ]
        all_scores = []
        for span, parts in plan:
            q2 = stacked(q_ref[span, :], masks)
            all_scores.append([dot_nt(q2, keys[place, :]) for keys, unused, place in parts])
        for (span, parts), scores in zip(plan, all_scores):
            scores[-1] = jnp.where(below, scores[-1], -1e30)
            peak = jnp.max(functools.reduce(jnp.maximum, scores), -1, keepdims=True)
            total, acc = None, None
            for part, (unused, values, place) in zip(scores, parts):
                raised = jnp.exp(part - peak)
                total = raised if total is None else total + raised
                term = dot_nn(raised.astype(BF16), values[place, :])
                acc = term if acc is None else acc + term
            total = jnp.sum(total, -1, keepdims=True)
            out_ref[span, :] = merged(acc / total).astype(BF16)
            log = peak + jnp.log(total)
            lane = lax.broadcasted_iota(jnp.int32, (rows, 2 * HEAD_DIM), 1)
            lse_ref[:, span] = jnp.where(lane == 0, log[:rows], log[rows:]).T[:8, :]

    run(variant)


def attention_forward(meta, queries, own, other):
    tokens = queries.shape[0]
    pairs = HEADS // 2
    wide = 2 * HEAD_DIM * PAIRS

    def at(offset):
        return pl.BlockSpec((tokens, wide), lambda g, m: (0, offset // PAIRS + g))

    return pl.pallas_call(
        attention_forward_kernel,
        grid_spec=pltpu.PrefetchScalarGridSpec(
            num_scalar_prefetch=1,
            grid=(pairs // PAIRS,),
            in_specs=[at(0), at(0), at(pairs), at(0), at(pairs)],
            out_specs=[at(0), pl.BlockSpec((PAIRS, 8, tokens), lambda g, m: (g, 0, 0))],
        ),
        out_shape=[
            pltpu.HBM((tokens, HEADS * HEAD_DIM), BF16),
            pltpu.HBM((pairs, 8, tokens), F32),
        ],
        compiler_params=pltpu.CompilerParams(vmem_limit_bytes=VMEM_BYTES),
        cost_estimate=SMALL_COST,
        name="attention_forward",
    )(meta, *in_hbm(queries, own, own, other, other))


def attention_backward_kernel(
    meta, q_ref, ko_ref, vo_ref, kx_ref, vx_ref, do_ref, o_ref, lse_ref,
    dq_ref, own_ref, other_ref, q4, do4,
):
    def run_all(variant):
        for pair in range(PAIRS):
            lanes = (slice(None), slice(pair * 2 * HEAD_DIM, (pair + 1) * 2 * HEAD_DIM))
            refs = [ref.at[lanes] for ref in (q_ref, ko_ref, vo_ref, kx_ref, vx_ref, do_ref, o_ref)]
            grads = [ref.at[(slice(None),) + lanes] for ref in (own_ref, other_ref)]
            attention_backward_pair(
                variant, *refs, lse_ref.at[pair], dq_ref.at[lanes], *grads, q4.at[pair], do4.at[pair]
            )

    by_variant(meta, run_all)


def attention_backward_pair(
    variant, q_ref, ko_ref, vo_ref, kx_ref, vx_ref, do_ref, o_ref, lse_ref,
    dq_ref, own_ref, other_ref, q4, do4,
):
    rows = q_ref.shape[0] // 2
    scale = 1.0 / math.sqrt(HEAD_DIM)
    scaled, plain = head_masks(scale), head_masks(1.0)
    product = (do_ref[...].astype(F32) * o_ref[...].astype(F32)).T
    first = jnp.sum(product[:HEAD_DIM], 0, keepdims=True)
    second = jnp.sum(product[HEAD_DIM:], 0, keepdims=True)
    logs = lse_ref[...]
    dot_row = jnp.concatenate([first[:, :rows], second[:, :rows], first[:, rows:], second[:, rows:]], 1)
    log_row = jnp.concatenate(
        [logs[0:1, :rows], logs[1:2, :rows], logs[0:1, rows:], logs[1:2, rows:]], 1
    )
    for block in range(2):
        span = slice(block * rows, (block + 1) * rows)
        q4[2 * block * rows : 2 * (block + 1) * rows, :] = stacked(q_ref[span, :], scaled)
        do4[2 * block * rows : 2 * (block + 1) * rows, :] = stacked(do_ref[span, :], plain)

    def run(variant):
        column = lax.broadcasted_iota(jnp.int32, (rows, 2 * rows), 1) % rows
        below = lax.broadcasted_iota(jnp.int32, (rows, 2 * rows), 0) <= column
        low, high = slice(0, rows), slice(rows, 2 * rows)
        both, upper, lower = slice(0, 4 * rows), slice(2 * rows, 4 * rows), slice(0, 2 * rows)
        plan = [(0, low, lower, True), (0, low, upper, False), (1, low, upper, False), (0, high, upper, True)]
        plan.insert(3, (1, high, upper, False) if variant == 0 else (1, low, lower, False))
        keys, values, grads = (ko_ref, kx_ref), (vo_ref, vx_ref), (own_ref, other_ref)
        dq_parts = {}
        sums = {}
        ahead = {}

        def products(index):
            source, place, cols, unused = plan[index]
            ahead[index] = dot_nt(keys[source][place, :], q4[cols, :]), dot_nt(values[source][place, :], do4[cols, :])

        products(0)
        products(1)
        for index, (source, place, cols, diagonal) in enumerate(plan):
            if index + 2 < len(plan):
                products(index + 2)
            scores, back = ahead.pop(index)
            raised = jnp.exp(scores - log_row[:, cols])
            if diagonal:
                raised = jnp.where(below, raised, 0.0)
            slope = (raised * (back - dot_row[:, cols])).astype(BF16)
            slot = (source, place.start)
            terms = dot_nn(slope, q4[cols, :]), dot_nn(raised.astype(BF16), do4[cols, :])
            sums[slot] = tuple(a + b for a, b in zip(sums[slot], terms)) if slot in sums else terms
            term = dot_tn(slope, keys[source][place, :])
            dq_parts[cols.start] = dq_parts[cols.start] + term if cols.start in dq_parts else term
        for block in range(2):
            dq_ref[block * rows : (block + 1) * rows, :] = (
                merged(dq_parts[2 * block * rows]) * scale
            ).astype(BF16)
        for source in range(2):
            for place in (low, high):
                zero = jnp.zeros((rows, 2 * HEAD_DIM), F32)
                for which, value in enumerate(sums.get((source, place.start), (zero, zero))):
                    grads[source][which, place, :] = value.astype(grads[source].dtype)

    run(variant)


def attention_backward(meta, queries, own, other, back_attended, attended, logs):
    tokens = queries.shape[0]
    pairs = HEADS // 2
    wide = 2 * HEAD_DIM * PAIRS
    width = HEADS * HEAD_DIM

    def at(offset):
        return pl.BlockSpec((tokens, wide), lambda g, m: (0, offset // PAIRS + g))

    return pl.pallas_call(
        attention_backward_kernel,
        grid_spec=pltpu.PrefetchScalarGridSpec(
            num_scalar_prefetch=1,
            grid=(pairs // PAIRS,),
            in_specs=[at(0), at(0), at(pairs), at(0), at(pairs), at(0), at(0),
                      pl.BlockSpec((PAIRS, 8, tokens), lambda g, m: (g, 0, 0))],
            out_specs=[at(0)] + [pl.BlockSpec((2, tokens, wide), lambda g, m: (0, 0, g))] * 2,
            scratch_shapes=[pltpu.VMEM((PAIRS, 2 * tokens, 2 * HEAD_DIM), BF16)] * 2,
        ),
        out_shape=[
            jax.ShapeDtypeStruct((tokens, width), BF16),
            pltpu.HBM((2, tokens, width), BF16),
            jax.ShapeDtypeStruct((2, tokens, width), BF16),
        ],
        compiler_params=pltpu.CompilerParams(vmem_limit_bytes=VMEM_BYTES),
        cost_estimate=SMALL_COST,
        name="attention_backward",
    )(meta, *in_hbm(queries, own, own, other, other, back_attended, attended, logs))


def normalised(rows_in):
    average = jnp.mean(rows_in, -1, keepdims=True)
    centred = rows_in - average
    inverse = lax.rsqrt(jnp.mean(centred * centred, -1, keepdims=True) + epsilon)
    return centred * inverse, inverse


def norm_back(rows_in, gain_row, back):
    unit, inverse = normalised(rows_in)
    slope = back * gain_row
    first = jnp.mean(slope, -1, keepdims=True)
    second = jnp.mean(slope * unit, -1, keepdims=True)
    return inverse * (slope - first - unit * second), (
        jnp.sum(back * unit, 0, keepdims=True), jnp.sum(back, 0, keepdims=True))


def with_rows(table, row, sums):
    index = lax.broadcasted_iota(jnp.int32, table.shape, 0)
    return jnp.where(index == row, sums[0], jnp.where(index == row + 1, sums[1], table))


def project_kernel(layer, stream, gain, shift, matrix, hidden, queries, pairs):
    width = stream.shape[1]
    groups = 4
    rows = stream.shape[0] // groups
    for group in range(groups):
        span = slice(group * rows, (group + 1) * rows)
        unit, unused = normalised(stream[span, :].astype(F32))
        hidden[span, :] = (unit * gain[layer : layer + 1] + shift[layer : layer + 1]).astype(BF16)
        pairs[span, :] = dot_nn(hidden[span, :], matrix[0, :, width:]).astype(BF16)
        queries[span, :] = dot_nn(hidden[span, :], matrix[0, :, :width]).astype(BF16)


def project(layer, stream, gain, shift, matrix):
    tokens, width = stream.shape
    whole = pl.BlockSpec((tokens, width), lambda j: (0, 0))
    row = pl.BlockSpec(gain.shape, lambda j: (0, 0))
    return pl.pallas_call(
        functools.partial(project_kernel, layer),
        grid=(1,),
        in_specs=[whole, row, row, pl.BlockSpec((1, width, 3 * width), lambda j: (layer, 0, 0))],
        out_specs=[whole, whole, pl.BlockSpec((tokens, 2 * width), lambda j: (0, 0))],
        out_shape=[
            pltpu.HBM((tokens, width), BF16),
            pltpu.HBM((tokens, width), BF16),
            pltpu.HBM((tokens, 2 * width), BF16),
        ],
        compiler_params=pltpu.CompilerParams(vmem_limit_bytes=VMEM_BYTES),
        cost_estimate=SMALL_COST,
        name="project",
    )(*in_hbm(stream), gain, shift, *in_hbm(matrix))


def feed_forward_kernel(
    layer, steps, attended, stream, matrix_out, gain, shift, up, down,
    middle, normed, active_ref, slope_ref, out, *rest,
):
    acc = rest[-1]
    step = pl.program_id(0)

    @pl.when(step == 0)
    def _():
        acc[...] = stream[...].astype(F32) + dot_nn(attended[...], matrix_out[0])
        middle[...] = acc[...].astype(BF16)
        unit, unused = normalised(acc[...])
        normed[...] = (unit * gain[layer : layer + 1] + shift[layer : layer + 1]).astype(BF16)

    groups = 4
    rows = normed.shape[0] // groups
    raw = {}
    for group in range(groups + 1):
        if group < groups:
            raw[group] = dot_nn(normed[group * rows : (group + 1) * rows, :], up[0])
        if group > 0:
            span = slice((group - 1) * rows, group * rows)
            active, slope = gelu_and_slope(raw.pop(group - 1))
            active = active.astype(BF16)
            active_ref[span, :] = active
            slope_ref[span, :] = slope.astype(BF16)
            acc[span, :] += dot_nn(active, down[0])

    @pl.when(step == steps - 1)
    def _():
        out[...] = acc[...].astype(out.dtype)
        if len(rest) == 2:
            rest[0][...] = acc[other_block(acc.shape[0] // 2), :].astype(out.dtype)


def other_block(rows):
    return pl.ds(pl.multiple_of((1 - lax.axis_index("seq") // 2) * rows, rows), rows)


def feed_forward(layer, attended, stream, matrix_out, gain, shift, up, down):
    tokens, width = stream.shape
    last = layer == LAYERS - 1
    block = pl.BlockSpec((tokens // 2, width), lambda j: (0, 0))
    hidden = up.shape[2]
    tile = 1024
    steps = hidden // tile
    whole = pl.BlockSpec((tokens, width), lambda j: (0, 0))
    row = pl.BlockSpec(gain.shape, lambda j: (0, 0))
    part = pl.BlockSpec((tokens, tile), lambda j: (0, j))
    return pl.pallas_call(
        functools.partial(feed_forward_kernel, layer, steps),
        grid=(steps,),
        in_specs=[
            whole, whole, pl.BlockSpec((1, width, width), lambda j: (layer, 0, 0)), row, row,
            pl.BlockSpec((1, width, tile), lambda j: (layer, 0, j)),
            pl.BlockSpec((1, tile, width), lambda j: (layer, j, 0)),
        ],
        out_specs=[whole, whole, part, part, whole] + [block] * last,
        out_shape=[
            pltpu.HBM((tokens, width), BF16),
            pltpu.HBM((tokens, width), BF16),
            pltpu.HBM((tokens, hidden), BF16),
            pltpu.HBM((tokens, hidden), BF16),
            pltpu.HBM((tokens, width), BF16),
        ] + [jax.ShapeDtypeStruct((tokens // 2, width), BF16)] * last,
        scratch_shapes=[pltpu.VMEM((tokens, width), F32)],
        compiler_params=pltpu.CompilerParams(vmem_limit_bytes=VMEM_BYTES),
        cost_estimate=SMALL_COST,
        name="feed_forward",
    )(*in_hbm(attended, stream, matrix_out), gain, shift, *in_hbm(up, down))


def feed_back_kernel(
    layer, steps, meta, back_out, slope, up, down, middle, gain, matrix_out, sums_in,
    own, send, back_branch, branch_send, back_attended, grads, acc,
):
    step = pl.program_id(0)
    half = branch_send.shape[1]
    theirs = pl.ds(pl.multiple_of((1 - meta[1]) * half, 128), half)

    @pl.when(step == 0)
    def _():
        acc[...] = jnp.zeros_like(acc)

    back_up = (dot_nt(back_out[...], down[0]) * slope[...].astype(F32)).astype(BF16)

    @pl.when(step < steps // 2)
    def _():
        send[...] = back_up

    @pl.when(step >= steps // 2)
    def _():
        own[...] = back_up

    acc[...] += dot_nt(back_up, up[0])

    @pl.when(step == steps - 1)
    def _():
        back, sums = norm_back(middle[...].astype(F32), gain[layer : layer + 1], acc[...])
        back = back + back_out[...].astype(F32)
        grads[...] = with_rows(sums_in[...], 4 * layer + 2, sums)
        back_branch[...] = back.astype(BF16)
        branch_send[...] = back_branch[:, theirs]
        back_attended[...] = dot_nt(back_branch[...], matrix_out[0]).astype(BF16)


def feed_back(layer, meta, back_out, slope, up, down, middle, gain, matrix_out, sums):
    tokens, width = back_out.shape
    hidden = up.shape[2]
    tile = 768
    steps = hidden // tile
    half = steps // 2

    def place(j, m):
        return jnp.where(j < half, (1 - m[1]) * half + j, m[1] * half + j - half)

    whole = pl.BlockSpec((tokens, width), lambda j, m: (0, 0))
    narrow = pl.BlockSpec((tokens, width // 2), lambda j, m: (0, 0))
    wide = jax.ShapeDtypeStruct((tokens, width), BF16)
    return pl.pallas_call(
        functools.partial(feed_back_kernel, layer, steps),
        grid_spec=pltpu.PrefetchScalarGridSpec(
            num_scalar_prefetch=1,
            grid=(steps,),
            in_specs=[
                whole, pl.BlockSpec((tokens, tile), lambda j, m: (0, place(j, m))),
                pl.BlockSpec((1, width, tile), lambda j, m: (layer, 0, place(j, m))),
                pl.BlockSpec((1, tile, width), lambda j, m: (layer, place(j, m), 0)),
                whole, pl.BlockSpec(gain.shape, lambda j, m: (0, 0)),
                pl.BlockSpec((1, width, width), lambda j, m: (layer, 0, 0)),
                pl.BlockSpec((8, width), lambda j, m: (0, 0)),
            ],
            out_specs=[
                pl.BlockSpec((tokens, tile), lambda j, m: (0, jnp.maximum(j - half, 0))),
                pl.BlockSpec((tokens, tile), lambda j, m: (0, jnp.minimum(j, half - 1))),
                whole, narrow, whole,
                pl.BlockSpec((8, width), lambda j, m: (0, 0)),
            ],
            scratch_shapes=[pltpu.VMEM((tokens, width), F32)],
        ),
        out_shape=[
            jax.ShapeDtypeStruct((tokens, hidden // 2), BF16),
            jax.ShapeDtypeStruct((tokens, hidden // 2), BF16),
            wide, jax.ShapeDtypeStruct((tokens, width // 2), BF16),
            wide, jax.ShapeDtypeStruct((8, width), F32),
        ],
        compiler_params=pltpu.CompilerParams(vmem_limit_bytes=VMEM_BYTES),
        cost_estimate=SMALL_COST,
        name="feed_back",
    )(meta, back_out, *in_hbm(slope, up, down, middle), gain, *in_hbm(matrix_out), sums)


def project_back_kernel(
    layer, meta, back_q, own, got, matrix, stream, gain, back_middle, sums_in,
    mine, theirs, back_out, back_out_send, grads, *rest,
):
    width = back_q.shape[1]
    table, acc = rest[-2:]

    def begin():
        table[0] = back_q[...]
        for which in range(2):
            table[1 + which] = (own[which].astype(F32) + got[which].astype(F32)).astype(BF16)
        half = width // 2

        @pl.when(meta[1] == 0)
        def _():
            mine[:, :width] = table[0]
            mine[:, width:] = table[1, :, :half]
            theirs[:, :half] = table[1, :, half:]
            theirs[:, half:] = table[2]

        @pl.when(meta[1] == 1)
        def _():
            theirs[:, :width] = table[0]
            theirs[:, width:] = table[1, :, :half]
            mine[:, :half] = table[1, :, half:]
            mine[:, half:] = table[2]

    begin()
    acc[...] = sum(
        dot_nt(table[which], matrix[0, :, which * width : (which + 1) * width]) for which in range(3)
    )

    def end():
        back, sums = norm_back(stream[...].astype(F32), gain[layer : layer + 1], acc[...])
        back = back + back_middle[...].astype(F32)
        back_out[...] = back.astype(BF16)
        half = width // 2
        back_out_send[...] = back_out[:, pl.ds(pl.multiple_of((1 - meta[1]) * half, 128), half)]
        grads[...] = with_rows(sums_in[...], 4 * layer, sums)
        if len(rest) == 3:
            rest[0][...] = back_out[other_block(back_out.shape[0] // 2), :]

    end()


def project_back(layer, meta, back_q, own, got, matrix, stream, gain, back_middle, sums):
    tokens, width = stream.shape
    whole = pl.BlockSpec((tokens, width), lambda j, m: (0, 0))
    both = pl.BlockSpec((2, tokens, width), lambda j, m: (0, 0, 0))
    side = pl.BlockSpec((tokens, 3 * width // 2), lambda j, m: (0, 0))
    return pl.pallas_call(
        functools.partial(project_back_kernel, layer),
        grid_spec=pltpu.PrefetchScalarGridSpec(
            num_scalar_prefetch=1,
            grid=(1,),
            in_specs=[
                whole, both, both, pl.BlockSpec((1, width, 3 * width), lambda j, m: (layer, 0, 0)),
                whole, pl.BlockSpec(gain.shape, lambda j, m: (0, 0)), whole,
                pl.BlockSpec((8, width), lambda j, m: (0, 0)),
            ],
            out_specs=[side, side, whole, pl.BlockSpec((tokens, width // 2), lambda j, m: (0, 0)),
                       pl.BlockSpec((8, width), lambda j, m: (0, 0))]
            + [pl.BlockSpec((tokens // 2, width), lambda j, m: (0, 0))] * (layer == 0),
            scratch_shapes=[pltpu.VMEM((3, tokens, width), BF16), pltpu.VMEM((tokens, width), F32)],
        ),
        out_shape=[
            jax.ShapeDtypeStruct((tokens, 3 * width // 2), BF16),
            jax.ShapeDtypeStruct((tokens, 3 * width // 2), BF16),
            jax.ShapeDtypeStruct((tokens, width), BF16),
            jax.ShapeDtypeStruct((tokens, width // 2), BF16),
            jax.ShapeDtypeStruct((8, width), F32),
        ] + [jax.ShapeDtypeStruct((tokens // 2, width), BF16)] * (layer == 0),
        compiler_params=pltpu.CompilerParams(vmem_limit_bytes=VMEM_BYTES),
        cost_estimate=SMALL_COST,
        name="project_back",
    )(meta, *in_hbm(back_q, own), got, *in_hbm(matrix, stream), gain, *in_hbm(back_middle), sums)


def weigh_kernel(weight, start, own, got, back_out, back_out_send):
    rows, half = own.shape[0], back_out_send.shape[1]
    place = lax.axis_index("seq")
    core, low = place % 2, ((place + 1) // 2) % 2
    step = lax.broadcasted_iota(jnp.int32, (rows, 1), 0)
    first = place < 2
    for which, block in enumerate((low, 3 - low)):
        span = slice(which * rows, (which + 1) * rows)
        scale = jnp.where(block * rows + step >= start[0], weight[0], 0.0)
        mine = own[...].astype(F32) if which == 0 else got[...].astype(F32)
        other = got[...].astype(F32) if which == 0 else own[...].astype(F32)
        back_out[span, :] = (jnp.where(first, mine, other) * scale).astype(BF16)
    back_out_send[...] = back_out[:, pl.ds(pl.multiple_of((1 - core) * half, 128), half)]


def weigh(weight, start, own, got):
    rows, width = own.shape
    scalar = pl.BlockSpec(memory_space=pltpu.SMEM)
    return pl.pallas_call(
        weigh_kernel,
        in_specs=[scalar, scalar, pl.BlockSpec(memory_space=pltpu.VMEM), pl.BlockSpec(memory_space=pltpu.VMEM)],
        out_specs=[pl.BlockSpec(memory_space=pltpu.VMEM)] * 2,
        out_shape=[
            jax.ShapeDtypeStruct((2 * rows, width), BF16),
            jax.ShapeDtypeStruct((2 * rows, width // 2), BF16),
        ],
        compiler_params=pltpu.CompilerParams(vmem_limit_bytes=VMEM_BYTES),
        cost_estimate=SMALL_COST,
        name="weigh",
    )(weight, start, own, got)


def store_chunks(chips, meta, acc, keep, send):
    rows = acc.shape[0] // chips
    for position in range(chips):
        chunk = acc[pl.ds(pl.multiple_of(meta[2 + position] * rows, 16), rows), :]
        if position < chips // 2:
            keep[position] = chunk
        else:
            send[position - chips // 2] = chunk


def grad_up_kernel(chips, meta, ao, ax, bo, bx, co, cx, do, dx, keep, send, acc):
    step = pl.program_id(0)
    rows, half = acc.shape[0] // chips, do.shape[1]

    @pl.when(step < 2)
    def _():
        acc[...] = (dot_tn(ao[...], bo[...]) + dot_tn(ax[...], bx[...])).astype(BF16)

    @pl.when(step == 2)
    def _():
        acc[:, :half] = (dot_tn(co[...], do[...]) + dot_tn(cx[...], dx[...])).astype(BF16)

    for position in range(chips):
        place = pl.ds(pl.multiple_of(meta[2 + position] * rows, 16), rows)
        target, index = (keep, position) if position < chips // 2 else (send, position - chips // 2)
        target[index, :rows, :] = acc[place, :half]
        target[index, rows:, :] = acc[place, half:]


def grad_down_kernel(chips, meta, ao, ax, bo, bx, *refs):
    keep, send = refs[-2:]
    rows = keep.shape[1]
    each = ao.shape[1] // rows
    total = (dot_tn(ao[...], bo[...]) + dot_tn(ax[...], bx[...])).astype(BF16)
    for local in range(each):
        position = meta[2 + chips + pl.program_id(0) * each + local]
        chunk = total[local * rows : (local + 1) * rows]

        @pl.when(position < chips // 2)
        def _():
            keep[position] = chunk

        @pl.when(position >= chips // 2)
        def _():
            send[position - chips // 2] = chunk


def grad_qkv_kernel(chips, meta, ao, ax, bo, bx, sums, keep, send, acc, columns):
    wide = bo.shape[1]
    acc[:, :wide] = (dot_tn(ao[...], bo[...]) + dot_tn(ax[...], bx[...])).astype(BF16)
    columns[...] = jnp.concatenate([sums[...], jnp.zeros((120, sums.shape[1]), F32)], 0).T
    acc[:, wide:] = columns[...].astype(BF16)
    store_chunks(chips, meta, acc, keep, send)


def ordered(total, ids, chips):
    split = total.astype(BF16).reshape(chips, total.shape[0] // chips, total.shape[1])
    return jnp.take(split, ids, axis=0)


def gradient_call(kernel, name, chips, grid, in_specs, out_spec, shape, scratch):
    return pl.pallas_call(
        functools.partial(kernel, chips),
        grid_spec=pltpu.PrefetchScalarGridSpec(
            num_scalar_prefetch=1, grid=(grid,), in_specs=in_specs, out_specs=[out_spec] * 2,
            scratch_shapes=scratch,
        ),
        out_shape=[pltpu.HBM(shape, BF16)] * 2,
        compiler_params=pltpu.CompilerParams(vmem_limit_bytes=VMEM_BYTES),
        cost_estimate=SMALL_COST,
        name=name,
    )


def up_gradients(
    meta, chips, normed, normed_x, back_up, back_up_x, attended, attended_x, back_branch, branch_x
):
    tokens, width = normed.shape
    half = width // 2
    rows = width // chips
    if rows % 16 != 0:
        ids = meta[2 : 2 + chips]
        up = dot_tn(normed, back_up) + dot_tn(normed_x, back_up_x)
        own = lax.dynamic_slice_in_dim(back_branch, meta[1] * half, half, 1)
        out = dot_tn(attended, own) + dot_tn(attended_x, branch_x)
        up = ordered(up, ids, chips).reshape(chips, rows, 4, half)
        up = up.transpose(0, 2, 1, 3).reshape(chips, 4 * rows, half)
        both = jnp.concatenate([up, ordered(out, ids, chips)], 1)
        return both[: chips // 2], both[chips // 2 :]
    whole = pl.BlockSpec((tokens, width), lambda j, m: (0, 0))
    fixed = pl.BlockSpec((tokens, half), lambda j, m: (0, 0))
    mine = pl.BlockSpec((tokens, half), lambda j, m: (0, m[1]))
    tile = pl.BlockSpec((tokens, 2 * half), lambda j, m: (0, jnp.minimum(j, 1)))
    return gradient_call(
        grad_up_kernel, "gradient_up", chips, 3, [whole, whole, tile, tile, whole, whole, mine, fixed],
        pl.BlockSpec((chips // 2, 2 * rows, half), lambda j, m: (0, j, 0)),
        (chips // 2, 5 * rows, half), [pltpu.VMEM((width, 2 * half), BF16)],
    )(meta, *in_hbm(normed, normed_x), back_up, back_up_x, *in_hbm(attended, attended_x), back_branch, branch_x)


def down_gradients(meta, chips, active, active_x, back_out, back_out_x):
    tokens, hidden = active.shape
    width = back_out.shape[1]
    half = width // 2
    rows = hidden // chips
    if rows % 64 != 0:
        own = lax.dynamic_slice_in_dim(back_out, meta[1] * half, half, 1)
        down = dot_tn(active, own) + dot_tn(active_x, back_out_x)
        down = ordered(down, meta[2 : 2 + chips], chips)
        return down[: chips // 2], down[chips // 2 :]
    fixed = pl.BlockSpec((tokens, half), lambda j, m: (0, 0))
    mine = pl.BlockSpec((tokens, half), lambda j, m: (0, m[1]))
    tile = pl.BlockSpec((tokens, 2 * width), lambda j, m: (0, j))
    return gradient_call(
        grad_down_kernel, "gradient_down", chips, hidden // (2 * width), [tile, tile, mine, fixed],
        pl.BlockSpec((chips // 2, rows, half), lambda j, m: (0, 0, 0)), (chips // 2, rows, half), [],
    )(meta, *in_hbm(active, active_x), back_out, back_out_x)


def qkv_gradients(meta, chips, hidden, hidden_x, back_projected, back_projected_x, sums):
    tokens, width = hidden.shape
    wide = back_projected.shape[1]
    rows = width // chips
    if rows % 16 != 0:
        qkv = dot_tn(hidden, back_projected) + dot_tn(hidden_x, back_projected_x)
        table = jnp.pad(sums.T, ((0, 0), (0, 120)))
        both = ordered(jnp.concatenate([qkv, table], -1), meta[2 : 2 + chips], chips)
        return both[: chips // 2], both[chips // 2 :]
    specs = [pl.BlockSpec((tokens, width), lambda j, m: (0, 0))] * 2
    specs += [pl.BlockSpec((tokens, wide), lambda j, m: (0, 0))] * 2
    specs += [pl.BlockSpec((8, width), lambda j, m: (0, 0))]
    return gradient_call(
        grad_qkv_kernel, "gradient_qkv", chips, 1, specs,
        pl.BlockSpec((chips // 2, rows, wide + 128), lambda j, m: (0, 0, 0)),
        (chips // 2, rows, wide + 128),
        [pltpu.VMEM((width, wide + 128), BF16), pltpu.VMEM((width, 128), F32)],
    )(meta, *in_hbm(hidden, hidden_x), back_projected, back_projected_x, sums)


class Exchange:
    def __init__(self, dp):
        self.dp = dp
        self.chips = 2 * dp
        self.bits = int(math.log2(self.chips))
        self.core_pairs = [(s, s ^ 1) for s in range(4)]
        self.mirror_pairs = [(s, 3 - s) for s in range(4)]
        rest = list(range(2, self.bits))
        self.orders = ([1, 0] + rest, [0, 1] + rest[::-1])

    def swap_core(self, value):
        return lax.ppermute(value, "seq", self.core_pairs)

    def mirror(self, value):
        return lax.ppermute(value, "seq", self.mirror_pairs)

    def pairs(self, phase):
        result = []
        for device in range(2 * self.chips):
            chip = (device // 4) * 2 + (device % 4) // 2
            core = device % 2
            other = chip ^ (1 << self.orders[core][phase])
            result.append((device, (other // 2) * 4 + (other % 2) * 2 + core))
        return result

    def tables(self, chip, core):
        index = np.arange(self.chips)
        maps = []
        for order in self.orders:
            value = np.zeros_like(index)
            for phase, bit in enumerate(order):
                value |= ((index >> (self.bits - 1 - phase)) & 1) << bit
            maps.append(value.astype(np.int32))
        ids = chip ^ jnp.where(core == 0, jnp.asarray(maps[0]), jnp.asarray(maps[1]))
        relative = jnp.asarray(index.astype(np.int32)) ^ chip
        places = []
        for order in self.orders:
            place = jnp.zeros_like(relative)
            for phase, bit in enumerate(order):
                place = place | (((relative >> bit) & 1) << (self.bits - 1 - phase))
            places.append(place)
        return ids.astype(jnp.int32), jnp.where(core == 0, places[0], places[1]).astype(jnp.int32)


class Reduction:
    def __init__(self, exchange, keep, send):
        self.exchange, self.parts, self.phase = exchange, [keep], 0
        self.first, self.kind = send, send.dtype

    def message(self):
        if self.phase == 0:
            return self.first
        size = self.parts[-1].shape[0]
        terms = [part[size // 2 : size].astype(F32) for part in self.parts]
        return functools.reduce(jnp.add, terms).astype(self.kind)

    def partner(self, phase):
        dp, seq = lax.axis_index("dp"), lax.axis_index("seq")
        where = []
        for order in self.exchange.orders:
            bit = order[phase]
            if bit == 0:
                where.append((dp, (seq + 2) % 4))
            else:
                size = 1 << (bit - 1)
                where.append((dp + size - 2 * size * ((dp // size) % 2), seq))
        (dp0, seq0), (dp1, seq1) = where
        return dp0 + (seq % 2) * (dp1 - dp0), seq0 + (seq % 2) * (seq1 - seq0)

    def transfer(self, message):
        self.phase += 1
        return lax.ppermute(message, AXES, self.exchange.pairs(self.phase - 1))

    def arrived(self, value):
        self.parts.append(value)

    def complete(self):
        while self.phase < self.exchange.bits:
            self.arrived(self.transfer(self.message()))


def total(parts):
    return functools.reduce(jnp.add, [part[0].astype(F32) for part in parts])


class Move:
    def __init__(self, transfer, value):
        self.transfer, self.value = transfer, value

    def message(self):
        return self.value

    def arrived(self, value):
        self.value = value


def host(run, inputs, *moves):
    count = len(inputs)
    tied = lax.optimization_barrier(tuple(inputs) + tuple(move.message() for move in moves))
    results = tuple(run(*tied[:count]))
    got = tuple(move.transfer(message) for move, message in zip(moves, tied[count:]))
    tied = lax.optimization_barrier(results + got)
    for move, value in zip(moves, tied[len(results) :]):
        move.arrived(value)
    return tied[: len(results)]


def by_core(core, mine, theirs, axis):
    return jnp.where(
        core == 0,
        jnp.concatenate([mine, theirs], axis),
        jnp.concatenate([theirs, mine], axis),
    )


def small_call(kernel, name, shapes, operands, scratch=()):
    def spec(value):
        if value.ndim == 3 and value.dtype == BF16:
            return pl.BlockSpec((1,) + value.shape[1:], lambda i: (0, 0, 0))
        return pl.BlockSpec(value.shape, lambda i: (0,) * value.ndim)

    return pl.pallas_call(
        kernel,
        grid=(1,),
        in_specs=[spec(value) for value in operands],
        out_specs=[spec(shape) for shape in shapes],
        out_shape=shapes,
        scratch_shapes=list(scratch),
        compiler_params=pltpu.CompilerParams(vmem_limit_bytes=VMEM_BYTES),
        cost_estimate=SMALL_COST,
        name=name,
    )(*operands)


def collect(groups):
    counts = [len(parts) for parts, unused in groups]
    units = [unit for unused, unit in groups]
    totals = [parts[0].shape[1:] for parts, unused in groups]
    wide = totals[0][1]
    half = sum(rows for rows, unused in totals) // 2

    def kernel(*refs):
        refs = list(refs)
        core = lax.axis_index("seq") % 2
        mine, theirs = refs[sum(counts) : sum(counts) + 2]
        sums = refs[sum(counts) + 2 :]
        at = 0
        for count, unit, scratch in zip(counts, units, sums):
            parts, refs = refs[:count], refs[count:]
            scratch[...] = functools.reduce(jnp.add, [part[0].astype(F32) for part in parts])
            each = unit // 2
            for start in range(0, scratch.shape[0], unit):
                span = slice(at, at + each)
                mine[span, :] = scratch[pl.ds(pl.multiple_of(start + core * each, 8), each), :]
                theirs[span, :] = scratch[pl.ds(pl.multiple_of(start + (1 - core) * each, 8), each), :]
                at += each

    shape = jax.ShapeDtypeStruct((half, wide), F32)
    operands = in_hbm(*[part for parts, unused in groups for part in parts])
    return small_call(kernel, "collect", [shape, shape], operands, [pltpu.VMEM(t, F32) for t in totals])


def place_mlp(each, mine_a, theirs_a, mine_b, theirs_b):
    half = mine_a.shape[1]

    def kernel(*refs):
        ups, downs, outs = refs[4:]
        core = lax.axis_index("seq") % 2
        for layer in range(2):
            for side, value in ((core, refs[2 * layer]), (1 - core, refs[2 * layer + 1])):
                narrow = pl.ds(pl.multiple_of(side * half, 128), half)
                downs[layer, :, narrow] = value[: 4 * each, :]
                for unit in range(4):
                    lanes = pl.ds(pl.multiple_of(side * 4 * half + unit * half, 128), half)
                    ups[layer, :, lanes] = value[(4 + unit) * each : (5 + unit) * each, :]
                outs[layer, :, narrow] = value[8 * each :, :]

    shapes = [
        jax.ShapeDtypeStruct((2, each, 8 * half), F32), jax.ShapeDtypeStruct((2, 4 * each, 2 * half), F32),
        jax.ShapeDtypeStruct((2, each, 2 * half), F32),
    ]
    return small_call(kernel, "place", shapes, (mine_a, theirs_a, mine_b, theirs_b))


def place_qkv(mine_a, theirs_a, mine_b, theirs_b):
    each, wide = mine_a.shape
    wide -= 128

    def kernel(*refs):
        out, table = refs[4:]
        core = lax.axis_index("seq") % 2
        for layer in range(2):
            for side, value in ((core, refs[2 * layer]), (1 - core, refs[2 * layer + 1])):
                out[layer, :, pl.ds(pl.multiple_of(side * wide, 128), wide)] = value[:, :wide]
        table[...] = refs[0][:, wide:] + refs[1][:, wide:]

    shapes = [jax.ShapeDtypeStruct((2, each, 2 * wide), F32), jax.ShapeDtypeStruct((each, 128), F32)]
    return small_call(kernel, "place_qkv", shapes, (mine_a, theirs_a, mine_b, theirs_b))


def last_exchanges(last, before, up, down, theirs_b):
    keep, message = last.parts[0], last.first
    chunk = keep.shape[1:]
    each, wide = chunk[0] // 2, chunk[1]
    up_rows, down_rows, half = up.parts[0].shape[1], down.parts[0].shape[1], up.parts[0].shape[2]
    mesh = pl.DeviceIdType.MESH

    def kernel(keep, message, *refs):
        refs = list(refs)

        def take(count):
            taken = refs[:count]
            del refs[:count]
            return taken

        before_parts, up_parts, down_parts, (theirs_b,) = take(3), take(4), take(5), take(1)
        mine_a, got_a, got_b, mine_l, got_l, mine_q, got_q = take(7)
        land1, land2, land3, land4, q_land3, q_land4, up_land = take(7)
        send2, send3, send4, q_send3, q_send4, up_send = take(6)
        sums, up_sum, down_sum, swap_q, swap_q_land, swap_a, swap_a_land = take(7)
        send_sem, recv_sem = take(2)
        seq = lax.axis_index("seq")
        core = seq % 2
        other = lax.axis_index("dp"), seq + 1 - 2 * core
        partners = [last.partner(phase) for phase in range(4)]
        barrier = pltpu.get_barrier_semaphore()
        for partner in partners + [other]:
            pl.semaphore_signal(barrier, inc=1, device_id=partner, device_id_type=mesh)
        pl.semaphore_wait(barrier, 5)

        def remote(index, source, target, partner):
            return pltpu.make_async_remote_copy(
                src_ref=source, dst_ref=target, send_sem=send_sem.at[index], recv_sem=recv_sem.at[index],
                device_id=partner, device_id_type=mesh,
            )

        def added(values, kind=BF16):
            return functools.reduce(jnp.add, [value.astype(F32) for value in values]).astype(kind)

        def rows_of(ref, start, count, side):
            return ref[pl.ds(pl.multiple_of(start + side * count, 8), count), :]

        pieces = (slice(4, 8), slice(2, 4), slice(0, 2))
        first = [remote(k, message.at[p], land1.at[p], partners[0]) for k, p in zip((0, 1, 13), pieces)]
        second = [remote(2, send2.at[2:4], land2.at[2:4], partners[1]), remote(3, send2.at[0:2], land2.at[0:2], partners[1])]
        third, fourth = remote(4, send3, land3, partners[2]), remote(5, send4, land4, partners[3])
        q_third, q_fourth = remote(6, q_send3, q_land3, partners[2]), remote(7, q_send4, q_land4, partners[3])
        up_fourth = remote(8, up_send, up_land, partners[3])
        swap_b, swap_own = (remote(9 + k, swap_a.at[k], swap_a_land.at[k], other) for k in range(2))
        swap_qs = [remote(11 + k, swap_q.at[k], swap_q_land.at[k], other) for k in range(2)]

        for copy in first:
            copy.start()
        up_send[...] = added([part[1:2] for part in up_parts])
        up_fourth.start()
        q_send3[...] = added([part[2:4] for part in before_parts])
        q_third.start()
        swap_a[0] = theirs_b[...]
        swap_b.start()
        down_sum[...] = added([part[0] for part in down_parts], F32)
        up_sum[...] = added([part[0] for part in up_parts], F32)
        sums[1] = added([part[0] for part in before_parts], F32)

        first[0].wait()
        send2[...] = added([keep[4:8], land1[4:8]])
        for copy in second:
            copy.start()

        q_third.wait()
        q_send4[...] = added([part[1:2] for part in before_parts] + [q_land3[1:2]])
        q_fourth.start()
        sums[1] = sums[1] + q_land3[0].astype(F32)

        up_fourth.wait()
        up_sum[...] = up_sum[...] + up_land[0].astype(F32)
        at = 0
        for scratch, unit in ((down_sum, 8 * each), (up_sum, 2 * each)):
            count = unit // 2
            for start in range(0, scratch.shape[0], unit):
                mine_a[at : at + count, :] = rows_of(scratch, start, count, core)
                swap_a[1, at : at + count, :] = rows_of(scratch, start, count, 1 - core)
                at += count
        swap_own.start()
        swap_b.wait()
        got_b[...] = swap_a_land[0]

        first[1].wait()
        second[0].wait()
        send3[...] = added([keep[2:4], land1[2:4], land2[2:4]])
        third.start()

        q_fourth.wait()
        sums[1] = sums[1] + q_land4[0].astype(F32)
        mine_q[...] = rows_of(sums.at[1], 0, each, core)
        swap_q[1] = rows_of(sums.at[1], 0, each, 1 - core)
        swap_qs[1].start()
        swap_own.wait()
        got_a[...] = swap_a_land[1]

        first[2].wait()
        second[1].wait()
        sums[0] = added([keep[0], land1[0], land2[0]], F32)
        third.wait()
        send4[...] = added([keep[1:2], land1[1:2], land2[1:2], land3[1:2]])
        fourth.start()
        swap_qs[1].wait()
        got_q[...] = swap_q_land[1]
        sums[0] = sums[0] + land3[0].astype(F32)
        fourth.wait()
        sums[0] = sums[0] + land4[0].astype(F32)
        mine_l[...] = rows_of(sums.at[0], 0, each, core)
        swap_q[0] = rows_of(sums.at[0], 0, each, 1 - core)
        swap_qs[0].start()
        swap_qs[0].wait()
        got_l[...] = swap_q_land[0]

    def leading(count, value):
        return pl.BlockSpec((count,) + value.shape[1:], lambda i: (0, 0, 0))

    long = theirs_b.shape
    flat, out = pl.BlockSpec(long, lambda i: (0, 0)), pl.BlockSpec((each, wide), lambda i: (0, 0))
    up_chunk = (1, up_rows, half)
    return pl.pallas_call(
        kernel,
        grid=(1,),
        in_specs=[leading(8, keep), pl.BlockSpec(memory_space=pl.ANY)]
        + [leading(4, part) for part in before.parts] + [leading(2, part) for part in up.parts]
        + [leading(1, part) for part in down.parts] + [flat],
        out_specs=[flat] * 3 + [out] * 4,
        out_shape=[jax.ShapeDtypeStruct(long, F32)] * 3 + [jax.ShapeDtypeStruct((each, wide), F32)] * 4,
        scratch_shapes=[pltpu.VMEM((size,) + chunk, BF16) for size in (8, 4, 2, 1, 2, 1)]
        + [pltpu.VMEM(up_chunk, BF16)]
        + [pltpu.VMEM((size,) + chunk, BF16) for size in (4, 2, 1, 2, 1)]
        + [
            pltpu.VMEM(up_chunk, BF16),
            pltpu.VMEM((2,) + chunk, F32), pltpu.VMEM(up_chunk[1:], F32), pltpu.VMEM((down_rows, half), F32),
            pltpu.VMEM((2, each, wide), F32), pltpu.VMEM((2, each, wide), F32),
            pltpu.VMEM((2,) + long, F32), pltpu.VMEM((2,) + long, F32),
            pltpu.SemaphoreType.DMA((14,)), pltpu.SemaphoreType.DMA((14,)),
        ],
        compiler_params=pltpu.CompilerParams(
            vmem_limit_bytes=VMEM_BYTES, collective_id=0, has_side_effects=True
        ),
        cost_estimate=SMALL_COST,
        name="last_exchanges",
    )(*in_hbm(keep, message, *before.parts, *up.parts, *down.parts), theirs_b)


def unpack_mlp(share, rows, core, exchange):
    half, each = share.shape[1], rows // 2
    down = share[: 4 * rows].reshape(2, 4 * each, half)
    rest = share[4 * rows :].reshape(share.shape[0] // rows - 4, 2, each, half)

    def pick(which):
        return jnp.concatenate(
            [lax.dynamic_index_in_dim(down, which, 0, False),
             lax.dynamic_index_in_dim(rest, which, 1, False).reshape(-1, half)], 0)

    mine, theirs = pick(core), exchange.swap_core(pick(1 - core))

    def widen(value, start, count):
        value = value[start * each : (start + count) * each].reshape(count, each, half)
        return value.transpose(1, 0, 2).reshape(each, count * half)

    def join(start, count):
        return by_core(core, widen(mine, start, count), widen(theirs, start, count), 1)

    grad_down = by_core(core, mine[: 4 * each], theirs[: 4 * each], 1)
    return grad_down, join(4, 4), join(8, 1)


def unpack_qkv(share, core, exchange):
    rows, wide = share.shape
    split = share.reshape(2, rows // 2, wide)
    mine = lax.dynamic_index_in_dim(split, core, 0, False)
    theirs = exchange.swap_core(lax.dynamic_index_in_dim(split, 1 - core, 0, False))
    wide -= 128
    table = mine[:, wide : wide + 8] + theirs[:, wide : wide + 8]
    return by_core(core, mine[:, :wide], theirs[:, :wide], 1), table


def per_device(
    inputs, cotangent, task_table, type_counts,
    gain_one, bias_one, proj_qkv, proj_out, gain_two, bias_two, proj_up, proj_down,
):
    slots, rows, width = inputs.shape
    length = rows * lax.axis_size("seq")
    exchange = Exchange(lax.axis_size("dp"))
    place = lax.axis_index("seq")
    side, core = place // 2, place % 2
    chip = lax.axis_index("dp") * 2 + side
    low = jnp.minimum(place, 3 - place)
    own_first = place < 2
    flag = low.astype(jnp.int32).reshape(1)

    meta = jnp.concatenate([flag, core.astype(jnp.int32).reshape(1), *exchange.tables(chip, core)])

    def gather_slot(value, got):
        own = lax.dynamic_index_in_dim(value, side, 0, False)
        return jnp.where(own_first, jnp.concatenate([own, got]), jnp.concatenate([got, own]))

    choose = (task_table[:, None] == jnp.arange(TASKS, dtype=jnp.int32)[None, :]).astype(F32)
    targets = (length - type_counts[:, 0]).astype(F32)
    totals = jnp.sum(choose * targets[:, None], 0)
    bits = int(math.log2(exchange.dp))

    for bit in range(bits):
        pairs = [(d, d ^ (1 << bit)) for d in range(exchange.dp)]
        totals = totals + lax.ppermute(totals, "dp", pairs)
    cotangent_own, cotangent_send = (lax.dynamic_index_in_dim(cotangent, s, 0, False) for s in (side, 1 - side))
    got = exchange.mirror(lax.dynamic_index_in_dim(inputs, 1 - side, 0, False))
    got, totals, cotangent_own, cotangent_send = lax.optimization_barrier(
        (got, totals, cotangent_own, cotangent_send)
    )
    stream = gather_slot(inputs, got)
    factor = jnp.sum(totals) / TASKS / totals
    seq_weight = jnp.sum(choose * factor[None, :], 1)
    own_weight = lax.dynamic_index_in_dim(seq_weight, side, 0, False)
    own_start = lax.dynamic_index_in_dim(type_counts[:, 0], side, 0, False)
    chips = exchange.chips
    half = width // 2
    swap, mirror = exchange.swap_core, exchange.mirror

    def forward(layer, stream, moves_project, moves_attention):
        hidden, queries, own = host(
            lambda v: project(layer, v, gain_one, bias_one, proj_qkv), (stream,), *moves_project
        )
        other = swap(own)
        hidden_x = Move(swap, hidden)
        attended, logs = host(
            lambda q, k, kx: attention_forward(flag, q, k, kx), (queries, own, other),
            hidden_x, *moves_attention
        )
        attended_x = Move(swap, attended)
        middle, normed, active, slope, *output = host(
            lambda a, v: feed_forward(layer, a, v, proj_out, gain_two, bias_two, proj_up, proj_down),
            (attended, stream), attended_x,
        )
        moves = Move(swap, normed), Move(swap, active)
        return output, moves, (stream, hidden, hidden_x, queries, own, other, logs, attended, attended_x, middle, normed, active, slope)

    def attention_step(layer, back_attended, moves):
        unused, unused, unused, queries, own, other, logs, attended, unused, unused, unused, unused, unused = kept[layer]
        back_q, back_own, back_other = host(
            lambda b: attention_backward(flag, queries, own, other, b, attended, logs), (back_attended,), *moves
        )
        return back_q, back_own, Move(swap, back_other)

    def project_step(layer, back_q, back_own, back_got, back_branch, sums, moves, beside=lambda: (), ready=()):
        return host(
            lambda q, k, kx, *more: (
                *project_back(layer, meta, q, k, kx, proj_qkv, kept[layer][0], gain_one, back_branch, sums),
                *beside(*more),
            ),
            (back_q, back_own, back_got) + tuple(ready), *moves
        )

    def feed_step(layer, back_out, sums, moves):
        middle, slope = kept[layer][9], kept[layer][12]
        return host(
            lambda b: feed_back(layer, meta, b, slope, proj_up, proj_down, middle, gain_two, proj_out, sums),
            (back_out,), *moves
        )

    def down_step(layer, back_out, back_out_x, active_x, moves):
        active = kept[layer][11]
        return Reduction(exchange, *host(
            lambda b, bx: down_gradients(meta, chips, active, active_x, b, bx), (back_out, back_out_x), *moves
        ))

    def up_step(layer, back_up, back_up_x, back_branch, branch_x, normed_x, moves):
        normed, attended, attended_x = kept[layer][10], kept[layer][7], kept[layer][8].value
        return Reduction(exchange, *host(
            lambda b, bx: up_gradients(
                meta, chips, normed, normed_x, b, bx, attended, attended_x, back_branch, branch_x
            ),
            (back_up, back_up_x), *moves
        ))

    def qkv_step(layer, mine, theirs_x, sums, moves):
        hidden, hidden_x = kept[layer][1], kept[layer][2].value
        return Reduction(exchange, *host(
            lambda b, bx: qkv_gradients(meta, chips, hidden, hidden_x, b, bx, sums), (mine, theirs_x), *moves
        ))

    got_cotangent = Move(mirror, cotangent_send)
    (stream,), moves, saved = forward(0, stream, (), (got_cotangent,))
    kept = [saved]
    back_out, back_out_send = weigh(
        own_weight.reshape(1), own_start.reshape(1), cotangent_own, got_cotangent.value
    )
    back_out_x = Move(swap, back_out_send)
    (stream, stream_send), last_moves, saved = forward(1, stream, moves, (back_out_x,))
    normed_x, active_x = (move.value for move in moves)
    kept.append(saved)
    outputs_move = Move(mirror, stream_send)

    sums = jnp.zeros((8, width), F32)
    back_up, back_up_send, back_branch, branch_send, back_attended, sums = feed_step(
        1, back_out, sums, last_moves + (outputs_move,)
    )
    last_normed_x, last_active_x = (move.value for move in last_moves)
    back_up_x, branch_x = Move(swap, back_up_send), Move(swap, branch_send)
    down1 = down_step(1, back_out, back_out_x.value, last_active_x, (back_up_x, branch_x))
    back_q, back_own, back_got = attention_step(1, back_attended, (down1,))
    up1 = up_step(1, back_up, back_up_x.value, back_branch, branch_x.value, last_normed_x, (down1, back_got))
    mine, theirs, back_out, back_out_send, sums = project_step(
        1, back_q, back_own, back_got.value, back_branch, sums, (up1, down1)
    )
    theirs_x = Move(swap, theirs)
    down0 = down_step(0, back_out, swap(back_out_send), active_x, (theirs_x, up1, down1))
    back_up, back_up_send, back_branch, branch_send, back_attended, sums0 = feed_step(
        0, back_out, sums, (down0, up1)
    )
    back_up_x, branch_x = Move(swap, back_up_send), Move(swap, branch_send)
    qkv1 = qkv_step(1, mine, theirs_x.value, sums, (back_up_x, branch_x, down0, up1))
    up0 = up_step(0, back_up, back_up_x.value, back_branch, branch_x.value, normed_x, (qkv1,))
    back_q, back_own, back_got = attention_step(0, back_attended, (up0, down0))
    unit = width // chips

    def return_slot(value, got):
        own = jnp.where(own_first, value[:rows], value[rows:])
        return jnp.where(side == 0, jnp.stack([own, got]), jnp.stack([got, own]))

    each = unit // 2
    whole_tiles = each % 8 == 0 and exchange.bits == 4
    ready = (outputs_move.value,) + tuple(down1.parts) + tuple(up1.parts)

    def beside(got, *parts):
        count = len(down1.parts)
        return (return_slot(stream, got), *collect([(parts[:count], 8 * each), (parts[count:], unit)]))

    mine, theirs, back_out, back_out_send, sums, back_send, *finished = project_step(
        0, back_q, back_own, swap(back_got.value), back_branch, sums0, (up0, qkv1, down0),
        *((beside, ready) if whole_tiles else ()),
    )
    back_move = Move(mirror, back_send)
    qkv0 = qkv_step(0, mine, swap(theirs), sums, (up0, back_move))
    back_inputs = return_slot(back_out, back_move.value).astype(F32)
    if not whole_tiles:
        for one in (down0, down1, up0, up1, qkv0, qkv1):
            one.complete()
        shares = [jnp.concatenate([total(d.parts), total(u.parts)], 0) for d, u in ((down0, up0), (down1, up1))]
        down, up, out = (
            jnp.stack(value) for value in zip(*(unpack_mlp(share, unit, core, exchange) for share in shares))
        )
        (qkv_a, table), (qkv_b, unused) = (unpack_qkv(total(one.parts), core, exchange) for one in (qkv0, qkv1))
        qkv = jnp.stack([qkv_a, qkv_b])
        outputs = return_slot(stream, outputs_move.value)
    else:
        outputs, mine_b, theirs_b = finished
        mine_a, got_a, got_b, last_q, last_got, mine_q, got_q = last_exchanges(qkv0, qkv1, up0, down0, theirs_b)
        up, down, out = place_mlp(each, mine_a, got_a, mine_b, got_b)
        qkv, table = place_qkv(last_q, last_got, mine_q, got_q)
        table = table[:, :8]
    table = table.T.reshape(LAYERS, 4, each)
    return outputs, back_inputs, table[:, 0], table[:, 1], qkv, out, table[:, 2], table[:, 3], up, down


def solution(mesh):
    tokens = P("dp", "seq", None)
    shared = P(None, AXES)
    in_specs = (tokens, tokens, P("dp"), P("dp", None)) + (P(),) * 8
    out_specs = (
        tokens, tokens, shared, shared, P(None, AXES, None), P(None, AXES, None),
        shared, shared, P(None, AXES, None), P(None, AXES, None),
    )
    return jax.shard_map(
        per_device, mesh=mesh, in_specs=in_specs, out_specs=out_specs, check_vma=False
    )
```

profile of v0, /device:TPU:0, one launch (start us, length us, event | category | flops | bytes accessed | tf_op | source)
XLA Modules:
  0.0 314.5 jit_solution(11448123375346325805)
XLA Ops:
  1.9 2.5 collective-permute-start
  4.6 1.5 collective-permute-start.1
  8.2 1.6 collective-permute-start.2
  9.8 2.0 collective-permute-done.2
  11.7 2.6 collective-permute-start.3
  14.3 1.9 collective-permute-done.3
  17.4 5.9 %project.2 = (bf16[512,768]{1,0:T(8,128)(2,1)}, bf16[512,768]{1,0:T(8,128)(2,1)}, bf16[512,1536]{1,0:T(8,128)(2,1)}) custom-call(bf16[512,768]{1,0:T(8,128)(2,1)} %maximum_select_fusion.stream, f32[2,768]{1,0:T(2,128)S(1)} %copy-done.7, f32[2,768]{1,0:T(2,128)S(1)} %copy-done.8, bf16[2,768,2304]{2,1,0:T(8,128)(2,1)} %matrix.7), custom_call_target="tpu_custom_call" | custom-call | flops 1000 | bytes 1000 | tf_op jit(solution)/shard_map/project/pallas_call | solution.py:305
  23.3 3.6 %collective-permute-done.4.kx_ref.vx_ref = bf16[512,1536]{1,0:T(8,128)(2,1)S(1)} collective-permute-done((bf16[512,1536]{1,0:T(8,128)(2,1)}, bf16[512,1536]{1,0:T(8,128)(2,1)S(1)}, u32[]{:S(2)}, u32[]{:S(2)}) %collective-permute-start.4) | collective-permute-done | bytes 1572896 | tf_op jit(solution)/shard_map/ppermute | solution.py:733
  28.0 10.1 %attention_forward.2 = (bf16[512,768]{1,0:T(8,128)(2,1)}, f32[6,8,512]{2,1,0:T(8,128)}) custom-call(s32[1]{0:T(128)} %bitcast.meta, bf16[512,768]{1,0:T(8,128)(2,1)} %get-tuple-element.271.q_ref, bf16[512,1536]{1,0:T(8,128)(2,1)} %get-tuple-element.272.ko_ref.vo_ref, bf16[512,1536]{1,0:T(8,128)(2,1)} %get-tuple-element.272.ko_ref.vo_ref, ...), custom_call_target="tpu_custom_call" | custom-call | flops 1000 | bytes 1000 | tf_op jit(solution)/shard_map/attention_forward/pallas_call | solution.py:140
  38.5 15.5 %feed_forward.2 = (bf16[512,768]{1,0:T(8,128)(2,1)}, bf16[512,768]{1,0:T(8,128)(2,1)}, bf16[512,3072]{1,0:T(8,128)(2,1)}, bf16[512,3072]{1,0:T(8,128)(2,1)}, bf16[512,768]{1,0:T(8,128)(2,1)}) custom-call(bf16[512,768]{1,0:T(8,128)(2,1)} %get-tuple-element.286.attended.co.o_ref, bf16[512,768]{1,0:T(8,128)(2,1)} %maximum_select_fusion.stream, ...), custom_call_target="tpu_custom_call" | custom-call | flops 1000 | bytes 1000 | tf_op jit(solution)/shard_map/feed_forward/pallas_call | solution.py:370
  55.5 5.9 %project.3 = (bf16[512,768]{1,0:T(8,128)(2,1)}, bf16[512,768]{1,0:T(8,128)(2,1)}, bf16[512,1536]{1,0:T(8,128)(2,1)}) custom-call(bf16[512,768]{1,0:T(8,128)(2,1)} %get-tuple-element.313.stream, f32[2,768]{1,0:T(2,128)S(1)} %copy-done.7, f32[2,768]{1,0:T(2,128)S(1)} %copy-done.8, bf16[2,768,2304]{2,1,0:T(8,128)(2,1)} %matrix.7), custom_call_target="tpu_custom_call" | custom-call | flops 1000 | bytes 1000 | tf_op jit(solution)/shard_map/project/pallas_call | solution.py:305
  62.0 1.8 copy-done.20
  66.7 1.8 weigh.1
  69.6 9.5 %attention_forward.3 = (bf16[512,768]{1,0:T(8,128)(2,1)}, f32[6,8,512]{2,1,0:T(8,128)}) custom-call(s32[1]{0:T(128)} %bitcast.meta, bf16[512,768]{1,0:T(8,128)(2,1)} %get-tuple-element.304.q_ref, bf16[512,1536]{1,0:T(8,128)(2,1)} %get-tuple-element.305.ko_ref.vo_ref, bf16[512,1536]{1,0:T(8,128)(2,1)} %get-tuple-element.305.ko_ref.vo_ref, ...), custom_call_target="tpu_custom_call" | custom-call | flops 1000 | bytes 1000 | tf_op jit(solution)/shard_map/attention_forward/pallas_call | solution.py:140
  79.3 15.7 %feed_forward.3 = (bf16[512,768]{1,0:T(8,128)(2,1)}, bf16[512,768]{1,0:T(8,128)(2,1)}, bf16[512,3072]{1,0:T(8,128)(2,1)}, bf16[512,3072]{1,0:T(8,128)(2,1)}, bf1...) custom-call(bf16[512,768]{1,0:T(8,128)(2,1)} %get-tuple-element.320.attended.o_ref.co, ...), custom_call_target="tpu_custom_call" | custom-call | flops 1000 | bytes 1000 | tf_op jit(solution)/shard_map/feed_forward/pallas_call | solution.py:370
  96.5 14.2 %feed_back.2 = (bf16[512,1536]{1,0:T(8,128)(2,1)S(1)}, bf16[512,1536]{1,0:T(8,128)(2,1)S(1)}, bf16[512,768]{1,0:T(8,128)(2,1)S(1)}, bf16[512,384]{1,0:T(8,128)(2...) custom-call(s32[34]{0:T(128)S(1)} %pad_add_fusion.meta, ...), custom_call_target="tpu_custom_call" | custom-call | flops 1000 | bytes 1000 | tf_op jit(solution)/shard_map/feed_back/pallas_call | solution.py:440
  112.1 8.0 %gradient_down.2 = (bf16[8,192,384]{2,1,0:T(8,128)(2,1)}, bf16[8,192,384]{2,1,0:T(8,128)(2,1)}) custom-call(s32[34]{0:T(128)S(1)} %pad_add_fusion.meta, bf16[512,3072]{1,0:T(8,128)(2,1)} %get-tuple-element.334.ao, bf16[512,3072]{1,0:T(8,128)(2,1)} %collective-permute-done.15.ax, bf16[512,768]{1,0:T(8,128)(2,1)S(1)} %get-tuple-element.341.back_out.bo, ...), custom_call_target="tpu_custom_call" | custom-call | flops 1000 | bytes 1000 | tf_op jit(solution)/shard_map/gradient_down/pallas_call | solution.py:696
  120.1 1.5 collective-permute-start.19
  121.7 14.0 %attention_backward.2 = (bf16[512,768]{1,0:T(8,128)(2,1)S(1)}, bf16[2,512,768]{2,1,0:T(8,128)(2,1)}, bf16[2,512,768]{2,1,0:T(8,128)(2,1)S(1)}) custom-call(s32[1]{0:T(128)} %bitcast.meta, bf16[512,768]{1,0:T(8,128)(2,1)} %get-tuple-element.304.q_ref, bf16[512,1536]{1,0:T(8,128)(2,1)} %get-tuple-element.305.ko_ref.vo_ref, ...), custom_call_target="tpu_custom_call" | custom-call | flops 1000 | bytes 1000 | tf_op jit(solution)/shard_map/attention_backward/pallas_call | solution.py:247
  136.8 1.4 collective-permute-start.20
  138.3 7.7 %gradient_up.2 = (bf16[8,240,384]{2,1,0:T(8,128)(2,1)}, bf16[8,240,384]{2,1,0:T(8,128)(2,1)}) custom-call(s32[34]{0:T(128)S(1)} %pad_add_fusion.meta, bf16[512,768]{1,0:T(8,128)(2,1)} %get-tuple-element.333.ao, bf16[512,768]{1,0:T(8,128)(2,1)} %collective-permute-done.14.ax, bf16[512,1536]{1,0:T(8,128)(2,1)S(1)} %get-tuple-element.362.bo, ...), custom_call_target="tpu_custom_call" | custom-call | flops 1000 | bytes 1000 | tf_op jit(solution)/shard_map/gradient_up/pallas_call | solution.py:676
  146.9 1.5 collective-permute-start.22
  148.5 1.6 collective-permute-start.23
  150.1 7.1 %project_back.2 = (bf16[512,1152]{1,0:T(8,128)(2,1)S(1)}, bf16[512,1152]{1,0:T(8,128)(2,1)S(1)}, bf16[512,768]{1,0:T(8,128)(2,1)S(1)}, bf16[512,384]{1,0:T(8,128)(2,1)S(1)}, f32[8,768]{1,0:T(8,128)S(1)}) custom-call(s32[34]{0:T(128)S(1)} %pad_add_fusion.meta, bf16[512,768]{1,0:T(8,128)(2,1)} %copy-done.3, bf16[2,512,768]{2,1,0:T(8,128)(2,1)} %get-tuple-element.375.own, ...), custom_call_target="tpu_custom_call" | custom-call | flops 1000 | bytes 1000 | tf_op jit(solution)/shard_map/project_back/pallas_call | solution.py:523
  157.2 9.4 %collective-permute-done.22.refs_6_ = bf16[8,240,384]{2,1,0:T(8,128)(2,1)S(1)} collective-permute-done((bf16[8,240,384]{2,1,0:T(8,128)(2,1)}, bf16[8,240,384]{2,1,0:T(8,128)(2,1)S(1)}, u32[]{:S(2)}, u32[]{:S(2)}) %collective-permute-start.22) | collective-permute-done | bytes 1474592 | tf_op jit(solution)/shard_map/ppermute | solution.py:793
  166.9 1.4 collective-permute-done.24.bx
  168.4 1.3 collective-permute-start.26
  169.8 2.6 collective-permute-start.27
  172.4 8.0 %gradient_down.3 = (bf16[8,192,384]{2,1,0:T(8,128)(2,1)}, bf16[8,192,384]{2,1,0:T(8,128)(2,1)}) custom-call(s32[34]{0:T(128)S(1)} %pad_add_fusion.meta, bf16[512,3072]{1,0:T(8,128)(2,1)} %get-tuple-element.295.ao, bf16[512,3072]{1,0:T(8,128)(2,1)} %copy-done.20, bf16[512,768]{1,0:T(8,128)(2,1)S(1)} %get-tuple-element.401.bo.back_out, ...), custom_call_target="tpu_custom_call" | custom-call | flops 1000 | bytes 1000 | tf_op jit(solution)/shard_map/gradient_down/pallas_call | solution.py:696
  181.9 1.5 collective-permute-start.28
  183.4 1.6 collective-permute-start.29
  185.0 14.3 %feed_back.3 = (bf16[512,1536]{1,0:T(8,128)(2,1)S(1)}, bf16[512,1536]{1,0:T(8,128)(2,1)S(1)}, bf16[512,768]{1,0:T(8,128)(2,1)S(1)}, bf16[512,384]{1,0:T(8,128)(2...) custom-call(s32[34]{0:T(128)S(1)} %pad_add_fusion.meta, ...), custom_call_target="tpu_custom_call" | custom-call | flops 1000 | bytes 1000 | tf_op jit(solution)/shard_map/feed_back/pallas_call | solution.py:440
  200.5 1.4 collective-permute-start.33
  201.9 5.5 %gradient_qkv.2 = (bf16[8,48,1280]{2,1,0:T(8,128)(2,1)}, bf16[8,48,1280]{2,1,0:T(8,128)(2,1)}) custom-call(s32[34]{0:T(128)S(1)} %pad_add_fusion.meta, bf16[512,768]{1,0:T(8,128)(2,1)} %get-tuple-element.309.ao, bf16[512,768]{1,0:T(8,128)(2,1)} %copy-done.28, bf16[512,1152]{1,0:T(8,128)(2,1)S(1)} %get-tuple-element.424.bo, ...), custom_call_target="tpu_custom_call" | custom-call | flops 1000 | bytes 1000 | tf_op jit(solution)/shard_map/gradient_qkv/pallas_call | solution.py:714
  207.4 1.5 collective-permute-done.33.refs_9_
  210.4 7.7 %gradient_up.3 = (bf16[8,240,384]{2,1,0:T(8,128)(2,1)}, bf16[8,240,384]{2,1,0:T(8,128)(2,1)}) custom-call(s32[34]{0:T(128)S(1)} %pad_add_fusion.meta, bf16[512,768]{1,0:T(8,128)(2,1)} %get-tuple-element.294.ao, bf16[512,768]{1,0:T(8,128)(2,1)} %copy-done.30, bf16[512,1536]{1,0:T(8,128)(2,1)S(1)} %get-tuple-element.434.bo, ...), custom_call_target="tpu_custom_call" | custom-call | flops 1000 | bytes 1000 | tf_op jit(solution)/shard_map/gradient_up/pallas_call | solution.py:676
  218.3 5.7 %collective-permute-done.34.refs_1_ = bf16[8,48,1280]{2,1,0:T(8,128)(2,1)S(1)} collective-permute-done((bf16[8,48,1280]{2,1,0:T(8,128)(2,1)}, bf16[8,48,1280]{2,1,0:T(8,128)(2,1)S(1)}, u32[]{:S(2)}, u32[]{:S(2)}) %collective-permute-start.34) | collective-permute-done | bytes 983072 | tf_op jit(solution)/shard_map/ppermute | solution.py:793
  225.8 13.8 %attention_backward.3 = (bf16[512,768]{1,0:T(8,128)(2,1)S(1)}, bf16[2,512,768]{2,1,0:T(8,128)(2,1)}, bf16[2,512,768]{2,1,0:T(8,128)(2,1)S(1)}) custom-call(s32[1]{0:T(128)} %bitcast.meta, bf16[512,768]{1,0:T(8,128)(2,1)} %get-tuple-element.271.q_ref, bf16[512,1536]{1,0:T(8,128)(2,1)} %get-tuple-element.272.ko_ref.vo_ref, ...), custom_call_target="tpu_custom_call" | custom-call | flops 1000 | bytes 1000 | tf_op jit(solution)/shard_map/attention_backward/pallas_call | solution.py:247
  239.7 3.9 %collective-permute-done.35.refs_4_ = bf16[8,240,384]{2,1,0:T(8,128)(2,1)S(1)} collective-permute-done((bf16[8,240,384]{2,1,0:T(8,128)(2,1)}, bf16[8,240,384]{2,1,0:T(8,128)(2,1)S(1)}, u32[]{:S(2)}, u32[]{:S(2)}) %collective-permute-start.35) | collective-permute-done | bytes 1474592 | tf_op jit(solution)/shard_map/ppermute | solution.py:793
  247.7 1.3 collective-permute-start.39
  251.0 7.9 %project_back.3 = (bf16[512,1152]{1,0:T(8,128)(2,1)S(1)}, bf16[512,1152]{1,0:T(8,128)(2,1)S(1)}, bf16[512,768]{1,0:T(8,128)(2,1)S(1)}, bf16[512,384]{1,0:T(8,128...) custom-call(s32[34]{0:T(128)S(1)} %pad_add_fusion.meta, bf16[512,768]{1,0:T(8,128)(2,1)} %copy-done.4, ...), custom_call_target="tpu_custom_call" | custom-call | flops 1000 | bytes 1000 | tf_op jit(solution)/shard_map/project_back/pallas_call | solution.py:523
  258.9 1.9 collect.1
  261.8 2.2 collective-permute-done.39.refs_2_
  265.3 1.6 collective-permute-done.41.bx
  267.8 5.5 %gradient_qkv.3 = (bf16[8,48,1280]{2,1,0:T(8,128)(2,1)}, bf16[8,48,1280]{2,1,0:T(8,128)(2,1)}) custom-call(s32[34]{0:T(128)S(1)} %pad_add_fusion.meta, bf16[512,768]{1,0:T(8,128)(2,1)} %get-tuple-element.276.ao, bf16[512,768]{1,0:T(8,128)(2,1)} %collective-permute-done.5.ax, bf16[512,1152]{1,0:T(8,128)(2,1)S(1)} %get-tuple-element.495.bo, ...), custom_call_target="tpu_custom_call" | custom-call | flops 1000 | bytes 1000 | tf_op jit(solution)/shard_map/gradient_qkv/pallas_call | solution.py:714
  273.3 4.6 %collective-permute-done.42.refs_6_ = bf16[2,240,384]{2,1,0:T(8,128)(2,1)S(1)} collective-permute-done((bf16[2,240,384]{2,1,0:T(8,128)(2,1)S(1)}, bf16[2,240,384]{2,1,0:T(8,128)(2,1)S(1)}, u32[]{:S(2)}, u32[]{:S(2)}) %collective-permute-start.42) | collective-permute-done | bytes 368672 | tf_op jit(solution)/shard_map/ppermute | solution.py:793
  278.7 31.6 %last_exchanges.1 = (f32[216,384]{1,0:T(8,128)S(1)}, f32[216,384]{1,0:T(8,128)S(1)}, f32[216,384]{1,0:T(8,128)S(1)}, f32[24,1280]{1,0:T(8,128)S(1)}, f32[24,1280...) custom-call(bf16[8,48,1280]{2,1,0:T(8,128)(2,1)} %get-tuple-element.503.keep, ...), custom_call_target="tpu_custom_call" | custom-call | flops 1000 | bytes 1000 | tf_op jit(solution)/shard_map/last_exchanges/pallas_call | solution.py:1044
  311.8 1.3 fusion
  (188 shorter events, 35.9 us)
Async XLA Ops:
  1.9 14.2 %collective-permute-start = (bf16[256,768]{1,0:T(8,128)(2,1)S(1)}, bf16[256,768]{1,0:T(8,128)(2,1)S(1)}, u32[]{:S(2)}, u32[]{:S(2)}) collective-permute-start(bf16[256,768]{1,0:T(8,128)(2,1)S(1)} %get-tuple-element.523), channel_id=1, source_target_pairs={{0,3},{1,2},{2,1},{3,0},{4,7},{5,6},{6,5},{7,4},{8,11},{9,10},{10,... | collective-permute-start | bytes 1179656 | tf_op jit(solution)/shard_map/ppermute | solution.py:736
  4.6 3.6 %collective-permute-start.1 = (f32[3]{0:T(128)S(1)}, f32[3]{0:T(128)S(1)}, u32[]{:S(2)}, u32[]{:S(2)}) collective-permute-start(f32[3]{0:T(128)S(1)} %select_reduce_fusion.1), channel_id=1, source_target_pairs={{0,4},{4,0},{8,12},{12,8},{16,20},{20,16},{24,28},{28,24},{1,5},{5... | collective-permute-start | bytes 44 | tf_op jit(solution)/shard_map/ppermute | solution.py:1130
  8.2 3.5 %collective-permute-start.2 = (f32[3]{0:T(128)S(1)}, f32[3]{0:T(128)S(1)}, u32[]{:S(2)}, u32[]{:S(2)}) collective-permute-start(f32[3]{0:T(128)S(1)} %add.101), channel_id=1, source_target_pairs={{0,8},{4,12},{8,0},{12,4},{16,24},{20,28},{24,16},{28,20},{1,9},{5... | collective-permute-start | bytes 44 | tf_op jit(solution)/shard_map/ppermute | solution.py:1130
  11.7 4.4 %collective-permute-start.3 = (f32[3]{0:T(128)S(1)}, f32[3]{0:T(128)S(1)}, u32[]{:S(2)}, u32[]{:S(2)}) collective-permute-start(f32[3]{0:T(128)S(1)} %add.102), channel_id=1, source_target_pairs={{0,16},{4,20},{8,24},{12,28},{16,0},{20,4},{24,8},{28,12},{1,17},{... | collective-permute-start | bytes 44 | tf_op jit(solution)/shard_map/ppermute | solution.py:1130
  23.3 3.6 %collective-permute-start.4 = (bf16[512,1536]{1,0:T(8,128)(2,1)}, bf16[512,1536]{1,0:T(8,128)(2,1)S(1)}, u32[]{:S(2)}, u32[]{:S(2)}) collective-permute-start(bf16[512,1536]{1,0:T(8,128)(2,1)} %get-tuple-element.272.ko_ref.vo_ref), channel_id=1, source_target_pairs={{0,1},{1,0},{2,3},{3,2},{4,5},{5,4},{6,7},{7,6},{8,9},{9,8},{10,11... | collective-permute-start | bytes 4718600 | tf_op jit(solution)/shard_map/ppermute | solution.py:733
  26.9 11.3 %collective-permute-start.5 = (bf16[512,768]{1,0:T(8,128)(2,1)}, bf16[512,768]{1,0:T(8,128)(2,1)}, u32[]{:S(2)}, u32[]{:S(2)}) collective-permute-start(bf16[512,768]{1,0:T(8,128)(2,1)} %get-tuple-element.276.ao), channel_id=1, source_target_pairs={{0,1},{1,0},{2,3},{3,2},{4,5},{5,4},{6,7},{7,6},{8,9},{9,8},{10,11... | collective-permute-start | bytes 2359304 | tf_op jit(solution)/shard_map/ppermute | solution.py:733
  27.0 11.2 %collective-permute-start.6 = (bf16[256,768]{1,0:T(8,128)(2,1)}, bf16[256,768]{1,0:T(8,128)(2,1)S(1)}, u32[]{:S(2)}, u32[]{:S(2)}) collective-permute-start(bf16[256,768]{1,0:T(8,128)(2,1)} %get-tuple-element.277), channel_id=1, source_target_pairs={{0,3},{1,2},{2,1},{3,0},{4,7},{5,6},{6,5},{7,4},{8,11},{9,10},{10,... | collective-permute-start | bytes 1179656 | tf_op jit(solution)/shard_map/ppermute | solution.py:736
  38.2 15.9 %collective-permute-start.7 = (bf16[512,768]{1,0:T(8,128)(2,1)}, bf16[512,768]{1,0:T(8,128)(2,1)S(1)}, u32[]{:S(2)}, u32[]{:S(2)}) collective-permute-start(bf16[512,768]{1,0:T(8,128)(2,1)} %get-tuple-element.286.attended.co.o_ref), channel_id=1, source_target_pairs={{0,1},{1,0},{2,3},{3,2},{4,5},{5,4},{6,7},{7,6},{8,9},{9,8},{10,11... | collective-permute-start | bytes 2359304 | tf_op jit(solution)/shard_map/ppermute | solution.py:733
  55.0 7.0 %collective-permute-start.9 = (bf16[512,3072]{1,0:T(8,128)(2,1)}, bf16[512,3072]{1,0:T(8,128)(2,1)S(1)}, u32[]{:S(2)}, u32[]{:S(2)}) collective-permute-start(bf16[512,3072]{1,0:T(8,128)(2,1)} %get-tuple-element.295.ao), channel_id=1, source_target_pairs={{0,1},{1,0},{2,3},{3,2},{4,5},{5,4},{6,7},{7,6},{8,9},{9,8},{10,11... | collective-permute-start | bytes 9437192 | tf_op jit(solution)/shard_map/ppermute | solution.py:733
  55.2 6.8 %collective-permute-start.8 = (bf16[512,768]{1,0:T(8,128)(2,1)}, bf16[512,768]{1,0:T(8,128)(2,1)S(1)}, u32[]{:S(2)}, u32[]{:S(2)}) collective-permute-start(bf16[512,768]{1,0:T(8,128)(2,1)} %get-tuple-element.294.ao), channel_id=1, source_target_pairs={{0,1},{1,0},{2,3},{3,2},{4,5},{5,4},{6,7},{7,6},{8,9},{9,8},{10,11... | collective-permute-start | bytes 2359304 | tf_op jit(solution)/shard_map/ppermute | solution.py:733
  63.9 4.5 %collective-permute-start.10 = (bf16[512,1536]{1,0:T(8,128)(2,1)}, bf16[512,1536]{1,0:T(8,128)(2,1)S(1)}, u32[]{:S(2)}, u32[]{:S(2)}) collective-permute-start(bf16[512,1536]{1,0:T(8,128)(2,1)} %get-tuple-element.305.ko_ref.vo_ref), channel_id=1, source_target_pairs={{0,1},{1,0},{2,3},{3,2},{4,5},{5,4},{6,7},{7,6},{8,9},{9,8},{10,11... | collective-permute-start | bytes 4718600 | tf_op jit(solution)/shard_map/ppermute | solution.py:733
  68.5 10.7 %collective-permute-start.11 = (bf16[512,768]{1,0:T(8,128)(2,1)}, bf16[512,768]{1,0:T(8,128)(2,1)S(1)}, u32[]{:S(2)}, u32[]{:S(2)}) collective-permute-start(bf16[512,768]{1,0:T(8,128)(2,1)} %get-tuple-element.309.ao), channel_id=1, source_target_pairs={{0,1},{1,0},{2,3},{3,2},{4,5},{5,4},{6,7},{7,6},{8,9},{9,8},{10,11... | collective-permute-start | bytes 2359304 | tf_op jit(solution)/shard_map/ppermute | solution.py:733
  68.8 10.3 %collective-permute-start.12 = (bf16[512,384]{1,0:T(8,128)(2,1)S(1)}, bf16[512,384]{1,0:T(8,128)(2,1)S(1)}, u32[]{:S(2)}, u32[]{:S(2)}) collective-permute-start(bf16[512,384]{1,0:T(8,128)(2,1)S(1)} %get-tuple-element.310), channel_id=1, source_target_pairs={{0,1},{1,0},{2,3},{3,2},{4,5},{5,4},{6,7},{7,6},{8,9},{9,8},{10,11... | collective-permute-start | bytes 1179656 | tf_op jit(solution)/shard_map/ppermute | solution.py:733
  79.2 15.8 %collective-permute-start.13 = (bf16[512,768]{1,0:T(8,128)(2,1)}, bf16[512,768]{1,0:T(8,128)(2,1)S(1)}, u32[]{:S(2)}, u32[]{:S(2)}) collective-permute-start(bf16[512,768]{1,0:T(8,128)(2,1)} %get-tuple-element.320.attended.o_ref.co), channel_id=1, source_target_pairs={{0,1},{1,0},{2,3},{3,2},{4,5},{5,4},{6,7},{7,6},{8,9},{9,8},{10,11... | collective-permute-start | bytes 2359304 | tf_op jit(solution)/shard_map/ppermute | solution.py:733
  95.0 16.5 %collective-permute-start.15 = (bf16[512,3072]{1,0:T(8,128)(2,1)}, bf16[512,3072]{1,0:T(8,128)(2,1)}, u32[]{:S(2)}, u32[]{:S(2)}) collective-permute-start(bf16[512,3072]{1,0:T(8,128)(2,1)} %get-tuple-element.334.ao), channel_id=1, source_target_pairs={{0,1},{1,0},{2,3},{3,2},{4,5},{5,4},{6,7},{7,6},{8,9},{9,8},{10,11... | collective-permute-start | bytes 9437192 | tf_op jit(solution)/shard_map/ppermute | solution.py:733
  95.6 16.0 %collective-permute-start.14 = (bf16[512,768]{1,0:T(8,128)(2,1)}, bf16[512,768]{1,0:T(8,128)(2,1)}, u32[]{:S(2)}, u32[]{:S(2)}) collective-permute-start(bf16[512,768]{1,0:T(8,128)(2,1)} %get-tuple-element.333.ao), channel_id=1, source_target_pairs={{0,1},{1,0},{2,3},{3,2},{4,5},{5,4},{6,7},{7,6},{8,9},{9,8},{10,11... | collective-permute-start | bytes 2359304 | tf_op jit(solution)/shard_map/ppermute | solution.py:733
  95.6 15.9 %collective-permute-start.16 = (bf16[256,768]{1,0:T(8,128)(2,1)S(1)}, bf16[256,768]{1,0:T(8,128)(2,1)S(1)}, u32[]{:S(2)}, u32[]{:S(2)}) collective-permute-start(bf16[256,768]{1,0:T(8,128)(2,1)S(1)} %get-tuple-element.335), channel_id=1, source_target_pairs={{0,3},{1,2},{2,1},{3,0},{4,7},{5,6},{6,5},{7,4},{8,11},{9,10},{10,... | collective-permute-start | bytes 1179656 | tf_op jit(solution)/shard_map/ppermute | solution.py:736
  111.6 8.6 %collective-permute-start.17 = (bf16[512,1536]{1,0:T(8,128)(2,1)S(1)}, bf16[512,1536]{1,0:T(8,128)(2,1)S(1)}, u32[]{:S(2)}, u32[]{:S(2)}) collective-permute-start(bf16[512,1536]{1,0:T(8,128)(2,1)S(1)} %get-tuple-element.345), channel_id=1, source_target_pairs={{0,1},{1,0},{2,3},{3,2},{4,5},{5,4},{6,7},{7,6},{8,9},{9,8},{10,11... | collective-permute-start | bytes 4718600 | tf_op jit(solution)/shard_map/ppermute | solution.py:733
  112.0 8.1 %collective-permute-start.18 = (bf16[512,384]{1,0:T(8,128)(2,1)S(1)}, bf16[512,384]{1,0:T(8,128)(2,1)S(1)}, u32[]{:S(2)}, u32[]{:S(2)}) collective-permute-start(bf16[512,384]{1,0:T(8,128)(2,1)S(1)} %get-tuple-element.346), channel_id=1, source_target_pairs={{0,1},{1,0},{2,3},{3,2},{4,5},{5,4},{6,7},{7,6},{8,9},{9,8},{10,11... | collective-permute-start | bytes 1179656 | tf_op jit(solution)/shard_map/ppermute | solution.py:733
  120.1 16.5 %collective-permute-start.19 = (bf16[8,192,384]{2,1,0:T(8,128)(2,1)}, bf16[8,192,384]{2,1,0:T(8,128)(2,1)S(1)}, u32[]{:S(2)}, u32[]{:S(2)}) collective-permute-start(bf16[8,192,384]{2,1,0:T(8,128)(2,1)} %get-tuple-element.353), channel_id=1, source_target_pairs={{0,4},{1,3},{2,6},{3,1},{4,0},{5,7},{6,2},{7,5},{8,12},{9,11},{10,... | collective-permute-start | bytes 3538952 | tf_op jit(solution)/shard_map/ppermute | solution.py:793
  136.6 30.0 %copy-start.19 = (bf16[8,192,384]{2,1,0:T(8,128)(2,1)}, bf16[8,192,384]{2,1,0:T(8,128)(2,1)S(1)}, u32[]{:S(2)}) copy-start(bf16[8,192,384]{2,1,0:T(8,128)(2,1)S(1)} %collective-permute-done.19.refs_1_) | copy-start | bytes 3538948
  136.8 10.0 %collective-permute-start.21 = (bf16[2,512,768]{2,1,0:T(8,128)(2,1)S(1)}, bf16[2,512,768]{2,1,0:T(8,128)(2,1)S(1)}, u32[]{:S(2)}, u32[]{:S(2)}) collective-permute-start(bf16[2,512,768]{2,1,0:T(8,128)(2,1)S(1)} %get-tuple-element.370), channel_id=1, source_target_pairs={{0,1},{1,0},{2,3},{3,2},{4,5},{5,4},{6,7},{7,6},{8,9},{9,8},{10,11... | collective-permute-start | bytes 4718600 | tf_op jit(solution)/shard_map/ppermute | solution.py:733
  136.8 9.9 %collective-permute-start.20 = (bf16[4,192,384]{2,1,0:T(8,128)(2,1)S(1)}, bf16[4,192,384]{2,1,0:T(8,128)(2,1)S(1)}, u32[]{:S(2)}, u32[]{:S(2)}) collective-permute-start(bf16[4,192,384]{2,1,0:T(8,128)(2,1)S(1)} %add_convert_fusion.3), channel_id=1, source_target_pairs={{0,2},{1,5},{2,0},{3,7},{4,6},{5,1},{6,4},{7,3},{8,10},{9,13},{10,... | collective-permute-start | bytes 1769480 | tf_op jit(solution)/shard_map/ppermute | solution.py:793
  146.9 19.6 %collective-permute-start.22 = (bf16[8,240,384]{2,1,0:T(8,128)(2,1)}, bf16[8,240,384]{2,1,0:T(8,128)(2,1)S(1)}, u32[]{:S(2)}, u32[]{:S(2)}) collective-permute-start(bf16[8,240,384]{2,1,0:T(8,128)(2,1)} %get-tuple-element.383), channel_id=1, source_target_pairs={{0,4},{1,3},{2,6},{3,1},{4,0},{5,7},{6,2},{7,5},{8,12},{9,11},{10,... | collective-permute-start | bytes 4423688 | tf_op jit(solution)/shard_map/ppermute | solution.py:793
  148.5 8.7 %collective-permute-start.23 = (bf16[2,192,384]{2,1,0:T(8,128)(2,1)S(1)}, bf16[2,192,384]{2,1,0:T(8,128)(2,1)S(1)}, u32[]{:S(2)}, u32[]{:S(2)}) collective-permute-start(bf16[2,192,384]{2,1,0:T(8,128)(2,1)S(1)} %add_convert_fusion.8), channel_id=1, source_target_pairs={{0,8},{1,17},{2,10},{3,19},{4,12},{5,21},{6,14},{7,23},{8,0},{9,25... | collective-permute-start | bytes 884744 | tf_op jit(solution)/shard_map/ppermute | solution.py:793
  166.6 32.8 %copy-start.13 = (bf16[8,240,384]{2,1,0:T(8,128)(2,1)}, bf16[8,240,384]{2,1,0:T(8,128)(2,1)S(1)}, u32[]{:S(2)}) copy-start(bf16[8,240,384]{2,1,0:T(8,128)(2,1)S(1)} %collective-permute-done.22.refs_6_) | copy-start | bytes 4423684
  166.6 1.7 collective-permute-start.24
  168.3 12.1 %collective-permute-start.25 = (bf16[512,1152]{1,0:T(8,128)(2,1)S(1)}, bf16[512,1152]{1,0:T(8,128)(2,1)S(1)}, u32[]{:S(2)}, u32[]{:S(2)}) collective-permute-start(bf16[512,1152]{1,0:T(8,128)(2,1)S(1)} %get-tuple-element.396), channel_id=1, source_target_pairs={{0,1},{1,0},{2,3},{3,2},{4,5},{5,4},{6,7},{7,6},{8,9},{9,8},{10,11... | collective-permute-start | bytes 3538952 | tf_op jit(solution)/shard_map/ppermute | solution.py:733
  168.4 11.9 %collective-permute-start.26 = (bf16[4,240,384]{2,1,0:T(8,128)(2,1)S(1)}, bf16[4,240,384]{2,1,0:T(8,128)(2,1)S(1)}, u32[]{:S(2)}, u32[]{:S(2)}) collective-permute-start(bf16[4,240,384]{2,1,0:T(8,128)(2,1)S(1)} %add_convert_fusion.1), channel_id=1, source_target_pairs={{0,2},{1,5},{2,0},{3,7},{4,6},{5,1},{6,4},{7,3},{8,10},{9,13},{10,... | collective-permute-start | bytes 2211848 | tf_op jit(solution)/shard_map/ppermute | solution.py:793
  169.8 10.6 %collective-permute-start.27 = (bf16[1,192,384]{2,1,0:T(8,128)(2,1)S(1)}, bf16[1,192,384]{2,1,0:T(8,128)(2,1)S(1)}, u32[]{:S(2)}, u32[]{:S(2)}) collective-permute-start(bf16[1,192,384]{2,1,0:T(8,128)(2,1)S(1)} %add_convert_fusion.11), channel_id=1, source_target_pairs={{0,16},{1,9},{2,18},{3,11},{4,20},{5,13},{6,22},{7,15},{8,24},{9,1... | collective-permute-start | bytes 442376 | tf_op jit(solution)/shard_map/ppermute | solution.py:793
  181.9 17.4 %collective-permute-start.28 = (bf16[8,192,384]{2,1,0:T(8,128)(2,1)S(1)}, bf16[8,192,384]{2,1,0:T(8,128)(2,1)S(1)}, u32[]{:S(2)}, u32[]{:S(2)}) collective-permute-start(bf16[8,192,384]{2,1,0:T(8,128)(2,1)S(1)} %copy-done.42), channel_id=1, source_target_pairs={{0,4},{1,3},{2,6},{3,1},{4,0},{5,7},{6,2},{7,5},{8,12},{9,11},{10,... | collective-permute-start | bytes 3538952 | tf_op jit(solution)/shard_map/ppermute | solution.py:793
  183.4 15.9 %collective-permute-start.29 = (bf16[2,240,384]{2,1,0:T(8,128)(2,1)S(1)}, bf16[2,240,384]{2,1,0:T(8,128)(2,1)S(1)}, u32[]{:S(2)}, u32[]{:S(2)}) collective-permute-start(bf16[2,240,384]{2,1,0:T(8,128)(2,1)S(1)} %add_convert_fusion.6), channel_id=1, source_target_pairs={{0,8},{1,17},{2,10},{3,19},{4,12},{5,21},{6,14},{7,23},{8,0},{9,25... | collective-permute-start | bytes 1105928 | tf_op jit(solution)/shard_map/ppermute | solution.py:793
  199.3 45.3 %copy-start.17 = (bf16[8,192,384]{2,1,0:T(8,128)(2,1)}, bf16[8,192,384]{2,1,0:T(8,128)(2,1)S(1)}, u32[]{:S(2)}) copy-start(bf16[8,192,384]{2,1,0:T(8,128)(2,1)S(1)} %collective-permute-done.28.refs_8_) | copy-start | bytes 3538948
  199.6 10.0 %collective-permute-start.30 = (bf16[512,1536]{1,0:T(8,128)(2,1)S(1)}, bf16[512,1536]{1,0:T(8,128)(2,1)S(1)}, u32[]{:S(2)}, u32[]{:S(2)}) collective-permute-start(bf16[512,1536]{1,0:T(8,128)(2,1)S(1)} %get-tuple-element.428), channel_id=1, source_target_pairs={{0,1},{1,0},{2,3},{3,2},{4,5},{5,4},{6,7},{7,6},{8,9},{9,8},{10,11... | collective-permute-start | bytes 4718600 | tf_op jit(solution)/shard_map/ppermute | solution.py:733
  199.7 9.9 %collective-permute-start.32 = (bf16[4,192,384]{2,1,0:T(8,128)(2,1)S(1)}, bf16[4,192,384]{2,1,0:T(8,128)(2,1)S(1)}, u32[]{:S(2)}, u32[]{:S(2)}) collective-permute-start(bf16[4,192,384]{2,1,0:T(8,128)(2,1)S(1)} %add_convert_fusion.2), channel_id=1, source_target_pairs={{0,2},{1,5},{2,0},{3,7},{4,6},{5,1},{6,4},{7,3},{8,10},{9,13},{10,... | collective-permute-start | bytes 1769480 | tf_op jit(solution)/shard_map/ppermute | solution.py:793
  200.5 8.4 %collective-permute-start.31 = (bf16[512,384]{1,0:T(8,128)(2,1)S(1)}, bf16[512,384]{1,0:T(8,128)(2,1)S(1)}, u32[]{:S(2)}, u32[]{:S(2)}) collective-permute-start(bf16[512,384]{1,0:T(8,128)(2,1)S(1)} %get-tuple-element.429), channel_id=1, source_target_pairs={{0,1},{1,0},{2,3},{3,2},{4,5},{5,4},{6,7},{7,6},{8,9},{9,8},{10,11... | collective-permute-start | bytes 1179656 | tf_op jit(solution)/shard_map/ppermute | solution.py:733
  200.5 8.4 %collective-permute-start.33 = (bf16[1,240,384]{2,1,0:T(8,128)(2,1)S(1)}, bf16[1,240,384]{2,1,0:T(8,128)(2,1)S(1)}, u32[]{:S(2)}, u32[]{:S(2)}) collective-permute-start(bf16[1,240,384]{2,1,0:T(8,128)(2,1)S(1)} %add_convert_fusion.9), channel_id=1, source_target_pairs={{0,16},{1,9},{2,18},{3,11},{4,20},{5,13},{6,22},{7,15},{8,24},{9,1... | collective-permute-start | bytes 552968 | tf_op jit(solution)/shard_map/ppermute | solution.py:793
  209.7 35.0 %copy-start.25 = (bf16[4,192,384]{2,1,0:T(8,128)(2,1)}, bf16[4,192,384]{2,1,0:T(8,128)(2,1)S(1)}, u32[]{:S(2)}) copy-start(bf16[4,192,384]{2,1,0:T(8,128)(2,1)S(1)} %collective-permute-done.32.refs_9_) | copy-start | bytes 1769476
  209.7 14.3 %collective-permute-start.34 = (bf16[8,48,1280]{2,1,0:T(8,128)(2,1)}, bf16[8,48,1280]{2,1,0:T(8,128)(2,1)S(1)}, u32[]{:S(2)}, u32[]{:S(2)}) collective-permute-start(bf16[8,48,1280]{2,1,0:T(8,128)(2,1)} %get-tuple-element.441), channel_id=1, source_target_pairs={{0,4},{1,3},{2,6},{3,1},{4,0},{5,7},{6,2},{7,5},{8,12},{9,11},{10,... | collective-permute-start | bytes 2949128 | tf_op jit(solution)/shard_map/ppermute | solution.py:793
  224.0 19.6 %collective-permute-start.35 = (bf16[8,240,384]{2,1,0:T(8,128)(2,1)}, bf16[8,240,384]{2,1,0:T(8,128)(2,1)S(1)}, u32[]{:S(2)}, u32[]{:S(2)}) collective-permute-start(bf16[8,240,384]{2,1,0:T(8,128)(2,1)} %get-tuple-element.449), channel_id=1, source_target_pairs={{0,4},{1,3},{2,6},{3,1},{4,0},{5,7},{6,2},{7,5},{8,12},{9,11},{10,... | collective-permute-start | bytes 4423688 | tf_op jit(solution)/shard_map/ppermute | solution.py:793
  224.7 14.9 %collective-permute-start.36 = (bf16[2,192,384]{2,1,0:T(8,128)(2,1)S(1)}, bf16[2,192,384]{2,1,0:T(8,128)(2,1)S(1)}, u32[]{:S(2)}, u32[]{:S(2)}) collective-permute-start(bf16[2,192,384]{2,1,0:T(8,128)(2,1)S(1)} %add_convert_fusion.7), channel_id=1, source_target_pairs={{0,8},{1,17},{2,10},{3,19},{4,12},{5,21},{6,14},{7,23},{8,0},{9,25... | collective-permute-start | bytes 884744 | tf_op jit(solution)/shard_map/ppermute | solution.py:793
  243.6 3.4 %collective-permute-start.37 = (bf16[2,512,768]{2,1,0:T(8,128)(2,1)S(1)}, bf16[2,512,768]{2,1,0:T(8,128)(2,1)S(1)}, u32[]{:S(2)}, u32[]{:S(2)}) collective-permute-start(bf16[2,512,768]{2,1,0:T(8,128)(2,1)S(1)} %get-tuple-element.453), channel_id=1, source_target_pairs={{0,1},{1,0},{2,3},{3,2},{4,5},{5,4},{6,7},{7,6},{8,9},{9,8},{10,11... | collective-permute-start | bytes 4718600 | tf_op jit(solution)/shard_map/ppermute | solution.py:733
  247.0 17.0 %collective-permute-start.38 = (bf16[4,240,384]{2,1,0:T(8,128)(2,1)}, bf16[4,240,384]{2,1,0:T(8,128)(2,1)}, u32[]{:S(2)}, u32[]{:S(2)}) collective-permute-start(bf16[4,240,384]{2,1,0:T(8,128)(2,1)} %add_convert_fusion), channel_id=1, source_target_pairs={{0,2},{1,5},{2,0},{3,7},{4,6},{5,1},{6,4},{7,3},{8,10},{9,13},{10,... | collective-permute-start | bytes 2211848 | tf_op jit(solution)/shard_map/ppermute | solution.py:793
  247.7 16.3 %collective-permute-start.39 = (bf16[4,48,1280]{2,1,0:T(8,128)(2,1)}, bf16[4,48,1280]{2,1,0:T(8,128)(2,1)}, u32[]{:S(2)}, u32[]{:S(2)}) collective-permute-start(bf16[4,48,1280]{2,1,0:T(8,128)(2,1)} %add_convert_fusion.4), channel_id=1, source_target_pairs={{0,2},{1,5},{2,0},{3,7},{4,6},{5,1},{6,4},{7,3},{8,10},{9,13},{10,... | collective-permute-start | bytes 1474568 | tf_op jit(solution)/shard_map/ppermute | solution.py:793
  249.0 12.8 %collective-permute-start.40 = (bf16[1,192,384]{2,1,0:T(8,128)(2,1)S(1)}, bf16[1,192,384]{2,1,0:T(8,128)(2,1)S(1)}, u32[]{:S(2)}, u32[]{:S(2)}) collective-permute-start(bf16[1,192,384]{2,1,0:T(8,128)(2,1)S(1)} %add_convert_fusion.10), channel_id=1, source_target_pairs={{0,16},{1,9},{2,18},{3,11},{4,20},{5,13},{6,22},{7,15},{8,24},{9,1... | collective-permute-start | bytes 442376 | tf_op jit(solution)/shard_map/ppermute | solution.py:793
  264.0 2.8 collective-permute-start.41
  266.9 11.1 %collective-permute-start.43 = (bf16[256,768]{1,0:T(8,128)(2,1)S(1)}, bf16[256,768]{1,0:T(8,128)(2,1)S(1)}, u32[]{:S(2)}, u32[]{:S(2)}) collective-permute-start(bf16[256,768]{1,0:T(8,128)(2,1)S(1)} %get-tuple-element.501), channel_id=1, source_target_pairs={{0,3},{1,2},{2,1},{3,0},{4,7},{5,6},{6,5},{7,4},{8,11},{9,10},{10,... | collective-permute-start | bytes 1179656 | tf_op jit(solution)/shard_map/ppermute | solution.py:736
  267.3 10.6 %collective-permute-start.42 = (bf16[2,240,384]{2,1,0:T(8,128)(2,1)S(1)}, bf16[2,240,384]{2,1,0:T(8,128)(2,1)S(1)}, u32[]{:S(2)}, u32[]{:S(2)}) collective-permute-start(bf16[2,240,384]{2,1,0:T(8,128)(2,1)S(1)} %add_convert_fusion.5), channel_id=1, source_target_pairs={{0,8},{1,17},{2,10},{3,19},{4,12},{5,21},{6,14},{7,23},{8,0},{9,25... | collective-permute-start | bytes 1105928 | tf_op jit(solution)/shard_map/ppermute | solution.py:793
  (41 other events, 389.8 us)
where the time goes:
time: 318 us; the launch traced here: 315 us
  Pallas kernels  214 us (67%)
  waiting for transfers between devices  43.3 us (14%)
  starting transfers between devices  34.3 us (11%)
  local copies, waits for them, and re-layouts  10.8 us (3%)
  other arithmetic  10.3 us (3%)
    pallas_call x1, Pallas kernels, last_exchanges(): pl.pallas_call(kernel, grid=(1,), in_specs=[leading(8, keep), pl.BlockSpe...  31.6 us
    pallas_call x2, Pallas kernels, feed_forward(): pl.pallas_call(functools.partial(feed_forward_kernel, layer, steps), grid...  31.2 us
    ppermute x17, waiting for transfers between devices, transfer(): return lax.ppermute(message, AXES, self.exchange.pairs(self.phase - 1))  29.8 us
    pallas_call x2, Pallas kernels, feed_back(): pl.pallas_call(functools.partial(feed_back_kernel, layer, steps), grid_sp...  28.5 us
    pallas_call x2, Pallas kernels, attention_backward(): pl.pallas_call(attention_backward_kernel, grid_spec=pltpu.PrefetchScalarG...  27.8 us
    ppermute x17, starting transfers between devices, transfer(): return lax.ppermute(message, AXES, self.exchange.pairs(self.phase - 1))  21.1 us
    pallas_call x2, Pallas kernels, attention_forward(): pl.pallas_call(attention_forward_kernel, grid_spec=pltpu.PrefetchScalarGr...  19.6 us
    pallas_call x2, Pallas kernels, down_gradients(): gradient_call(grad_down_kernel, 'gradient_down', chips, hidden // (2 * wi...  16 us
  transfers between devices with their start and end apart: 44, of which 18 were waited for; matrix products, arithmetic and copies ran while one was open for 3% of the time, Pallas kernels for 55%

commit v1 on v0

--- a/solution.py
+++ b/solution.py
@@ -926,7 +926,10 @@
     up_rows, down_rows, half = up.parts[0].shape[1], down.parts[0].shape[1], up.parts[0].shape[2]
     mesh = pl.DeviceIdType.MESH
 
-    def kernel(keep, message, *refs):
+    loaded = [(8, keep)] + [(4, v) for v in before.parts] + [(2, v) for v in up.parts] + [(1, v) for v in down.parts]
+    buffers = [pltpu.VMEM((size,) + value.shape[1:], BF16) for size, value in loaded]
+
+    def kernel(*refs):
         refs = list(refs)
 
         def take(count):
@@ -934,12 +937,19 @@
             del refs[:count]
             return taken
 
-        before_parts, up_parts, down_parts, (theirs_b,) = take(3), take(4), take(5), take(1)
+        given, (message, theirs_b) = take(len(loaded)), take(2)
         mine_a, got_a, got_b, mine_l, got_l, mine_q, got_q = take(7)
         land1, land2, land3, land4, q_land3, q_land4, up_land = take(7)
         send2, send3, send4, q_send3, q_send4, up_send = take(6)
         sums, up_sum, down_sum, swap_q, swap_q_land, swap_a, swap_a_land = take(7)
-        send_sem, recv_sem = take(2)
+        send_sem, recv_sem, load_sem = take(3)
+        held = take(len(loaded))
+        keep, before_parts, up_parts, down_parts = held[0], held[1:4], held[4:8], held[8:]
+        loads = [
+            pltpu.make_async_copy(ref.at[0 : loaded[k][0]], held[k], load_sem.at[k]) for k, ref in enumerate(given)
+        ]
+        for load in loads:
+            load.start()
         seq = lax.axis_index("seq")
         core = seq % 2
         other = lax.axis_index("dp"), seq + 1 - 2 * core
@@ -972,6 +982,8 @@
 
         for copy in first:
             copy.start()
+        for load in loads:
+            load.wait()
         up_send[...] = added([part[1:2] for part in up_parts])
         up_fourth.start()
         q_send3[...] = added([part[2:4] for part in before_parts])
@@ -1035,18 +1047,13 @@
         swap_qs[0].wait()
         got_l[...] = swap_q_land[0]
 
-    def leading(count, value):
-        return pl.BlockSpec((count,) + value.shape[1:], lambda i: (0, 0, 0))
-
     long = theirs_b.shape
     flat, out = pl.BlockSpec(long, lambda i: (0, 0)), pl.BlockSpec((each, wide), lambda i: (0, 0))
     up_chunk = (1, up_rows, half)
     return pl.pallas_call(
         kernel,
         grid=(1,),
-        in_specs=[leading(8, keep), pl.BlockSpec(memory_space=pl.ANY)]
-        + [leading(4, part) for part in before.parts] + [leading(2, part) for part in up.parts]
-        + [leading(1, part) for part in down.parts] + [flat],
+        in_specs=[pl.BlockSpec(memory_space=pl.ANY)] * (len(loaded) + 1) + [flat],
         out_specs=[flat] * 3 + [out] * 4,
         out_shape=[jax.ShapeDtypeStruct(long, F32)] * 3 + [jax.ShapeDtypeStruct((each, wide), F32)] * 4,
         scratch_shapes=[pltpu.VMEM((size,) + chunk, BF16) for size in (8, 4, 2, 1, 2, 1)]
@@ -1058,13 +1065,14 @@
             pltpu.VMEM((2, each, wide), F32), pltpu.VMEM((2, each, wide), F32),
             pltpu.VMEM((2,) + long, F32), pltpu.VMEM((2,) + long, F32),
             pltpu.SemaphoreType.DMA((14,)), pltpu.SemaphoreType.DMA((14,)),
-        ],
+            pltpu.SemaphoreType.DMA((len(loaded),)),
+        ] + buffers,
         compiler_params=pltpu.CompilerParams(
             vmem_limit_bytes=VMEM_BYTES, collective_id=0, has_side_effects=True
         ),
         cost_estimate=SMALL_COST,
         name="last_exchanges",
-    )(*in_hbm(keep, message, *before.parts, *up.parts, *down.parts), theirs_b)
+    )(*in_hbm(*[value for unused, value in loaded], message), theirs_b)
 
 
 def unpack_mlp(share, rows, core, exchange):

time: 318 us -> 316 us (level)
  transfers between devices with their start and end apart: 44 -> 44, of which waited for: 18 -> 18; matrix products, arithmetic and copies ran while one was open for 3% -> 3% of each run, Pallas kernels for 55% -> 56%
where the time goes in v1:
time: 316 us; the launch traced here: 312 us
  Pallas kernels  211 us (67%)
  waiting for transfers between devices  43.3 us (14%)
  starting transfers between devices  34.3 us (11%)
  local copies, waits for them, and re-layouts  10.8 us (3%)
  other arithmetic  10.3 us (3%)
    pallas_call x2, Pallas kernels, feed_forward(): pl.pallas_call(functools.partial(feed_forward_kernel, layer, steps), grid...  31.2 us
    ppermute x17, waiting for transfers between devices, transfer(): return lax.ppermute(message, AXES, self.exchange.pairs(self.phase - 1))  29.8 us
    pallas_call x1, Pallas kernels, last_exchanges(): pl.pallas_call(kernel, grid=(1,), in_specs=[pl.BlockSpec(memory_space=pl....  29.4 us
    pallas_call x2, Pallas kernels, feed_back(): pl.pallas_call(functools.partial(feed_back_kernel, layer, steps), grid_sp...  28.5 us
    pallas_call x2, Pallas kernels, attention_backward(): pl.pallas_call(attention_backward_kernel, grid_spec=pltpu.PrefetchScalarG...  27.8 us
    ppermute x17, starting transfers between devices, transfer(): return lax.ppermute(message, AXES, self.exchange.pairs(self.phase - 1))  21.1 us
    pallas_call x2, Pallas kernels, attention_forward(): pl.pallas_call(attention_forward_kernel, grid_spec=pltpu.PrefetchScalarGr...  19.6 us
    pallas_call x2, Pallas kernels, down_gradients(): gradient_call(grad_down_kernel, 'gradient_down', chips, hidden // (2 * wi...  16 us
  transfers between devices with their start and end apart: 44, of which 18 were waited for; matrix products, arithmetic and copies ran while one was open for 3% of the time, Pallas kernels for 56%

profile of v1, /device:TPU:0, one launch (start us, length us, event | category | flops | bytes accessed | tf_op | source)
XLA Modules:
  0.0 312.3 jit_solution(8156829844888500131)
XLA Ops:
  1.9 2.5 collective-permute-start
  4.6 1.5 collective-permute-start.1
  8.2 1.6 collective-permute-start.2
  9.8 2.0 collective-permute-done.2
  11.7 2.6 collective-permute-start.3
  14.3 1.9 collective-permute-done.3
  17.4 5.9 %project.2 = (bf16[512,768]{1,0:T(8,128)(2,1)}, bf16[512,768]{1,0:T(8,128)(2,1)}, bf16[512,1536]{1,0:T(8,128)(2,1)}) custom-call(bf16[512,768]{1,0:T(8,128)(2,1)} %maximum_select_fusion.stream, f32[2,768]{1,0:T(2,128)S(1)} %copy-done.7, f32[2,768]{1,0:T(2,128)S(1)} %copy-done.8, bf16[2,768,2304]{2,1,0:T(8,128)(2,1)} %matrix.7), custom_call_target="tpu_custom_call" | custom-call | flops 1000 | bytes 1000 | tf_op jit(solution)/shard_map/project/pallas_call | solution.py:305
  23.3 3.6 %collective-permute-done.4.kx_ref.vx_ref = bf16[512,1536]{1,0:T(8,128)(2,1)S(1)} collective-permute-done((bf16[512,1536]{1,0:T(8,128)(2,1)}, bf16[512,1536]{1,0:T(8,128)(2,1)S(1)}, u32[]{:S(2)}, u32[]{:S(2)}) %collective-permute-start.4) | collective-permute-done | bytes 1572896 | tf_op jit(solution)/shard_map/ppermute | solution.py:733
  28.0 10.1 %attention_forward.2 = (bf16[512,768]{1,0:T(8,128)(2,1)}, f32[6,8,512]{2,1,0:T(8,128)}) custom-call(s32[1]{0:T(128)} %bitcast.meta, bf16[512,768]{1,0:T(8,128)(2,1)} %get-tuple-element.271.q_ref, bf16[512,1536]{1,0:T(8,128)(2,1)} %get-tuple-element.272.ko_ref.vo_ref, bf16[512,1536]{1,0:T(8,128)(2,1)} %get-tuple-element.272.ko_ref.vo_ref, ...), custom_call_target="tpu_custom_call" | custom-call | flops 1000 | bytes 1000 | tf_op jit(solution)/shard_map/attention_forward/pallas_call | solution.py:140
  38.5 15.5 %feed_forward.2 = (bf16[512,768]{1,0:T(8,128)(2,1)}, bf16[512,768]{1,0:T(8,128)(2,1)}, bf16[512,3072]{1,0:T(8,128)(2,1)}, bf16[512,3072]{1,0:T(8,128)(2,1)}, bf16[512,768]{1,0:T(8,128)(2,1)}) custom-call(bf16[512,768]{1,0:T(8,128)(2,1)} %get-tuple-element.286.attended.co.o_ref, bf16[512,768]{1,0:T(8,128)(2,1)} %maximum_select_fusion.stream, ...), custom_call_target="tpu_custom_call" | custom-call | flops 1000 | bytes 1000 | tf_op jit(solution)/shard_map/feed_forward/pallas_call | solution.py:370
  55.5 5.9 %project.3 = (bf16[512,768]{1,0:T(8,128)(2,1)}, bf16[512,768]{1,0:T(8,128)(2,1)}, bf16[512,1536]{1,0:T(8,128)(2,1)}) custom-call(bf16[512,768]{1,0:T(8,128)(2,1)} %get-tuple-element.313.stream, f32[2,768]{1,0:T(2,128)S(1)} %copy-done.7, f32[2,768]{1,0:T(2,128)S(1)} %copy-done.8, bf16[2,768,2304]{2,1,0:T(8,128)(2,1)} %matrix.7), custom_call_target="tpu_custom_call" | custom-call | flops 1000 | bytes 1000 | tf_op jit(solution)/shard_map/project/pallas_call | solution.py:305
  62.0 1.8 copy-done.20
  66.7 1.8 weigh.1
  69.6 9.5 %attention_forward.3 = (bf16[512,768]{1,0:T(8,128)(2,1)}, f32[6,8,512]{2,1,0:T(8,128)}) custom-call(s32[1]{0:T(128)} %bitcast.meta, bf16[512,768]{1,0:T(8,128)(2,1)} %get-tuple-element.304.q_ref, bf16[512,1536]{1,0:T(8,128)(2,1)} %get-tuple-element.305.ko_ref.vo_ref, bf16[512,1536]{1,0:T(8,128)(2,1)} %get-tuple-element.305.ko_ref.vo_ref, ...), custom_call_target="tpu_custom_call" | custom-call | flops 1000 | bytes 1000 | tf_op jit(solution)/shard_map/attention_forward/pallas_call | solution.py:140
  79.3 15.7 %feed_forward.3 = (bf16[512,768]{1,0:T(8,128)(2,1)}, bf16[512,768]{1,0:T(8,128)(2,1)}, bf16[512,3072]{1,0:T(8,128)(2,1)}, bf16[512,3072]{1,0:T(8,128)(2,1)}, bf1...) custom-call(bf16[512,768]{1,0:T(8,128)(2,1)} %get-tuple-element.320.attended.o_ref.co, ...), custom_call_target="tpu_custom_call" | custom-call | flops 1000 | bytes 1000 | tf_op jit(solution)/shard_map/feed_forward/pallas_call | solution.py:370
  96.5 14.2 %feed_back.2 = (bf16[512,1536]{1,0:T(8,128)(2,1)S(1)}, bf16[512,1536]{1,0:T(8,128)(2,1)S(1)}, bf16[512,768]{1,0:T(8,128)(2,1)S(1)}, bf16[512,384]{1,0:T(8,128)(2...) custom-call(s32[34]{0:T(128)S(1)} %pad_add_fusion.meta, ...), custom_call_target="tpu_custom_call" | custom-call | flops 1000 | bytes 1000 | tf_op jit(solution)/shard_map/feed_back/pallas_call | solution.py:440
  112.1 8.0 %gradient_down.2 = (bf16[8,192,384]{2,1,0:T(8,128)(2,1)}, bf16[8,192,384]{2,1,0:T(8,128)(2,1)}) custom-call(s32[34]{0:T(128)S(1)} %pad_add_fusion.meta, bf16[512,3072]{1,0:T(8,128)(2,1)} %get-tuple-element.334.ao, bf16[512,3072]{1,0:T(8,128)(2,1)} %collective-permute-done.15.ax, bf16[512,768]{1,0:T(8,128)(2,1)S(1)} %get-tuple-element.341.back_out.bo, ...), custom_call_target="tpu_custom_call" | custom-call | flops 1000 | bytes 1000 | tf_op jit(solution)/shard_map/gradient_down/pallas_call | solution.py:696
  120.1 1.5 collective-permute-start.19
  121.7 14.0 %attention_backward.2 = (bf16[512,768]{1,0:T(8,128)(2,1)S(1)}, bf16[2,512,768]{2,1,0:T(8,128)(2,1)}, bf16[2,512,768]{2,1,0:T(8,128)(2,1)S(1)}) custom-call(s32[1]{0:T(128)} %bitcast.meta, bf16[512,768]{1,0:T(8,128)(2,1)} %get-tuple-element.304.q_ref, bf16[512,1536]{1,0:T(8,128)(2,1)} %get-tuple-element.305.ko_ref.vo_ref, ...), custom_call_target="tpu_custom_call" | custom-call | flops 1000 | bytes 1000 | tf_op jit(solution)/shard_map/attention_backward/pallas_call | solution.py:247
  136.8 1.4 collective-permute-start.20
  138.3 7.7 %gradient_up.2 = (bf16[8,240,384]{2,1,0:T(8,128)(2,1)}, bf16[8,240,384]{2,1,0:T(8,128)(2,1)}) custom-call(s32[34]{0:T(128)S(1)} %pad_add_fusion.meta, bf16[512,768]{1,0:T(8,128)(2,1)} %get-tuple-element.333.ao, bf16[512,768]{1,0:T(8,128)(2,1)} %collective-permute-done.14.ax, bf16[512,1536]{1,0:T(8,128)(2,1)S(1)} %get-tuple-element.362.bo, ...), custom_call_target="tpu_custom_call" | custom-call | flops 1000 | bytes 1000 | tf_op jit(solution)/shard_map/gradient_up/pallas_call | solution.py:676
  146.9 1.5 collective-permute-start.22
  148.5 1.6 collective-permute-start.23
  150.1 7.1 %project_back.2 = (bf16[512,1152]{1,0:T(8,128)(2,1)S(1)}, bf16[512,1152]{1,0:T(8,128)(2,1)S(1)}, bf16[512,768]{1,0:T(8,128)(2,1)S(1)}, bf16[512,384]{1,0:T(8,128)(2,1)S(1)}, f32[8,768]{1,0:T(8,128)S(1)}) custom-call(s32[34]{0:T(128)S(1)} %pad_add_fusion.meta, bf16[512,768]{1,0:T(8,128)(2,1)} %copy-done.3, bf16[2,512,768]{2,1,0:T(8,128)(2,1)} %get-tuple-element.375.own, ...), custom_call_target="tpu_custom_call" | custom-call | flops 1000 | bytes 1000 | tf_op jit(solution)/shard_map/project_back/pallas_call | solution.py:523
  157.2 9.4 %collective-permute-done.22.refs_6_ = bf16[8,240,384]{2,1,0:T(8,128)(2,1)S(1)} collective-permute-done((bf16[8,240,384]{2,1,0:T(8,128)(2,1)}, bf16[8,240,384]{2,1,0:T(8,128)(2,1)S(1)}, u32[]{:S(2)}, u32[]{:S(2)}) %collective-permute-start.22) | collective-permute-done | bytes 1474592 | tf_op jit(solution)/shard_map/ppermute | solution.py:793
  166.9 1.4 collective-permute-done.24.bx
  168.4 1.3 collective-permute-start.26
  169.8 2.6 collective-permute-start.27
  172.4 8.0 %gradient_down.3 = (bf16[8,192,384]{2,1,0:T(8,128)(2,1)}, bf16[8,192,384]{2,1,0:T(8,128)(2,1)}) custom-call(s32[34]{0:T(128)S(1)} %pad_add_fusion.meta, bf16[512,3072]{1,0:T(8,128)(2,1)} %get-tuple-element.295.ao, bf16[512,3072]{1,0:T(8,128)(2,1)} %copy-done.20, bf16[512,768]{1,0:T(8,128)(2,1)S(1)} %get-tuple-element.401.bo.back_out, ...), custom_call_target="tpu_custom_call" | custom-call | flops 1000 | bytes 1000 | tf_op jit(solution)/shard_map/gradient_down/pallas_call | solution.py:696
  181.9 1.5 collective-permute-start.28
  183.4 1.6 collective-permute-start.29
  185.0 14.3 %feed_back.3 = (bf16[512,1536]{1,0:T(8,128)(2,1)S(1)}, bf16[512,1536]{1,0:T(8,128)(2,1)S(1)}, bf16[512,768]{1,0:T(8,128)(2,1)S(1)}, bf16[512,384]{1,0:T(8,128)(2...) custom-call(s32[34]{0:T(128)S(1)} %pad_add_fusion.meta, ...), custom_call_target="tpu_custom_call" | custom-call | flops 1000 | bytes 1000 | tf_op jit(solution)/shard_map/feed_back/pallas_call | solution.py:440
  200.5 1.4 collective-permute-start.33
  201.9 5.5 %gradient_qkv.2 = (bf16[8,48,1280]{2,1,0:T(8,128)(2,1)}, bf16[8,48,1280]{2,1,0:T(8,128)(2,1)}) custom-call(s32[34]{0:T(128)S(1)} %pad_add_fusion.meta, bf16[512,768]{1,0:T(8,128)(2,1)} %get-tuple-element.309.ao, bf16[512,768]{1,0:T(8,128)(2,1)} %copy-done.28, bf16[512,1152]{1,0:T(8,128)(2,1)S(1)} %get-tuple-element.424.bo, ...), custom_call_target="tpu_custom_call" | custom-call | flops 1000 | bytes 1000 | tf_op jit(solution)/shard_map/gradient_qkv/pallas_call | solution.py:714
  207.4 1.5 collective-permute-done.33.refs_9_
  210.4 7.7 %gradient_up.3 = (bf16[8,240,384]{2,1,0:T(8,128)(2,1)}, bf16[8,240,384]{2,1,0:T(8,128)(2,1)}) custom-call(s32[34]{0:T(128)S(1)} %pad_add_fusion.meta, bf16[512,768]{1,0:T(8,128)(2,1)} %get-tuple-element.294.ao, bf16[512,768]{1,0:T(8,128)(2,1)} %copy-done.30, bf16[512,1536]{1,0:T(8,128)(2,1)S(1)} %get-tuple-element.434.bo, ...), custom_call_target="tpu_custom_call" | custom-call | flops 1000 | bytes 1000 | tf_op jit(solution)/shard_map/gradient_up/pallas_call | solution.py:676
  218.3 5.7 %collective-permute-done.34.refs_2_ = bf16[8,48,1280]{2,1,0:T(8,128)(2,1)S(1)} collective-permute-done((bf16[8,48,1280]{2,1,0:T(8,128)(2,1)}, bf16[8,48,1280]{2,1,0:T(8,128)(2,1)S(1)}, u32[]{:S(2)}, u32[]{:S(2)}) %collective-permute-start.34) | collective-permute-done | bytes 983072 | tf_op jit(solution)/shard_map/ppermute | solution.py:793
  225.8 13.8 %attention_backward.3 = (bf16[512,768]{1,0:T(8,128)(2,1)S(1)}, bf16[2,512,768]{2,1,0:T(8,128)(2,1)}, bf16[2,512,768]{2,1,0:T(8,128)(2,1)S(1)}) custom-call(s32[1]{0:T(128)} %bitcast.meta, bf16[512,768]{1,0:T(8,128)(2,1)} %get-tuple-element.271.q_ref, bf16[512,1536]{1,0:T(8,128)(2,1)} %get-tuple-element.272.ko_ref.vo_ref, ...), custom_call_target="tpu_custom_call" | custom-call | flops 1000 | bytes 1000 | tf_op jit(solution)/shard_map/attention_backward/pallas_call | solution.py:247
  239.7 3.9 %collective-permute-done.35.refs_5_ = bf16[8,240,384]{2,1,0:T(8,128)(2,1)S(1)} collective-permute-done((bf16[8,240,384]{2,1,0:T(8,128)(2,1)}, bf16[8,240,384]{2,1,0:T(8,128)(2,1)S(1)}, u32[]{:S(2)}, u32[]{:S(2)}) %collective-permute-start.35) | collective-permute-done | bytes 1474592 | tf_op jit(solution)/shard_map/ppermute | solution.py:793
  247.7 1.3 collective-permute-start.39
  251.0 7.9 %project_back.3 = (bf16[512,1152]{1,0:T(8,128)(2,1)S(1)}, bf16[512,1152]{1,0:T(8,128)(2,1)S(1)}, bf16[512,768]{1,0:T(8,128)(2,1)S(1)}, bf16[512,384]{1,0:T(8,128...) custom-call(s32[34]{0:T(128)S(1)} %pad_add_fusion.meta, bf16[512,768]{1,0:T(8,128)(2,1)} %copy-done.4, ...), custom_call_target="tpu_custom_call" | custom-call | flops 1000 | bytes 1000 | tf_op jit(solution)/shard_map/project_back/pallas_call | solution.py:523
  258.9 1.9 collect.1
  261.8 2.2 collective-permute-done.39.refs_3_
  265.3 1.6 collective-permute-done.41.bx
  267.8 5.5 %gradient_qkv.3 = (bf16[8,48,1280]{2,1,0:T(8,128)(2,1)}, bf16[8,48,1280]{2,1,0:T(8,128)(2,1)}) custom-call(s32[34]{0:T(128)S(1)} %pad_add_fusion.meta, bf16[512,768]{1,0:T(8,128)(2,1)} %get-tuple-element.276.ao, bf16[512,768]{1,0:T(8,128)(2,1)} %collective-permute-done.5.ax, bf16[512,1152]{1,0:T(8,128)(2,1)S(1)} %get-tuple-element.495.bo, ...), custom_call_target="tpu_custom_call" | custom-call | flops 1000 | bytes 1000 | tf_op jit(solution)/shard_map/gradient_qkv/pallas_call | solution.py:714
  273.3 4.6 %collective-permute-done.42.refs_7_ = bf16[2,240,384]{2,1,0:T(8,128)(2,1)S(1)} collective-permute-done((bf16[2,240,384]{2,1,0:T(8,128)(2,1)S(1)}, bf16[2,240,384]{2,1,0:T(8,128)(2,1)S(1)}, u32[]{:S(2)}, u32[]{:S(2)}) %collective-permute-start.42) | collective-permute-done | bytes 368672 | tf_op jit(solution)/shard_map/ppermute | solution.py:793
  278.7 29.4 %last_exchanges.1 = (f32[216,384]{1,0:T(8,128)S(1)}, f32[216,384]{1,0:T(8,128)S(1)}, f32[216,384]{1,0:T(8,128)S(1)}, f32[24,1280]{1,0:T(8,128)S(1)}, f32[24,1280...) custom-call(bf16[8,48,1280]{2,1,0:T(8,128)(2,1)} %get-tuple-element.503.refs_0_, ...), custom_call_target="tpu_custom_call" | custom-call | flops 1000 | bytes 1000 | tf_op jit(solution)/shard_map/last_exchanges/pallas_call | solution.py:1053
  309.5 1.3 fusion
  (188 shorter events, 35.9 us)
Async XLA Ops:
  1.9 14.2 %collective-permute-start = (bf16[256,768]{1,0:T(8,128)(2,1)S(1)}, bf16[256,768]{1,0:T(8,128)(2,1)S(1)}, u32[]{:S(2)}, u32[]{:S(2)}) collective-permute-start(bf16[256,768]{1,0:T(8,128)(2,1)S(1)} %get-tuple-element.523), channel_id=1, source_target_pairs={{0,3},{1,2},{2,1},{3,0},{4,7},{5,6},{6,5},{7,4},{8,11},{9,10},{10,... | collective-permute-start | bytes 1179656 | tf_op jit(solution)/shard_map/ppermute | solution.py:736
  4.6 3.6 %collective-permute-start.1 = (f32[3]{0:T(128)S(1)}, f32[3]{0:T(128)S(1)}, u32[]{:S(2)}, u32[]{:S(2)}) collective-permute-start(f32[3]{0:T(128)S(1)} %select_reduce_fusion.1), channel_id=1, source_target_pairs={{0,4},{4,0},{8,12},{12,8},{16,20},{20,16},{24,28},{28,24},{1,5},{5... | collective-permute-start | bytes 44 | tf_op jit(solution)/shard_map/ppermute | solution.py:1138
  8.2 3.5 %collective-permute-start.2 = (f32[3]{0:T(128)S(1)}, f32[3]{0:T(128)S(1)}, u32[]{:S(2)}, u32[]{:S(2)}) collective-permute-start(f32[3]{0:T(128)S(1)} %add.101), channel_id=1, source_target_pairs={{0,8},{4,12},{8,0},{12,4},{16,24},{20,28},{24,16},{28,20},{1,9},{5... | collective-permute-start | bytes 44 | tf_op jit(solution)/shard_map/ppermute | solution.py:1138
  11.7 4.4 %collective-permute-start.3 = (f32[3]{0:T(128)S(1)}, f32[3]{0:T(128)S(1)}, u32[]{:S(2)}, u32[]{:S(2)}) collective-permute-start(f32[3]{0:T(128)S(1)} %add.102), channel_id=1, source_target_pairs={{0,16},{4,20},{8,24},{12,28},{16,0},{20,4},{24,8},{28,12},{1,17},{... | collective-permute-start | bytes 44 | tf_op jit(solution)/shard_map/ppermute | solution.py:1138
  23.3 3.6 %collective-permute-start.4 = (bf16[512,1536]{1,0:T(8,128)(2,1)}, bf16[512,1536]{1,0:T(8,128)(2,1)S(1)}, u32[]{:S(2)}, u32[]{:S(2)}) collective-permute-start(bf16[512,1536]{1,0:T(8,128)(2,1)} %get-tuple-element.272.ko_ref.vo_ref), channel_id=1, source_target_pairs={{0,1},{1,0},{2,3},{3,2},{4,5},{5,4},{6,7},{7,6},{8,9},{9,8},{10,11... | collective-permute-start | bytes 4718600 | tf_op jit(solution)/shard_map/ppermute | solution.py:733
  26.9 11.3 %collective-permute-start.5 = (bf16[512,768]{1,0:T(8,128)(2,1)}, bf16[512,768]{1,0:T(8,128)(2,1)}, u32[]{:S(2)}, u32[]{:S(2)}) collective-permute-start(bf16[512,768]{1,0:T(8,128)(2,1)} %get-tuple-element.276.ao), channel_id=1, source_target_pairs={{0,1},{1,0},{2,3},{3,2},{4,5},{5,4},{6,7},{7,6},{8,9},{9,8},{10,11... | collective-permute-start | bytes 2359304 | tf_op jit(solution)/shard_map/ppermute | solution.py:733
  27.0 11.2 %collective-permute-start.6 = (bf16[256,768]{1,0:T(8,128)(2,1)}, bf16[256,768]{1,0:T(8,128)(2,1)S(1)}, u32[]{:S(2)}, u32[]{:S(2)}) collective-permute-start(bf16[256,768]{1,0:T(8,128)(2,1)} %get-tuple-element.277), channel_id=1, source_target_pairs={{0,3},{1,2},{2,1},{3,0},{4,7},{5,6},{6,5},{7,4},{8,11},{9,10},{10,... | collective-permute-start | bytes 1179656 | tf_op jit(solution)/shard_map/ppermute | solution.py:736
  38.2 15.9 %collective-permute-start.7 = (bf16[512,768]{1,0:T(8,128)(2,1)}, bf16[512,768]{1,0:T(8,128)(2,1)S(1)}, u32[]{:S(2)}, u32[]{:S(2)}) collective-permute-start(bf16[512,768]{1,0:T(8,128)(2,1)} %get-tuple-element.286.attended.co.o_ref), channel_id=1, source_target_pairs={{0,1},{1,0},{2,3},{3,2},{4,5},{5,4},{6,7},{7,6},{8,9},{9,8},{10,11... | collective-permute-start | bytes 2359304 | tf_op jit(solution)/shard_map/ppermute | solution.py:733
  55.0 7.0 %collective-permute-start.9 = (bf16[512,3072]{1,0:T(8,128)(2,1)}, bf16[512,3072]{1,0:T(8,128)(2,1)S(1)}, u32[]{:S(2)}, u32[]{:S(2)}) collective-permute-start(bf16[512,3072]{1,0:T(8,128)(2,1)} %get-tuple-element.295.ao), channel_id=1, source_target_pairs={{0,1},{1,0},{2,3},{3,2},{4,5},{5,4},{6,7},{7,6},{8,9},{9,8},{10,11... | collective-permute-start | bytes 9437192 | tf_op jit(solution)/shard_map/ppermute | solution.py:733
  55.2 6.8 %collective-permute-start.8 = (bf16[512,768]{1,0:T(8,128)(2,1)}, bf16[512,768]{1,0:T(8,128)(2,1)S(1)}, u32[]{:S(2)}, u32[]{:S(2)}) collective-permute-start(bf16[512,768]{1,0:T(8,128)(2,1)} %get-tuple-element.294.ao), channel_id=1, source_target_pairs={{0,1},{1,0},{2,3},{3,2},{4,5},{5,4},{6,7},{7,6},{8,9},{9,8},{10,11... | collective-permute-start | bytes 2359304 | tf_op jit(solution)/shard_map/ppermute | solution.py:733
  63.9 4.5 %collective-permute-start.10 = (bf16[512,1536]{1,0:T(8,128)(2,1)}, bf16[512,1536]{1,0:T(8,128)(2,1)S(1)}, u32[]{:S(2)}, u32[]{:S(2)}) collective-permute-start(bf16[512,1536]{1,0:T(8,128)(2,1)} %get-tuple-element.305.ko_ref.vo_ref), channel_id=1, source_target_pairs={{0,1},{1,0},{2,3},{3,2},{4,5},{5,4},{6,7},{7,6},{8,9},{9,8},{10,11... | collective-permute-start | bytes 4718600 | tf_op jit(solution)/shard_map/ppermute | solution.py:733
  68.5 10.7 %collective-permute-start.11 = (bf16[512,768]{1,0:T(8,128)(2,1)}, bf16[512,768]{1,0:T(8,128)(2,1)S(1)}, u32[]{:S(2)}, u32[]{:S(2)}) collective-permute-start(bf16[512,768]{1,0:T(8,128)(2,1)} %get-tuple-element.309.ao), channel_id=1, source_target_pairs={{0,1},{1,0},{2,3},{3,2},{4,5},{5,4},{6,7},{7,6},{8,9},{9,8},{10,11... | collective-permute-start | bytes 2359304 | tf_op jit(solution)/shard_map/ppermute | solution.py:733
  68.8 10.3 %collective-permute-start.12 = (bf16[512,384]{1,0:T(8,128)(2,1)S(1)}, bf16[512,384]{1,0:T(8,128)(2,1)S(1)}, u32[]{:S(2)}, u32[]{:S(2)}) collective-permute-start(bf16[512,384]{1,0:T(8,128)(2,1)S(1)} %get-tuple-element.310), channel_id=1, source_target_pairs={{0,1},{1,0},{2,3},{3,2},{4,5},{5,4},{6,7},{7,6},{8,9},{9,8},{10,11... | collective-permute-start | bytes 1179656 | tf_op jit(solution)/shard_map/ppermute | solution.py:733
  79.2 15.8 %collective-permute-start.13 = (bf16[512,768]{1,0:T(8,128)(2,1)}, bf16[512,768]{1,0:T(8,128)(2,1)S(1)}, u32[]{:S(2)}, u32[]{:S(2)}) collective-permute-start(bf16[512,768]{1,0:T(8,128)(2,1)} %get-tuple-element.320.attended.o_ref.co), channel_id=1, source_target_pairs={{0,1},{1,0},{2,3},{3,2},{4,5},{5,4},{6,7},{7,6},{8,9},{9,8},{10,11... | collective-permute-start | bytes 2359304 | tf_op jit(solution)/shard_map/ppermute | solution.py:733
  95.0 16.5 %collective-permute-start.15 = (bf16[512,3072]{1,0:T(8,128)(2,1)}, bf16[512,3072]{1,0:T(8,128)(2,1)}, u32[]{:S(2)}, u32[]{:S(2)}) collective-permute-start(bf16[512,3072]{1,0:T(8,128)(2,1)} %get-tuple-element.334.ao), channel_id=1, source_target_pairs={{0,1},{1,0},{2,3},{3,2},{4,5},{5,4},{6,7},{7,6},{8,9},{9,8},{10,11... | collective-permute-start | bytes 9437192 | tf_op jit(solution)/shard_map/ppermute | solution.py:733
  95.6 16.0 %collective-permute-start.14 = (bf16[512,768]{1,0:T(8,128)(2,1)}, bf16[512,768]{1,0:T(8,128)(2,1)}, u32[]{:S(2)}, u32[]{:S(2)}) collective-permute-start(bf16[512,768]{1,0:T(8,128)(2,1)} %get-tuple-element.333.ao), channel_id=1, source_target_pairs={{0,1},{1,0},{2,3},{3,2},{4,5},{5,4},{6,7},{7,6},{8,9},{9,8},{10,11... | collective-permute-start | bytes 2359304 | tf_op jit(solution)/shard_map/ppermute | solution.py:733
  95.6 15.9 %collective-permute-start.16 = (bf16[256,768]{1,0:T(8,128)(2,1)S(1)}, bf16[256,768]{1,0:T(8,128)(2,1)S(1)}, u32[]{:S(2)}, u32[]{:S(2)}) collective-permute-start(bf16[256,768]{1,0:T(8,128)(2,1)S(1)} %get-tuple-element.335), channel_id=1, source_target_pairs={{0,3},{1,2},{2,1},{3,0},{4,7},{5,6},{6,5},{7,4},{8,11},{9,10},{10,... | collective-permute-start | bytes 1179656 | tf_op jit(solution)/shard_map/ppermute | solution.py:736
  111.6 8.6 %collective-permute-start.17 = (bf16[512,1536]{1,0:T(8,128)(2,1)S(1)}, bf16[512,1536]{1,0:T(8,128)(2,1)S(1)}, u32[]{:S(2)}, u32[]{:S(2)}) collective-permute-start(bf16[512,1536]{1,0:T(8,128)(2,1)S(1)} %get-tuple-element.345), channel_id=1, source_target_pairs={{0,1},{1,0},{2,3},{3,2},{4,5},{5,4},{6,7},{7,6},{8,9},{9,8},{10,11... | collective-permute-start | bytes 4718600 | tf_op jit(solution)/shard_map/ppermute | solution.py:733
  112.0 8.1 %collective-permute-start.18 = (bf16[512,384]{1,0:T(8,128)(2,1)S(1)}, bf16[512,384]{1,0:T(8,128)(2,1)S(1)}, u32[]{:S(2)}, u32[]{:S(2)}) collective-permute-start(bf16[512,384]{1,0:T(8,128)(2,1)S(1)} %get-tuple-element.346), channel_id=1, source_target_pairs={{0,1},{1,0},{2,3},{3,2},{4,5},{5,4},{6,7},{7,6},{8,9},{9,8},{10,11... | collective-permute-start | bytes 1179656 | tf_op jit(solution)/shard_map/ppermute | solution.py:733
  120.1 16.5 %collective-permute-start.19 = (bf16[8,192,384]{2,1,0:T(8,128)(2,1)}, bf16[8,192,384]{2,1,0:T(8,128)(2,1)S(1)}, u32[]{:S(2)}, u32[]{:S(2)}) collective-permute-start(bf16[8,192,384]{2,1,0:T(8,128)(2,1)} %get-tuple-element.353), channel_id=1, source_target_pairs={{0,4},{1,3},{2,6},{3,1},{4,0},{5,7},{6,2},{7,5},{8,12},{9,11},{10,... | collective-permute-start | bytes 3538952 | tf_op jit(solution)/shard_map/ppermute | solution.py:793
  136.6 30.0 %copy-start.19 = (bf16[8,192,384]{2,1,0:T(8,128)(2,1)}, bf16[8,192,384]{2,1,0:T(8,128)(2,1)S(1)}, u32[]{:S(2)}) copy-start(bf16[8,192,384]{2,1,0:T(8,128)(2,1)S(1)} %collective-permute-done.19.refs_1_) | copy-start | bytes 3538948
  136.8 10.0 %collective-permute-start.21 = (bf16[2,512,768]{2,1,0:T(8,128)(2,1)S(1)}, bf16[2,512,768]{2,1,0:T(8,128)(2,1)S(1)}, u32[]{:S(2)}, u32[]{:S(2)}) collective-permute-start(bf16[2,512,768]{2,1,0:T(8,128)(2,1)S(1)} %get-tuple-element.370), channel_id=1, source_target_pairs={{0,1},{1,0},{2,3},{3,2},{4,5},{5,4},{6,7},{7,6},{8,9},{9,8},{10,11... | collective-permute-start | bytes 4718600 | tf_op jit(solution)/shard_map/ppermute | solution.py:733
  136.8 9.9 %collective-permute-start.20 = (bf16[4,192,384]{2,1,0:T(8,128)(2,1)S(1)}, bf16[4,192,384]{2,1,0:T(8,128)(2,1)S(1)}, u32[]{:S(2)}, u32[]{:S(2)}) collective-permute-start(bf16[4,192,384]{2,1,0:T(8,128)(2,1)S(1)} %add_convert_fusion.3), channel_id=1, source_target_pairs={{0,2},{1,5},{2,0},{3,7},{4,6},{5,1},{6,4},{7,3},{8,10},{9,13},{10,... | collective-permute-start | bytes 1769480 | tf_op jit(solution)/shard_map/ppermute | solution.py:793
  146.9 19.6 %collective-permute-start.22 = (bf16[8,240,384]{2,1,0:T(8,128)(2,1)}, bf16[8,240,384]{2,1,0:T(8,128)(2,1)S(1)}, u32[]{:S(2)}, u32[]{:S(2)}) collective-permute-start(bf16[8,240,384]{2,1,0:T(8,128)(2,1)} %get-tuple-element.383), channel_id=1, source_target_pairs={{0,4},{1,3},{2,6},{3,1},{4,0},{5,7},{6,2},{7,5},{8,12},{9,11},{10,... | collective-permute-start | bytes 4423688 | tf_op jit(solution)/shard_map/ppermute | solution.py:793
  148.5 8.7 %collective-permute-start.23 = (bf16[2,192,384]{2,1,0:T(8,128)(2,1)S(1)}, bf16[2,192,384]{2,1,0:T(8,128)(2,1)S(1)}, u32[]{:S(2)}, u32[]{:S(2)}) collective-permute-start(bf16[2,192,384]{2,1,0:T(8,128)(2,1)S(1)} %add_convert_fusion.8), channel_id=1, source_target_pairs={{0,8},{1,17},{2,10},{3,19},{4,12},{5,21},{6,14},{7,23},{8,0},{9,25... | collective-permute-start | bytes 884744 | tf_op jit(solution)/shard_map/ppermute | solution.py:793
  166.6 32.8 %copy-start.13 = (bf16[8,240,384]{2,1,0:T(8,128)(2,1)}, bf16[8,240,384]{2,1,0:T(8,128)(2,1)S(1)}, u32[]{:S(2)}) copy-start(bf16[8,240,384]{2,1,0:T(8,128)(2,1)S(1)} %collective-permute-done.22.refs_6_) | copy-start | bytes 4423684
  166.6 1.7 collective-permute-start.24
  168.3 12.1 %collective-permute-start.25 = (bf16[512,1152]{1,0:T(8,128)(2,1)S(1)}, bf16[512,1152]{1,0:T(8,128)(2,1)S(1)}, u32[]{:S(2)}, u32[]{:S(2)}) collective-permute-start(bf16[512,1152]{1,0:T(8,128)(2,1)S(1)} %get-tuple-element.396), channel_id=1, source_target_pairs={{0,1},{1,0},{2,3},{3,2},{4,5},{5,4},{6,7},{7,6},{8,9},{9,8},{10,11... | collective-permute-start | bytes 3538952 | tf_op jit(solution)/shard_map/ppermute | solution.py:733
  168.4 11.9 %collective-permute-start.26 = (bf16[4,240,384]{2,1,0:T(8,128)(2,1)S(1)}, bf16[4,240,384]{2,1,0:T(8,128)(2,1)S(1)}, u32[]{:S(2)}, u32[]{:S(2)}) collective-permute-start(bf16[4,240,384]{2,1,0:T(8,128)(2,1)S(1)} %add_convert_fusion.1), channel_id=1, source_target_pairs={{0,2},{1,5},{2,0},{3,7},{4,6},{5,1},{6,4},{7,3},{8,10},{9,13},{10,... | collective-permute-start | bytes 2211848 | tf_op jit(solution)/shard_map/ppermute | solution.py:793
  169.8 10.6 %collective-permute-start.27 = (bf16[1,192,384]{2,1,0:T(8,128)(2,1)S(1)}, bf16[1,192,384]{2,1,0:T(8,128)(2,1)S(1)}, u32[]{:S(2)}, u32[]{:S(2)}) collective-permute-start(bf16[1,192,384]{2,1,0:T(8,128)(2,1)S(1)} %add_convert_fusion.11), channel_id=1, source_target_pairs={{0,16},{1,9},{2,18},{3,11},{4,20},{5,13},{6,22},{7,15},{8,24},{9,1... | collective-permute-start | bytes 442376 | tf_op jit(solution)/shard_map/ppermute | solution.py:793
  181.9 17.4 %collective-permute-start.28 = (bf16[8,192,384]{2,1,0:T(8,128)(2,1)S(1)}, bf16[8,192,384]{2,1,0:T(8,128)(2,1)S(1)}, u32[]{:S(2)}, u32[]{:S(2)}) collective-permute-start(bf16[8,192,384]{2,1,0:T(8,128)(2,1)S(1)} %copy-done.42), channel_id=1, source_target_pairs={{0,4},{1,3},{2,6},{3,1},{4,0},{5,7},{6,2},{7,5},{8,12},{9,11},{10,... | collective-permute-start | bytes 3538952 | tf_op jit(solution)/shard_map/ppermute | solution.py:793
  183.4 15.9 %collective-permute-start.29 = (bf16[2,240,384]{2,1,0:T(8,128)(2,1)S(1)}, bf16[2,240,384]{2,1,0:T(8,128)(2,1)S(1)}, u32[]{:S(2)}, u32[]{:S(2)}) collective-permute-start(bf16[2,240,384]{2,1,0:T(8,128)(2,1)S(1)} %add_convert_fusion.6), channel_id=1, source_target_pairs={{0,8},{1,17},{2,10},{3,19},{4,12},{5,21},{6,14},{7,23},{8,0},{9,25... | collective-permute-start | bytes 1105928 | tf_op jit(solution)/shard_map/ppermute | solution.py:793
  199.3 45.3 %copy-start.17 = (bf16[8,192,384]{2,1,0:T(8,128)(2,1)}, bf16[8,192,384]{2,1,0:T(8,128)(2,1)S(1)}, u32[]{:S(2)}) copy-start(bf16[8,192,384]{2,1,0:T(8,128)(2,1)S(1)} %collective-permute-done.28.refs_9_) | copy-start | bytes 3538948
  199.6 10.0 %collective-permute-start.30 = (bf16[512,1536]{1,0:T(8,128)(2,1)S(1)}, bf16[512,1536]{1,0:T(8,128)(2,1)S(1)}, u32[]{:S(2)}, u32[]{:S(2)}) collective-permute-start(bf16[512,1536]{1,0:T(8,128)(2,1)S(1)} %get-tuple-element.428), channel_id=1, source_target_pairs={{0,1},{1,0},{2,3},{3,2},{4,5},{5,4},{6,7},{7,6},{8,9},{9,8},{10,11... | collective-permute-start | bytes 4718600 | tf_op jit(solution)/shard_map/ppermute | solution.py:733
  199.7 9.9 %collective-permute-start.32 = (bf16[4,192,384]{2,1,0:T(8,128)(2,1)S(1)}, bf16[4,192,384]{2,1,0:T(8,128)(2,1)S(1)}, u32[]{:S(2)}, u32[]{:S(2)}) collective-permute-start(bf16[4,192,384]{2,1,0:T(8,128)(2,1)S(1)} %add_convert_fusion.2), channel_id=1, source_target_pairs={{0,2},{1,5},{2,0},{3,7},{4,6},{5,1},{6,4},{7,3},{8,10},{9,13},{10,... | collective-permute-start | bytes 1769480 | tf_op jit(solution)/shard_map/ppermute | solution.py:793
  200.5 8.4 %collective-permute-start.31 = (bf16[512,384]{1,0:T(8,128)(2,1)S(1)}, bf16[512,384]{1,0:T(8,128)(2,1)S(1)}, u32[]{:S(2)}, u32[]{:S(2)}) collective-permute-start(bf16[512,384]{1,0:T(8,128)(2,1)S(1)} %get-tuple-element.429), channel_id=1, source_target_pairs={{0,1},{1,0},{2,3},{3,2},{4,5},{5,4},{6,7},{7,6},{8,9},{9,8},{10,11... | collective-permute-start | bytes 1179656 | tf_op jit(solution)/shard_map/ppermute | solution.py:733
  200.5 8.4 %collective-permute-start.33 = (bf16[1,240,384]{2,1,0:T(8,128)(2,1)S(1)}, bf16[1,240,384]{2,1,0:T(8,128)(2,1)S(1)}, u32[]{:S(2)}, u32[]{:S(2)}) collective-permute-start(bf16[1,240,384]{2,1,0:T(8,128)(2,1)S(1)} %add_convert_fusion.9), channel_id=1, source_target_pairs={{0,16},{1,9},{2,18},{3,11},{4,20},{5,13},{6,22},{7,15},{8,24},{9,1... | collective-permute-start | bytes 552968 | tf_op jit(solution)/shard_map/ppermute | solution.py:793
  209.7 35.0 %copy-start.25 = (bf16[4,192,384]{2,1,0:T(8,128)(2,1)}, bf16[4,192,384]{2,1,0:T(8,128)(2,1)S(1)}, u32[]{:S(2)}) copy-start(bf16[4,192,384]{2,1,0:T(8,128)(2,1)S(1)} %collective-permute-done.32.refs_10_) | copy-start | bytes 1769476
  209.7 14.3 %collective-permute-start.34 = (bf16[8,48,1280]{2,1,0:T(8,128)(2,1)}, bf16[8,48,1280]{2,1,0:T(8,128)(2,1)S(1)}, u32[]{:S(2)}, u32[]{:S(2)}) collective-permute-start(bf16[8,48,1280]{2,1,0:T(8,128)(2,1)} %get-tuple-element.441), channel_id=1, source_target_pairs={{0,4},{1,3},{2,6},{3,1},{4,0},{5,7},{6,2},{7,5},{8,12},{9,11},{10,... | collective-permute-start | bytes 2949128 | tf_op jit(solution)/shard_map/ppermute | solution.py:793
  224.0 19.6 %collective-permute-start.35 = (bf16[8,240,384]{2,1,0:T(8,128)(2,1)}, bf16[8,240,384]{2,1,0:T(8,128)(2,1)S(1)}, u32[]{:S(2)}, u32[]{:S(2)}) collective-permute-start(bf16[8,240,384]{2,1,0:T(8,128)(2,1)} %get-tuple-element.449), channel_id=1, source_target_pairs={{0,4},{1,3},{2,6},{3,1},{4,0},{5,7},{6,2},{7,5},{8,12},{9,11},{10,... | collective-permute-start | bytes 4423688 | tf_op jit(solution)/shard_map/ppermute | solution.py:793
  224.7 14.9 %collective-permute-start.36 = (bf16[2,192,384]{2,1,0:T(8,128)(2,1)S(1)}, bf16[2,192,384]{2,1,0:T(8,128)(2,1)S(1)}, u32[]{:S(2)}, u32[]{:S(2)}) collective-permute-start(bf16[2,192,384]{2,1,0:T(8,128)(2,1)S(1)} %add_convert_fusion.7), channel_id=1, source_target_pairs={{0,8},{1,17},{2,10},{3,19},{4,12},{5,21},{6,14},{7,23},{8,0},{9,25... | collective-permute-start | bytes 884744 | tf_op jit(solution)/shard_map/ppermute | solution.py:793
  243.6 3.4 %collective-permute-start.37 = (bf16[2,512,768]{2,1,0:T(8,128)(2,1)S(1)}, bf16[2,512,768]{2,1,0:T(8,128)(2,1)S(1)}, u32[]{:S(2)}, u32[]{:S(2)}) collective-permute-start(bf16[2,512,768]{2,1,0:T(8,128)(2,1)S(1)} %get-tuple-element.453), channel_id=1, source_target_pairs={{0,1},{1,0},{2,3},{3,2},{4,5},{5,4},{6,7},{7,6},{8,9},{9,8},{10,11... | collective-permute-start | bytes 4718600 | tf_op jit(solution)/shard_map/ppermute | solution.py:733
  247.0 17.0 %collective-permute-start.38 = (bf16[4,240,384]{2,1,0:T(8,128)(2,1)}, bf16[4,240,384]{2,1,0:T(8,128)(2,1)}, u32[]{:S(2)}, u32[]{:S(2)}) collective-permute-start(bf16[4,240,384]{2,1,0:T(8,128)(2,1)} %add_convert_fusion), channel_id=1, source_target_pairs={{0,2},{1,5},{2,0},{3,7},{4,6},{5,1},{6,4},{7,3},{8,10},{9,13},{10,... | collective-permute-start | bytes 2211848 | tf_op jit(solution)/shard_map/ppermute | solution.py:793
  247.7 16.3 %collective-permute-start.39 = (bf16[4,48,1280]{2,1,0:T(8,128)(2,1)}, bf16[4,48,1280]{2,1,0:T(8,128)(2,1)}, u32[]{:S(2)}, u32[]{:S(2)}) collective-permute-start(bf16[4,48,1280]{2,1,0:T(8,128)(2,1)} %add_convert_fusion.4), channel_id=1, source_target_pairs={{0,2},{1,5},{2,0},{3,7},{4,6},{5,1},{6,4},{7,3},{8,10},{9,13},{10,... | collective-permute-start | bytes 1474568 | tf_op jit(solution)/shard_map/ppermute | solution.py:793
  249.0 12.8 %collective-permute-start.40 = (bf16[1,192,384]{2,1,0:T(8,128)(2,1)S(1)}, bf16[1,192,384]{2,1,0:T(8,128)(2,1)S(1)}, u32[]{:S(2)}, u32[]{:S(2)}) collective-permute-start(bf16[1,192,384]{2,1,0:T(8,128)(2,1)S(1)} %add_convert_fusion.10), channel_id=1, source_target_pairs={{0,16},{1,9},{2,18},{3,11},{4,20},{5,13},{6,22},{7,15},{8,24},{9,1... | collective-permute-start | bytes 442376 | tf_op jit(solution)/shard_map/ppermute | solution.py:793
  264.0 2.8 collective-permute-start.41
  266.9 11.1 %collective-permute-start.43 = (bf16[256,768]{1,0:T(8,128)(2,1)S(1)}, bf16[256,768]{1,0:T(8,128)(2,1)S(1)}, u32[]{:S(2)}, u32[]{:S(2)}) collective-permute-start(bf16[256,768]{1,0:T(8,128)(2,1)S(1)} %get-tuple-element.501), channel_id=1, source_target_pairs={{0,3},{1,2},{2,1},{3,0},{4,7},{5,6},{6,5},{7,4},{8,11},{9,10},{10,... | collective-permute-start | bytes 1179656 | tf_op jit(solution)/shard_map/ppermute | solution.py:736
  267.3 10.6 %collective-permute-start.42 = (bf16[2,240,384]{2,1,0:T(8,128)(2,1)S(1)}, bf16[2,240,384]{2,1,0:T(8,128)(2,1)S(1)}, u32[]{:S(2)}, u32[]{:S(2)}) collective-permute-start(bf16[2,240,384]{2,1,0:T(8,128)(2,1)S(1)} %add_convert_fusion.5), channel_id=1, source_target_pairs={{0,8},{1,17},{2,10},{3,19},{4,12},{5,21},{6,14},{7,23},{8,0},{9,25... | collective-permute-start | bytes 1105928 | tf_op jit(solution)/shard_map/ppermute | solution.py:793
  (41 other events, 389.8 us)

commit v2 on v1

--- a/solution.py
+++ b/solution.py
@@ -974,7 +974,8 @@
         pieces = (slice(4, 8), slice(2, 4), slice(0, 2))
         first = [remote(k, message.at[p], land1.at[p], partners[0]) for k, p in zip((0, 1, 13), pieces)]
         second = [remote(2, send2.at[2:4], land2.at[2:4], partners[1]), remote(3, send2.at[0:2], land2.at[0:2], partners[1])]
-        third, fourth = remote(4, send3, land3, partners[2]), remote(5, send4, land4, partners[3])
+        third = [remote(k, send3.at[p], land3.at[p], partners[2]) for k, p in ((4, slice(1, 2)), (14, slice(0, 1)))]
+        fourth = remote(5, send4, land4, partners[3])
         q_third, q_fourth = remote(6, q_send3, q_land3, partners[2]), remote(7, q_send4, q_land4, partners[3])
         up_fourth = remote(8, up_send, up_land, partners[3])
         swap_b, swap_own = (remote(9 + k, swap_a.at[k], swap_a_land.at[k], other) for k in range(2))
@@ -1020,7 +1021,8 @@
         first[1].wait()
         second[0].wait()
         send3[...] = added([keep[2:4], land1[2:4], land2[2:4]])
-        third.start()
+        for copy in third:
+            copy.start()
 
         q_fourth.wait()
         sums[1] = sums[1] + q_land4[0].astype(F32)
@@ -1033,11 +1035,12 @@
         first[2].wait()
         second[1].wait()
         sums[0] = added([keep[0], land1[0], land2[0]], F32)
-        third.wait()
+        third[0].wait()
         send4[...] = added([keep[1:2], land1[1:2], land2[1:2], land3[1:2]])
         fourth.start()
         swap_qs[1].wait()
         got_q[...] = swap_q_land[1]
+        third[1].wait()
         sums[0] = sums[0] + land3[0].astype(F32)
         fourth.wait()
         sums[0] = sums[0] + land4[0].astype(F32)
@@ -1064,7 +1067,7 @@
             pltpu.VMEM((2,) + chunk, F32), pltpu.VMEM(up_chunk[1:], F32), pltpu.VMEM((down_rows, half), F32),
             pltpu.VMEM((2, each, wide), F32), pltpu.VMEM((2, each, wide), F32),
             pltpu.VMEM((2,) + long, F32), pltpu.VMEM((2,) + long, F32),
-            pltpu.SemaphoreType.DMA((14,)), pltpu.SemaphoreType.DMA((14,)),
+            pltpu.SemaphoreType.DMA((15,)), pltpu.SemaphoreType.DMA((15,)),
             pltpu.SemaphoreType.DMA((len(loaded),)),
         ] + buffers,
         compiler_params=pltpu.CompilerParams(

time: 316 us -> 316 us (level)
  no operation moved by 1% of the time
where the time goes in v2:
time: 316 us; the launch traced here: 312 us
  Pallas kernels  211 us (67%)
  waiting for transfers between devices  43.3 us (14%)
  starting transfers between devices  34.3 us (11%)
  local copies, waits for them, and re-layouts  10.8 us (3%)
  other arithmetic  10.3 us (3%)
    pallas_call x2, Pallas kernels, feed_forward(): pl.pallas_call(functools.partial(feed_forward_kernel, layer, steps), grid...  31.2 us
    ppermute x17, waiting for transfers between devices, transfer(): return lax.ppermute(message, AXES, self.exchange.pairs(self.phase - 1))  29.8 us
    pallas_call x1, Pallas kernels, last_exchanges(): pl.pallas_call(kernel, grid=(1,), in_specs=[pl.BlockSpec(memory_space=pl....  29.4 us
    pallas_call x2, Pallas kernels, feed_back(): pl.pallas_call(functools.partial(feed_back_kernel, layer, steps), grid_sp...  28.5 us
    pallas_call x2, Pallas kernels, attention_backward(): pl.pallas_call(attention_backward_kernel, grid_spec=pltpu.PrefetchScalarG...  27.8 us
    ppermute x17, starting transfers between devices, transfer(): return lax.ppermute(message, AXES, self.exchange.pairs(self.phase - 1))  21.1 us
    pallas_call x2, Pallas kernels, attention_forward(): pl.pallas_call(attention_forward_kernel, grid_spec=pltpu.PrefetchScalarGr...  19.6 us
    pallas_call x2, Pallas kernels, down_gradients(): gradient_call(grad_down_kernel, 'gradient_down', chips, hidden // (2 * wi...  16 us
  transfers between devices with their start and end apart: 44, of which 18 were waited for; matrix products, arithmetic and copies ran while one was open for 3% of the time, Pallas kernels for 56%

profile of v2, /device:TPU:0, one launch (start us, length us, event | category | flops | bytes accessed | tf_op | source)
XLA Modules:
  0.0 312.2 jit_solution(8504603164695946310)
XLA Ops:
  1.9 2.5 collective-permute-start
  4.6 1.5 collective-permute-start.1
  8.2 1.6 collective-permute-start.2
  9.8 2.0 collective-permute-done.2
  11.7 2.6 collective-permute-start.3
  14.3 1.9 collective-permute-done.3
  17.4 5.9 %project.2 = (bf16[512,768]{1,0:T(8,128)(2,1)}, bf16[512,768]{1,0:T(8,128)(2,1)}, bf16[512,1536]{1,0:T(8,128)(2,1)}) custom-call(bf16[512,768]{1,0:T(8,128)(2,1)} %maximum_select_fusion.stream, f32[2,768]{1,0:T(2,128)S(1)} %copy-done.7, f32[2,768]{1,0:T(2,128)S(1)} %copy-done.8, bf16[2,768,2304]{2,1,0:T(8,128)(2,1)} %matrix.7), custom_call_target="tpu_custom_call" | custom-call | flops 1000 | bytes 1000 | tf_op jit(solution)/shard_map/project/pallas_call | solution.py:305
  23.3 3.6 %collective-permute-done.4.kx_ref.vx_ref = bf16[512,1536]{1,0:T(8,128)(2,1)S(1)} collective-permute-done((bf16[512,1536]{1,0:T(8,128)(2,1)}, bf16[512,1536]{1,0:T(8,128)(2,1)S(1)}, u32[]{:S(2)}, u32[]{:S(2)}) %collective-permute-start.4) | collective-permute-done | bytes 1572896 | tf_op jit(solution)/shard_map/ppermute | solution.py:733
  28.0 10.1 %attention_forward.2 = (bf16[512,768]{1,0:T(8,128)(2,1)}, f32[6,8,512]{2,1,0:T(8,128)}) custom-call(s32[1]{0:T(128)} %bitcast.meta, bf16[512,768]{1,0:T(8,128)(2,1)} %get-tuple-element.271.q_ref, bf16[512,1536]{1,0:T(8,128)(2,1)} %get-tuple-element.272.ko_ref.vo_ref, bf16[512,1536]{1,0:T(8,128)(2,1)} %get-tuple-element.272.ko_ref.vo_ref, ...), custom_call_target="tpu_custom_call" | custom-call | flops 1000 | bytes 1000 | tf_op jit(solution)/shard_map/attention_forward/pallas_call | solution.py:140
  38.5 15.5 %feed_forward.2 = (bf16[512,768]{1,0:T(8,128)(2,1)}, bf16[512,768]{1,0:T(8,128)(2,1)}, bf16[512,3072]{1,0:T(8,128)(2,1)}, bf16[512,3072]{1,0:T(8,128)(2,1)}, bf16[512,768]{1,0:T(8,128)(2,1)}) custom-call(bf16[512,768]{1,0:T(8,128)(2,1)} %get-tuple-element.286.attended.co.o_ref, bf16[512,768]{1,0:T(8,128)(2,1)} %maximum_select_fusion.stream, ...), custom_call_target="tpu_custom_call" | custom-call | flops 1000 | bytes 1000 | tf_op jit(solution)/shard_map/feed_forward/pallas_call | solution.py:370
  55.5 5.9 %project.3 = (bf16[512,768]{1,0:T(8,128)(2,1)}, bf16[512,768]{1,0:T(8,128)(2,1)}, bf16[512,1536]{1,0:T(8,128)(2,1)}) custom-call(bf16[512,768]{1,0:T(8,128)(2,1)} %get-tuple-element.313.stream, f32[2,768]{1,0:T(2,128)S(1)} %copy-done.7, f32[2,768]{1,0:T(2,128)S(1)} %copy-done.8, bf16[2,768,2304]{2,1,0:T(8,128)(2,1)} %matrix.7), custom_call_target="tpu_custom_call" | custom-call | flops 1000 | bytes 1000 | tf_op jit(solution)/shard_map/project/pallas_call | solution.py:305
  62.0 1.8 copy-done.20
  66.7 1.8 weigh.1
  69.6 9.5 %attention_forward.3 = (bf16[512,768]{1,0:T(8,128)(2,1)}, f32[6,8,512]{2,1,0:T(8,128)}) custom-call(s32[1]{0:T(128)} %bitcast.meta, bf16[512,768]{1,0:T(8,128)(2,1)} %get-tuple-element.304.q_ref, bf16[512,1536]{1,0:T(8,128)(2,1)} %get-tuple-element.305.ko_ref.vo_ref, bf16[512,1536]{1,0:T(8,128)(2,1)} %get-tuple-element.305.ko_ref.vo_ref, ...), custom_call_target="tpu_custom_call" | custom-call | flops 1000 | bytes 1000 | tf_op jit(solution)/shard_map/attention_forward/pallas_call | solution.py:140
  79.3 15.7 %feed_forward.3 = (bf16[512,768]{1,0:T(8,128)(2,1)}, bf16[512,768]{1,0:T(8,128)(2,1)}, bf16[512,3072]{1,0:T(8,128)(2,1)}, bf16[512,3072]{1,0:T(8,128)(2,1)}, bf1...) custom-call(bf16[512,768]{1,0:T(8,128)(2,1)} %get-tuple-element.320.attended.o_ref.co, ...), custom_call_target="tpu_custom_call" | custom-call | flops 1000 | bytes 1000 | tf_op jit(solution)/shard_map/feed_forward/pallas_call | solution.py:370
  96.5 14.2 %feed_back.2 = (bf16[512,1536]{1,0:T(8,128)(2,1)S(1)}, bf16[512,1536]{1,0:T(8,128)(2,1)S(1)}, bf16[512,768]{1,0:T(8,128)(2,1)S(1)}, bf16[512,384]{1,0:T(8,128)(2...) custom-call(s32[34]{0:T(128)S(1)} %pad_add_fusion.meta, ...), custom_call_target="tpu_custom_call" | custom-call | flops 1000 | bytes 1000 | tf_op jit(solution)/shard_map/feed_back/pallas_call | solution.py:440
  112.1 8.0 %gradient_down.2 = (bf16[8,192,384]{2,1,0:T(8,128)(2,1)}, bf16[8,192,384]{2,1,0:T(8,128)(2,1)}) custom-call(s32[34]{0:T(128)S(1)} %pad_add_fusion.meta, bf16[512,3072]{1,0:T(8,128)(2,1)} %get-tuple-element.334.ao, bf16[512,3072]{1,0:T(8,128)(2,1)} %collective-permute-done.15.ax, bf16[512,768]{1,0:T(8,128)(2,1)S(1)} %get-tuple-element.341.back_out.bo, ...), custom_call_target="tpu_custom_call" | custom-call | flops 1000 | bytes 1000 | tf_op jit(solution)/shard_map/gradient_down/pallas_call | solution.py:696
  120.1 1.5 collective-permute-start.19
  121.7 14.0 %attention_backward.2 = (bf16[512,768]{1,0:T(8,128)(2,1)S(1)}, bf16[2,512,768]{2,1,0:T(8,128)(2,1)}, bf16[2,512,768]{2,1,0:T(8,128)(2,1)S(1)}) custom-call(s32[1]{0:T(128)} %bitcast.meta, bf16[512,768]{1,0:T(8,128)(2,1)} %get-tuple-element.304.q_ref, bf16[512,1536]{1,0:T(8,128)(2,1)} %get-tuple-element.305.ko_ref.vo_ref, ...), custom_call_target="tpu_custom_call" | custom-call | flops 1000 | bytes 1000 | tf_op jit(solution)/shard_map/attention_backward/pallas_call | solution.py:247
  136.8 1.4 collective-permute-start.20
  138.3 7.7 %gradient_up.2 = (bf16[8,240,384]{2,1,0:T(8,128)(2,1)}, bf16[8,240,384]{2,1,0:T(8,128)(2,1)}) custom-call(s32[34]{0:T(128)S(1)} %pad_add_fusion.meta, bf16[512,768]{1,0:T(8,128)(2,1)} %get-tuple-element.333.ao, bf16[512,768]{1,0:T(8,128)(2,1)} %collective-permute-done.14.ax, bf16[512,1536]{1,0:T(8,128)(2,1)S(1)} %get-tuple-element.362.bo, ...), custom_call_target="tpu_custom_call" | custom-call | flops 1000 | bytes 1000 | tf_op jit(solution)/shard_map/gradient_up/pallas_call | solution.py:676
  146.9 1.5 collective-permute-start.22
  148.5 1.6 collective-permute-start.23
  150.1 7.1 %project_back.2 = (bf16[512,1152]{1,0:T(8,128)(2,1)S(1)}, bf16[512,1152]{1,0:T(8,128)(2,1)S(1)}, bf16[512,768]{1,0:T(8,128)(2,1)S(1)}, bf16[512,384]{1,0:T(8,128)(2,1)S(1)}, f32[8,768]{1,0:T(8,128)S(1)}) custom-call(s32[34]{0:T(128)S(1)} %pad_add_fusion.meta, bf16[512,768]{1,0:T(8,128)(2,1)} %copy-done.3, bf16[2,512,768]{2,1,0:T(8,128)(2,1)} %get-tuple-element.375.own, ...), custom_call_target="tpu_custom_call" | custom-call | flops 1000 | bytes 1000 | tf_op jit(solution)/shard_map/project_back/pallas_call | solution.py:523
  157.2 9.4 %collective-permute-done.22.refs_6_ = bf16[8,240,384]{2,1,0:T(8,128)(2,1)S(1)} collective-permute-done((bf16[8,240,384]{2,1,0:T(8,128)(2,1)}, bf16[8,240,384]{2,1,0:T(8,128)(2,1)S(1)}, u32[]{:S(2)}, u32[]{:S(2)}) %collective-permute-start.22) | collective-permute-done | bytes 1474592 | tf_op jit(solution)/shard_map/ppermute | solution.py:793
  166.9 1.4 collective-permute-done.24.bx
  168.4 1.3 collective-permute-start.26
  169.8 2.6 collective-permute-start.27
  172.4 8.0 %gradient_down.3 = (bf16[8,192,384]{2,1,0:T(8,128)(2,1)}, bf16[8,192,384]{2,1,0:T(8,128)(2,1)}) custom-call(s32[34]{0:T(128)S(1)} %pad_add_fusion.meta, bf16[512,3072]{1,0:T(8,128)(2,1)} %get-tuple-element.295.ao, bf16[512,3072]{1,0:T(8,128)(2,1)} %copy-done.20, bf16[512,768]{1,0:T(8,128)(2,1)S(1)} %get-tuple-element.401.bo.back_out, ...), custom_call_target="tpu_custom_call" | custom-call | flops 1000 | bytes 1000 | tf_op jit(solution)/shard_map/gradient_down/pallas_call | solution.py:696
  181.9 1.5 collective-permute-start.28
  183.4 1.6 collective-permute-start.29
  185.0 14.3 %feed_back.3 = (bf16[512,1536]{1,0:T(8,128)(2,1)S(1)}, bf16[512,1536]{1,0:T(8,128)(2,1)S(1)}, bf16[512,768]{1,0:T(8,128)(2,1)S(1)}, bf16[512,384]{1,0:T(8,128)(2...) custom-call(s32[34]{0:T(128)S(1)} %pad_add_fusion.meta, ...), custom_call_target="tpu_custom_call" | custom-call | flops 1000 | bytes 1000 | tf_op jit(solution)/shard_map/feed_back/pallas_call | solution.py:440
  200.5 1.4 collective-permute-start.33
  201.9 5.5 %gradient_qkv.2 = (bf16[8,48,1280]{2,1,0:T(8,128)(2,1)}, bf16[8,48,1280]{2,1,0:T(8,128)(2,1)}) custom-call(s32[34]{0:T(128)S(1)} %pad_add_fusion.meta, bf16[512,768]{1,0:T(8,128)(2,1)} %get-tuple-element.309.ao, bf16[512,768]{1,0:T(8,128)(2,1)} %copy-done.28, bf16[512,1152]{1,0:T(8,128)(2,1)S(1)} %get-tuple-element.424.bo, ...), custom_call_target="tpu_custom_call" | custom-call | flops 1000 | bytes 1000 | tf_op jit(solution)/shard_map/gradient_qkv/pallas_call | solution.py:714
  207.4 1.5 collective-permute-done.33.refs_9_
  210.4 7.7 %gradient_up.3 = (bf16[8,240,384]{2,1,0:T(8,128)(2,1)}, bf16[8,240,384]{2,1,0:T(8,128)(2,1)}) custom-call(s32[34]{0:T(128)S(1)} %pad_add_fusion.meta, bf16[512,768]{1,0:T(8,128)(2,1)} %get-tuple-element.294.ao, bf16[512,768]{1,0:T(8,128)(2,1)} %copy-done.30, bf16[512,1536]{1,0:T(8,128)(2,1)S(1)} %get-tuple-element.434.bo, ...), custom_call_target="tpu_custom_call" | custom-call | flops 1000 | bytes 1000 | tf_op jit(solution)/shard_map/gradient_up/pallas_call | solution.py:676
  218.3 5.7 %collective-permute-done.34.refs_2_ = bf16[8,48,1280]{2,1,0:T(8,128)(2,1)S(1)} collective-permute-done((bf16[8,48,1280]{2,1,0:T(8,128)(2,1)}, bf16[8,48,1280]{2,1,0:T(8,128)(2,1)S(1)}, u32[]{:S(2)}, u32[]{:S(2)}) %collective-permute-start.34) | collective-permute-done | bytes 983072 | tf_op jit(solution)/shard_map/ppermute | solution.py:793
  225.8 13.8 %attention_backward.3 = (bf16[512,768]{1,0:T(8,128)(2,1)S(1)}, bf16[2,512,768]{2,1,0:T(8,128)(2,1)}, bf16[2,512,768]{2,1,0:T(8,128)(2,1)S(1)}) custom-call(s32[1]{0:T(128)} %bitcast.meta, bf16[512,768]{1,0:T(8,128)(2,1)} %get-tuple-element.271.q_ref, bf16[512,1536]{1,0:T(8,128)(2,1)} %get-tuple-element.272.ko_ref.vo_ref, ...), custom_call_target="tpu_custom_call" | custom-call | flops 1000 | bytes 1000 | tf_op jit(solution)/shard_map/attention_backward/pallas_call | solution.py:247
  239.7 3.9 %collective-permute-done.35.refs_5_ = bf16[8,240,384]{2,1,0:T(8,128)(2,1)S(1)} collective-permute-done((bf16[8,240,384]{2,1,0:T(8,128)(2,1)}, bf16[8,240,384]{2,1,0:T(8,128)(2,1)S(1)}, u32[]{:S(2)}, u32[]{:S(2)}) %collective-permute-start.35) | collective-permute-done | bytes 1474592 | tf_op jit(solution)/shard_map/ppermute | solution.py:793
  247.7 1.3 collective-permute-start.39
  251.0 7.9 %project_back.3 = (bf16[512,1152]{1,0:T(8,128)(2,1)S(1)}, bf16[512,1152]{1,0:T(8,128)(2,1)S(1)}, bf16[512,768]{1,0:T(8,128)(2,1)S(1)}, bf16[512,384]{1,0:T(8,128...) custom-call(s32[34]{0:T(128)S(1)} %pad_add_fusion.meta, bf16[512,768]{1,0:T(8,128)(2,1)} %copy-done.4, ...), custom_call_target="tpu_custom_call" | custom-call | flops 1000 | bytes 1000 | tf_op jit(solution)/shard_map/project_back/pallas_call | solution.py:523
  258.9 1.9 collect.1
  261.8 2.2 collective-permute-done.39.refs_3_
  265.3 1.6 collective-permute-done.41.bx
  267.8 5.5 %gradient_qkv.3 = (bf16[8,48,1280]{2,1,0:T(8,128)(2,1)}, bf16[8,48,1280]{2,1,0:T(8,128)(2,1)}) custom-call(s32[34]{0:T(128)S(1)} %pad_add_fusion.meta, bf16[512,768]{1,0:T(8,128)(2,1)} %get-tuple-element.276.ao, bf16[512,768]{1,0:T(8,128)(2,1)} %collective-permute-done.5.ax, bf16[512,1152]{1,0:T(8,128)(2,1)S(1)} %get-tuple-element.495.bo, ...), custom_call_target="tpu_custom_call" | custom-call | flops 1000 | bytes 1000 | tf_op jit(solution)/shard_map/gradient_qkv/pallas_call | solution.py:714
  273.3 4.6 %collective-permute-done.42.refs_7_ = bf16[2,240,384]{2,1,0:T(8,128)(2,1)S(1)} collective-permute-done((bf16[2,240,384]{2,1,0:T(8,128)(2,1)S(1)}, bf16[2,240,384]{2,1,0:T(8,128)(2,1)S(1)}, u32[]{:S(2)}, u32[]{:S(2)}) %collective-permute-start.42) | collective-permute-done | bytes 368672 | tf_op jit(solution)/shard_map/ppermute | solution.py:793
  278.7 29.4 %last_exchanges.1 = (f32[216,384]{1,0:T(8,128)S(1)}, f32[216,384]{1,0:T(8,128)S(1)}, f32[216,384]{1,0:T(8,128)S(1)}, f32[24,1280]{1,0:T(8,128)S(1)}, f32[24,1280...) custom-call(bf16[8,48,1280]{2,1,0:T(8,128)(2,1)} %get-tuple-element.503.refs_0_, ...), custom_call_target="tpu_custom_call" | custom-call | flops 1000 | bytes 1000 | tf_op jit(solution)/shard_map/last_exchanges/pallas_call | solution.py:1056
  309.5 1.3 fusion
  (188 shorter events, 35.9 us)
Async XLA Ops:
  1.9 14.2 %collective-permute-start = (bf16[256,768]{1,0:T(8,128)(2,1)S(1)}, bf16[256,768]{1,0:T(8,128)(2,1)S(1)}, u32[]{:S(2)}, u32[]{:S(2)}) collective-permute-start(bf16[256,768]{1,0:T(8,128)(2,1)S(1)} %get-tuple-element.523), channel_id=1, source_target_pairs={{0,3},{1,2},{2,1},{3,0},{4,7},{5,6},{6,5},{7,4},{8,11},{9,10},{10,... | collective-permute-start | bytes 1179656 | tf_op jit(solution)/shard_map/ppermute | solution.py:736
  4.6 3.6 %collective-permute-start.1 = (f32[3]{0:T(128)S(1)}, f32[3]{0:T(128)S(1)}, u32[]{:S(2)}, u32[]{:S(2)}) collective-permute-start(f32[3]{0:T(128)S(1)} %select_reduce_fusion.1), channel_id=1, source_target_pairs={{0,4},{4,0},{8,12},{12,8},{16,20},{20,16},{24,28},{28,24},{1,5},{5... | collective-permute-start | bytes 44 | tf_op jit(solution)/shard_map/ppermute | solution.py:1141
  8.2 3.5 %collective-permute-start.2 = (f32[3]{0:T(128)S(1)}, f32[3]{0:T(128)S(1)}, u32[]{:S(2)}, u32[]{:S(2)}) collective-permute-start(f32[3]{0:T(128)S(1)} %add.101), channel_id=1, source_target_pairs={{0,8},{4,12},{8,0},{12,4},{16,24},{20,28},{24,16},{28,20},{1,9},{5... | collective-permute-start | bytes 44 | tf_op jit(solution)/shard_map/ppermute | solution.py:1141
  11.7 4.4 %collective-permute-start.3 = (f32[3]{0:T(128)S(1)}, f32[3]{0:T(128)S(1)}, u32[]{:S(2)}, u32[]{:S(2)}) collective-permute-start(f32[3]{0:T(128)S(1)} %add.102), channel_id=1, source_target_pairs={{0,16},{4,20},{8,24},{12,28},{16,0},{20,4},{24,8},{28,12},{1,17},{... | collective-permute-start | bytes 44 | tf_op jit(solution)/shard_map/ppermute | solution.py:1141
  23.3 3.6 %collective-permute-start.4 = (bf16[512,1536]{1,0:T(8,128)(2,1)}, bf16[512,1536]{1,0:T(8,128)(2,1)S(1)}, u32[]{:S(2)}, u32[]{:S(2)}) collective-permute-start(bf16[512,1536]{1,0:T(8,128)(2,1)} %get-tuple-element.272.ko_ref.vo_ref), channel_id=1, source_target_pairs={{0,1},{1,0},{2,3},{3,2},{4,5},{5,4},{6,7},{7,6},{8,9},{9,8},{10,11... | collective-permute-start | bytes 4718600 | tf_op jit(solution)/shard_map/ppermute | solution.py:733
  26.9 11.3 %collective-permute-start.5 = (bf16[512,768]{1,0:T(8,128)(2,1)}, bf16[512,768]{1,0:T(8,128)(2,1)}, u32[]{:S(2)}, u32[]{:S(2)}) collective-permute-start(bf16[512,768]{1,0:T(8,128)(2,1)} %get-tuple-element.276.ao), channel_id=1, source_target_pairs={{0,1},{1,0},{2,3},{3,2},{4,5},{5,4},{6,7},{7,6},{8,9},{9,8},{10,11... | collective-permute-start | bytes 2359304 | tf_op jit(solution)/shard_map/ppermute | solution.py:733
  27.0 11.2 %collective-permute-start.6 = (bf16[256,768]{1,0:T(8,128)(2,1)}, bf16[256,768]{1,0:T(8,128)(2,1)S(1)}, u32[]{:S(2)}, u32[]{:S(2)}) collective-permute-start(bf16[256,768]{1,0:T(8,128)(2,1)} %get-tuple-element.277), channel_id=1, source_target_pairs={{0,3},{1,2},{2,1},{3,0},{4,7},{5,6},{6,5},{7,4},{8,11},{9,10},{10,... | collective-permute-start | bytes 1179656 | tf_op jit(solution)/shard_map/ppermute | solution.py:736
  38.2 15.9 %collective-permute-start.7 = (bf16[512,768]{1,0:T(8,128)(2,1)}, bf16[512,768]{1,0:T(8,128)(2,1)S(1)}, u32[]{:S(2)}, u32[]{:S(2)}) collective-permute-start(bf16[512,768]{1,0:T(8,128)(2,1)} %get-tuple-element.286.attended.co.o_ref), channel_id=1, source_target_pairs={{0,1},{1,0},{2,3},{3,2},{4,5},{5,4},{6,7},{7,6},{8,9},{9,8},{10,11... | collective-permute-start | bytes 2359304 | tf_op jit(solution)/shard_map/ppermute | solution.py:733
  55.0 7.0 %collective-permute-start.9 = (bf16[512,3072]{1,0:T(8,128)(2,1)}, bf16[512,3072]{1,0:T(8,128)(2,1)S(1)}, u32[]{:S(2)}, u32[]{:S(2)}) collective-permute-start(bf16[512,3072]{1,0:T(8,128)(2,1)} %get-tuple-element.295.ao), channel_id=1, source_target_pairs={{0,1},{1,0},{2,3},{3,2},{4,5},{5,4},{6,7},{7,6},{8,9},{9,8},{10,11... | collective-permute-start | bytes 9437192 | tf_op jit(solution)/shard_map/ppermute | solution.py:733
  55.2 6.8 %collective-permute-start.8 = (bf16[512,768]{1,0:T(8,128)(2,1)}, bf16[512,768]{1,0:T(8,128)(2,1)S(1)}, u32[]{:S(2)}, u32[]{:S(2)}) collective-permute-start(bf16[512,768]{1,0:T(8,128)(2,1)} %get-tuple-element.294.ao), channel_id=1, source_target_pairs={{0,1},{1,0},{2,3},{3,2},{4,5},{5,4},{6,7},{7,6},{8,9},{9,8},{10,11... | collective-permute-start | bytes 2359304 | tf_op jit(solution)/shard_map/ppermute | solution.py:733
  63.9 4.5 %collective-permute-start.10 = (bf16[512,1536]{1,0:T(8,128)(2,1)}, bf16[512,1536]{1,0:T(8,128)(2,1)S(1)}, u32[]{:S(2)}, u32[]{:S(2)}) collective-permute-start(bf16[512,1536]{1,0:T(8,128)(2,1)} %get-tuple-element.305.ko_ref.vo_ref), channel_id=1, source_target_pairs={{0,1},{1,0},{2,3},{3,2},{4,5},{5,4},{6,7},{7,6},{8,9},{9,8},{10,11... | collective-permute-start | bytes 4718600 | tf_op jit(solution)/shard_map/ppermute | solution.py:733
  68.5 10.7 %collective-permute-start.11 = (bf16[512,768]{1,0:T(8,128)(2,1)}, bf16[512,768]{1,0:T(8,128)(2,1)S(1)}, u32[]{:S(2)}, u32[]{:S(2)}) collective-permute-start(bf16[512,768]{1,0:T(8,128)(2,1)} %get-tuple-element.309.ao), channel_id=1, source_target_pairs={{0,1},{1,0},{2,3},{3,2},{4,5},{5,4},{6,7},{7,6},{8,9},{9,8},{10,11... | collective-permute-start | bytes 2359304 | tf_op jit(solution)/shard_map/ppermute | solution.py:733
  68.8 10.3 %collective-permute-start.12 = (bf16[512,384]{1,0:T(8,128)(2,1)S(1)}, bf16[512,384]{1,0:T(8,128)(2,1)S(1)}, u32[]{:S(2)}, u32[]{:S(2)}) collective-permute-start(bf16[512,384]{1,0:T(8,128)(2,1)S(1)} %get-tuple-element.310), channel_id=1, source_target_pairs={{0,1},{1,0},{2,3},{3,2},{4,5},{5,4},{6,7},{7,6},{8,9},{9,8},{10,11... | collective-permute-start | bytes 1179656 | tf_op jit(solution)/shard_map/ppermute | solution.py:733
  79.2 15.8 %collective-permute-start.13 = (bf16[512,768]{1,0:T(8,128)(2,1)}, bf16[512,768]{1,0:T(8,128)(2,1)S(1)}, u32[]{:S(2)}, u32[]{:S(2)}) collective-permute-start(bf16[512,768]{1,0:T(8,128)(2,1)} %get-tuple-element.320.attended.o_ref.co), channel_id=1, source_target_pairs={{0,1},{1,0},{2,3},{3,2},{4,5},{5,4},{6,7},{7,6},{8,9},{9,8},{10,11... | collective-permute-start | bytes 2359304 | tf_op jit(solution)/shard_map/ppermute | solution.py:733
  95.0 16.5 %collective-permute-start.15 = (bf16[512,3072]{1,0:T(8,128)(2,1)}, bf16[512,3072]{1,0:T(8,128)(2,1)}, u32[]{:S(2)}, u32[]{:S(2)}) collective-permute-start(bf16[512,3072]{1,0:T(8,128)(2,1)} %get-tuple-element.334.ao), channel_id=1, source_target_pairs={{0,1},{1,0},{2,3},{3,2},{4,5},{5,4},{6,7},{7,6},{8,9},{9,8},{10,11... | collective-permute-start | bytes 9437192 | tf_op jit(solution)/shard_map/ppermute | solution.py:733
  95.6 16.0 %collective-permute-start.14 = (bf16[512,768]{1,0:T(8,128)(2,1)}, bf16[512,768]{1,0:T(8,128)(2,1)}, u32[]{:S(2)}, u32[]{:S(2)}) collective-permute-start(bf16[512,768]{1,0:T(8,128)(2,1)} %get-tuple-element.333.ao), channel_id=1, source_target_pairs={{0,1},{1,0},{2,3},{3,2},{4,5},{5,4},{6,7},{7,6},{8,9},{9,8},{10,11... | collective-permute-start | bytes 2359304 | tf_op jit(solution)/shard_map/ppermute | solution.py:733
  95.6 15.9 %collective-permute-start.16 = (bf16[256,768]{1,0:T(8,128)(2,1)S(1)}, bf16[256,768]{1,0:T(8,128)(2,1)S(1)}, u32[]{:S(2)}, u32[]{:S(2)}) collective-permute-start(bf16[256,768]{1,0:T(8,128)(2,1)S(1)} %get-tuple-element.335), channel_id=1, source_target_pairs={{0,3},{1,2},{2,1},{3,0},{4,7},{5,6},{6,5},{7,4},{8,11},{9,10},{10,... | collective-permute-start | bytes 1179656 | tf_op jit(solution)/shard_map/ppermute | solution.py:736
  111.6 8.6 %collective-permute-start.17 = (bf16[512,1536]{1,0:T(8,128)(2,1)S(1)}, bf16[512,1536]{1,0:T(8,128)(2,1)S(1)}, u32[]{:S(2)}, u32[]{:S(2)}) collective-permute-start(bf16[512,1536]{1,0:T(8,128)(2,1)S(1)} %get-tuple-element.345), channel_id=1, source_target_pairs={{0,1},{1,0},{2,3},{3,2},{4,5},{5,4},{6,7},{7,6},{8,9},{9,8},{10,11... | collective-permute-start | bytes 4718600 | tf_op jit(solution)/shard_map/ppermute | solution.py:733
  112.0 8.1 %collective-permute-start.18 = (bf16[512,384]{1,0:T(8,128)(2,1)S(1)}, bf16[512,384]{1,0:T(8,128)(2,1)S(1)}, u32[]{:S(2)}, u32[]{:S(2)}) collective-permute-start(bf16[512,384]{1,0:T(8,128)(2,1)S(1)} %get-tuple-element.346), channel_id=1, source_target_pairs={{0,1},{1,0},{2,3},{3,2},{4,5},{5,4},{6,7},{7,6},{8,9},{9,8},{10,11... | collective-permute-start | bytes 1179656 | tf_op jit(solution)/shard_map/ppermute | solution.py:733
  120.1 16.5 %collective-permute-start.19 = (bf16[8,192,384]{2,1,0:T(8,128)(2,1)}, bf16[8,192,384]{2,1,0:T(8,128)(2,1)S(1)}, u32[]{:S(2)}, u32[]{:S(2)}) collective-permute-start(bf16[8,192,384]{2,1,0:T(8,128)(2,1)} %get-tuple-element.353), channel_id=1, source_target_pairs={{0,4},{1,3},{2,6},{3,1},{4,0},{5,7},{6,2},{7,5},{8,12},{9,11},{10,... | collective-permute-start | bytes 3538952 | tf_op jit(solution)/shard_map/ppermute | solution.py:793
  136.6 30.0 %copy-start.19 = (bf16[8,192,384]{2,1,0:T(8,128)(2,1)}, bf16[8,192,384]{2,1,0:T(8,128)(2,1)S(1)}, u32[]{:S(2)}) copy-start(bf16[8,192,384]{2,1,0:T(8,128)(2,1)S(1)} %collective-permute-done.19.refs_1_) | copy-start | bytes 3538948
  136.8 10.0 %collective-permute-start.21 = (bf16[2,512,768]{2,1,0:T(8,128)(2,1)S(1)}, bf16[2,512,768]{2,1,0:T(8,128)(2,1)S(1)}, u32[]{:S(2)}, u32[]{:S(2)}) collective-permute-start(bf16[2,512,768]{2,1,0:T(8,128)(2,1)S(1)} %get-tuple-element.370), channel_id=1, source_target_pairs={{0,1},{1,0},{2,3},{3,2},{4,5},{5,4},{6,7},{7,6},{8,9},{9,8},{10,11... | collective-permute-start | bytes 4718600 | tf_op jit(solution)/shard_map/ppermute | solution.py:733
  136.8 9.9 %collective-permute-start.20 = (bf16[4,192,384]{2,1,0:T(8,128)(2,1)S(1)}, bf16[4,192,384]{2,1,0:T(8,128)(2,1)S(1)}, u32[]{:S(2)}, u32[]{:S(2)}) collective-permute-start(bf16[4,192,384]{2,1,0:T(8,128)(2,1)S(1)} %add_convert_fusion.3), channel_id=1, source_target_pairs={{0,2},{1,5},{2,0},{3,7},{4,6},{5,1},{6,4},{7,3},{8,10},{9,13},{10,... | collective-permute-start | bytes 1769480 | tf_op jit(solution)/shard_map/ppermute | solution.py:793
  146.9 19.6 %collective-permute-start.22 = (bf16[8,240,384]{2,1,0:T(8,128)(2,1)}, bf16[8,240,384]{2,1,0:T(8,128)(2,1)S(1)}, u32[]{:S(2)}, u32[]{:S(2)}) collective-permute-start(bf16[8,240,384]{2,1,0:T(8,128)(2,1)} %get-tuple-element.383), channel_id=1, source_target_pairs={{0,4},{1,3},{2,6},{3,1},{4,0},{5,7},{6,2},{7,5},{8,12},{9,11},{10,... | collective-permute-start | bytes 4423688 | tf_op jit(solution)/shard_map/ppermute | solution.py:793
  148.5 8.7 %collective-permute-start.23 = (bf16[2,192,384]{2,1,0:T(8,128)(2,1)S(1)}, bf16[2,192,384]{2,1,0:T(8,128)(2,1)S(1)}, u32[]{:S(2)}, u32[]{:S(2)}) collective-permute-start(bf16[2,192,384]{2,1,0:T(8,128)(2,1)S(1)} %add_convert_fusion.8), channel_id=1, source_target_pairs={{0,8},{1,17},{2,10},{3,19},{4,12},{5,21},{6,14},{7,23},{8,0},{9,25... | collective-permute-start | bytes 884744 | tf_op jit(solution)/shard_map/ppermute | solution.py:793
  166.6 32.8 %copy-start.13 = (bf16[8,240,384]{2,1,0:T(8,128)(2,1)}, bf16[8,240,384]{2,1,0:T(8,128)(2,1)S(1)}, u32[]{:S(2)}) copy-start(bf16[8,240,384]{2,1,0:T(8,128)(2,1)S(1)} %collective-permute-done.22.refs_6_) | copy-start | bytes 4423684
  166.6 1.7 collective-permute-start.24
  168.3 12.1 %collective-permute-start.25 = (bf16[512,1152]{1,0:T(8,128)(2,1)S(1)}, bf16[512,1152]{1,0:T(8,128)(2,1)S(1)}, u32[]{:S(2)}, u32[]{:S(2)}) collective-permute-start(bf16[512,1152]{1,0:T(8,128)(2,1)S(1)} %get-tuple-element.396), channel_id=1, source_target_pairs={{0,1},{1,0},{2,3},{3,2},{4,5},{5,4},{6,7},{7,6},{8,9},{9,8},{10,11... | collective-permute-start | bytes 3538952 | tf_op jit(solution)/shard_map/ppermute | solution.py:733
  168.4 11.9 %collective-permute-start.26 = (bf16[4,240,384]{2,1,0:T(8,128)(2,1)S(1)}, bf16[4,240,384]{2,1,0:T(8,128)(2,1)S(1)}, u32[]{:S(2)}, u32[]{:S(2)}) collective-permute-start(bf16[4,240,384]{2,1,0:T(8,128)(2,1)S(1)} %add_convert_fusion.1), channel_id=1, source_target_pairs={{0,2},{1,5},{2,0},{3,7},{4,6},{5,1},{6,4},{7,3},{8,10},{9,13},{10,... | collective-permute-start | bytes 2211848 | tf_op jit(solution)/shard_map/ppermute | solution.py:793
  169.8 10.6 %collective-permute-start.27 = (bf16[1,192,384]{2,1,0:T(8,128)(2,1)S(1)}, bf16[1,192,384]{2,1,0:T(8,128)(2,1)S(1)}, u32[]{:S(2)}, u32[]{:S(2)}) collective-permute-start(bf16[1,192,384]{2,1,0:T(8,128)(2,1)S(1)} %add_convert_fusion.11), channel_id=1, source_target_pairs={{0,16},{1,9},{2,18},{3,11},{4,20},{5,13},{6,22},{7,15},{8,24},{9,1... | collective-permute-start | bytes 442376 | tf_op jit(solution)/shard_map/ppermute | solution.py:793
  181.9 17.4 %collective-permute-start.28 = (bf16[8,192,384]{2,1,0:T(8,128)(2,1)S(1)}, bf16[8,192,384]{2,1,0:T(8,128)(2,1)S(1)}, u32[]{:S(2)}, u32[]{:S(2)}) collective-permute-start(bf16[8,192,384]{2,1,0:T(8,128)(2,1)S(1)} %copy-done.42), channel_id=1, source_target_pairs={{0,4},{1,3},{2,6},{3,1},{4,0},{5,7},{6,2},{7,5},{8,12},{9,11},{10,... | collective-permute-start | bytes 3538952 | tf_op jit(solution)/shard_map/ppermute | solution.py:793
  183.4 15.9 %collective-permute-start.29 = (bf16[2,240,384]{2,1,0:T(8,128)(2,1)S(1)}, bf16[2,240,384]{2,1,0:T(8,128)(2,1)S(1)}, u32[]{:S(2)}, u32[]{:S(2)}) collective-permute-start(bf16[2,240,384]{2,1,0:T(8,128)(2,1)S(1)} %add_convert_fusion.6), channel_id=1, source_target_pairs={{0,8},{1,17},{2,10},{3,19},{4,12},{5,21},{6,14},{7,23},{8,0},{9,25... | collective-permute-start | bytes 1105928 | tf_op jit(solution)/shard_map/ppermute | solution.py:793
  199.3 45.3 %copy-start.17 = (bf16[8,192,384]{2,1,0:T(8,128)(2,1)}, bf16[8,192,384]{2,1,0:T(8,128)(2,1)S(1)}, u32[]{:S(2)}) copy-start(bf16[8,192,384]{2,1,0:T(8,128)(2,1)S(1)} %collective-permute-done.28.refs_9_) | copy-start | bytes 3538948
  199.6 10.0 %collective-permute-start.30 = (bf16[512,1536]{1,0:T(8,128)(2,1)S(1)}, bf16[512,1536]{1,0:T(8,128)(2,1)S(1)}, u32[]{:S(2)}, u32[]{:S(2)}) collective-permute-start(bf16[512,1536]{1,0:T(8,128)(2,1)S(1)} %get-tuple-element.428), channel_id=1, source_target_pairs={{0,1},{1,0},{2,3},{3,2},{4,5},{5,4},{6,7},{7,6},{8,9},{9,8},{10,11... | collective-permute-start | bytes 4718600 | tf_op jit(solution)/shard_map/ppermute | solution.py:733
  199.7 9.9 %collective-permute-start.32 = (bf16[4,192,384]{2,1,0:T(8,128)(2,1)S(1)}, bf16[4,192,384]{2,1,0:T(8,128)(2,1)S(1)}, u32[]{:S(2)}, u32[]{:S(2)}) collective-permute-start(bf16[4,192,384]{2,1,0:T(8,128)(2,1)S(1)} %add_convert_fusion.2), channel_id=1, source_target_pairs={{0,2},{1,5},{2,0},{3,7},{4,6},{5,1},{6,4},{7,3},{8,10},{9,13},{10,... | collective-permute-start | bytes 1769480 | tf_op jit(solution)/shard_map/ppermute | solution.py:793
  200.5 8.4 %collective-permute-start.31 = (bf16[512,384]{1,0:T(8,128)(2,1)S(1)}, bf16[512,384]{1,0:T(8,128)(2,1)S(1)}, u32[]{:S(2)}, u32[]{:S(2)}) collective-permute-start(bf16[512,384]{1,0:T(8,128)(2,1)S(1)} %get-tuple-element.429), channel_id=1, source_target_pairs={{0,1},{1,0},{2,3},{3,2},{4,5},{5,4},{6,7},{7,6},{8,9},{9,8},{10,11... | collective-permute-start | bytes 1179656 | tf_op jit(solution)/shard_map/ppermute | solution.py:733
  200.5 8.4 %collective-permute-start.33 = (bf16[1,240,384]{2,1,0:T(8,128)(2,1)S(1)}, bf16[1,240,384]{2,1,0:T(8,128)(2,1)S(1)}, u32[]{:S(2)}, u32[]{:S(2)}) collective-permute-start(bf16[1,240,384]{2,1,0:T(8,128)(2,1)S(1)} %add_convert_fusion.9), channel_id=1, source_target_pairs={{0,16},{1,9},{2,18},{3,11},{4,20},{5,13},{6,22},{7,15},{8,24},{9,1... | collective-permute-start | bytes 552968 | tf_op jit(solution)/shard_map/ppermute | solution.py:793
  209.7 35.0 %copy-start.25 = (bf16[4,192,384]{2,1,0:T(8,128)(2,1)}, bf16[4,192,384]{2,1,0:T(8,128)(2,1)S(1)}, u32[]{:S(2)}) copy-start(bf16[4,192,384]{2,1,0:T(8,128)(2,1)S(1)} %collective-permute-done.32.refs_10_) | copy-start | bytes 1769476
  209.7 14.3 %collective-permute-start.34 = (bf16[8,48,1280]{2,1,0:T(8,128)(2,1)}, bf16[8,48,1280]{2,1,0:T(8,128)(2,1)S(1)}, u32[]{:S(2)}, u32[]{:S(2)}) collective-permute-start(bf16[8,48,1280]{2,1,0:T(8,128)(2,1)} %get-tuple-element.441), channel_id=1, source_target_pairs={{0,4},{1,3},{2,6},{3,1},{4,0},{5,7},{6,2},{7,5},{8,12},{9,11},{10,... | collective-permute-start | bytes 2949128 | tf_op jit(solution)/shard_map/ppermute | solution.py:793
  224.0 19.6 %collective-permute-start.35 = (bf16[8,240,384]{2,1,0:T(8,128)(2,1)}, bf16[8,240,384]{2,1,0:T(8,128)(2,1)S(1)}, u32[]{:S(2)}, u32[]{:S(2)}) collective-permute-start(bf16[8,240,384]{2,1,0:T(8,128)(2,1)} %get-tuple-element.449), channel_id=1, source_target_pairs={{0,4},{1,3},{2,6},{3,1},{4,0},{5,7},{6,2},{7,5},{8,12},{9,11},{10,... | collective-permute-start | bytes 4423688 | tf_op jit(solution)/shard_map/ppermute | solution.py:793
  224.7 14.9 %collective-permute-start.36 = (bf16[2,192,384]{2,1,0:T(8,128)(2,1)S(1)}, bf16[2,192,384]{2,1,0:T(8,128)(2,1)S(1)}, u32[]{:S(2)}, u32[]{:S(2)}) collective-permute-start(bf16[2,192,384]{2,1,0:T(8,128)(2,1)S(1)} %add_convert_fusion.7), channel_id=1, source_target_pairs={{0,8},{1,17},{2,10},{3,19},{4,12},{5,21},{6,14},{7,23},{8,0},{9,25... | collective-permute-start | bytes 884744 | tf_op jit(solution)/shard_map/ppermute | solution.py:793
  243.6 3.4 %collective-permute-start.37 = (bf16[2,512,768]{2,1,0:T(8,128)(2,1)S(1)}, bf16[2,512,768]{2,1,0:T(8,128)(2,1)S(1)}, u32[]{:S(2)}, u32[]{:S(2)}) collective-permute-start(bf16[2,512,768]{2,1,0:T(8,128)(2,1)S(1)} %get-tuple-element.453), channel_id=1, source_target_pairs={{0,1},{1,0},{2,3},{3,2},{4,5},{5,4},{6,7},{7,6},{8,9},{9,8},{10,11... | collective-permute-start | bytes 4718600 | tf_op jit(solution)/shard_map/ppermute | solution.py:733
  247.0 17.0 %collective-permute-start.38 = (bf16[4,240,384]{2,1,0:T(8,128)(2,1)}, bf16[4,240,384]{2,1,0:T(8,128)(2,1)}, u32[]{:S(2)}, u32[]{:S(2)}) collective-permute-start(bf16[4,240,384]{2,1,0:T(8,128)(2,1)} %add_convert_fusion), channel_id=1, source_target_pairs={{0,2},{1,5},{2,0},{3,7},{4,6},{5,1},{6,4},{7,3},{8,10},{9,13},{10,... | collective-permute-start | bytes 2211848 | tf_op jit(solution)/shard_map/ppermute | solution.py:793
  247.7 16.3 %collective-permute-start.39 = (bf16[4,48,1280]{2,1,0:T(8,128)(2,1)}, bf16[4,48,1280]{2,1,0:T(8,128)(2,1)}, u32[]{:S(2)}, u32[]{:S(2)}) collective-permute-start(bf16[4,48,1280]{2,1,0:T(8,128)(2,1)} %add_convert_fusion.4), channel_id=1, source_target_pairs={{0,2},{1,5},{2,0},{3,7},{4,6},{5,1},{6,4},{7,3},{8,10},{9,13},{10,... | collective-permute-start | bytes 1474568 | tf_op jit(solution)/shard_map/ppermute | solution.py:793
  249.0 12.8 %collective-permute-start.40 = (bf16[1,192,384]{2,1,0:T(8,128)(2,1)S(1)}, bf16[1,192,384]{2,1,0:T(8,128)(2,1)S(1)}, u32[]{:S(2)}, u32[]{:S(2)}) collective-permute-start(bf16[1,192,384]{2,1,0:T(8,128)(2,1)S(1)} %add_convert_fusion.10), channel_id=1, source_target_pairs={{0,16},{1,9},{2,18},{3,11},{4,20},{5,13},{6,22},{7,15},{8,24},{9,1... | collective-permute-start | bytes 442376 | tf_op jit(solution)/shard_map/ppermute | solution.py:793
  264.0 2.8 collective-permute-start.41
  266.9 11.1 %collective-permute-start.43 = (bf16[256,768]{1,0:T(8,128)(2,1)S(1)}, bf16[256,768]{1,0:T(8,128)(2,1)S(1)}, u32[]{:S(2)}, u32[]{:S(2)}) collective-permute-start(bf16[256,768]{1,0:T(8,128)(2,1)S(1)} %get-tuple-element.501), channel_id=1, source_target_pairs={{0,3},{1,2},{2,1},{3,0},{4,7},{5,6},{6,5},{7,4},{8,11},{9,10},{10,... | collective-permute-start | bytes 1179656 | tf_op jit(solution)/shard_map/ppermute | solution.py:736
  267.3 10.6 %collective-permute-start.42 = (bf16[2,240,384]{2,1,0:T(8,128)(2,1)S(1)}, bf16[2,240,384]{2,1,0:T(8,128)(2,1)S(1)}, u32[]{:S(2)}, u32[]{:S(2)}) collective-permute-start(bf16[2,240,384]{2,1,0:T(8,128)(2,1)S(1)} %add_convert_fusion.5), channel_id=1, source_target_pairs={{0,8},{1,17},{2,10},{3,19},{4,12},{5,21},{6,14},{7,23},{8,0},{9,25... | collective-permute-start | bytes 1105928 | tf_op jit(solution)/shard_map/ppermute | solution.py:793
  (41 other events, 389.8 us)
